TPU v7x, 128 devices: a whole 4x4x4 slice. The times are simulated.
128 devices in a mesh: dp: 16 (over x, z), tensor: 8 (over y, core).
Axes of the slice: x: 4, y: 4, z: 4, core: 2. Of those that a mesh axis runs over, the one named last changes fastest.
Arguments:
- tokens: bfloat16 [2048, 4096], P('dp', 'tensor'), may hold values from -6 to 6
- cotangent: bfloat16 [2048, 4096], P('dp', 'tensor'), may hold values from -6 to 6
- gates: float32 [2048, 2], P('dp'), may hold values from 0.1 to 1
- routes: int32 [2048, 2], P('dp'), may hold values from 0 to 15, all different within a row; in each aligned block of 128 rows (0 to 127, 128 to 255, ...) at most 32 rows name the same one
- dense_gate: bfloat16 [4096, 4096], P(None, 'tensor'), may hold values from -0.125 to 0.125
- dense_up: bfloat16 [4096, 4096], P(None, 'tensor'), may hold values from -0.09375 to 0.09375
- dense_down: bfloat16 [4096, 4096], P('tensor'), may hold values from -0.125 to 0.125
- expert_gate: bfloat16 [16, 4096, 3072], P('dp', None, 'tensor'), may hold values from -0.125 to 0.125
- expert_up: bfloat16 [16, 4096, 3072], P('dp', None, 'tensor'), may hold values from -0.09375 to 0.09375
- expert_down: bfloat16 [16, 3072, 4096], P('dp', 'tensor'), may hold values from -0.15625 to 0.15625
Outputs:
- mixed: bfloat16 [2048, 4096], P('dp', 'tensor')
- token_grad: bfloat16 [2048, 4096], P('dp', 'tensor')
- gate_grad: float32 [2048, 2], P('dp')
Inputs may be any that keep to these rules, and one draw needn't show every extreme that they name: `routes`: each token names 2 different experts. Within each aligned block of 128 tokens no expert is named more than 32 times, and in some block some expert is named exactly 32 times; every expert is named somewhere.
All inputs are finite; a program needn't handle non-finite values.
Results may differ from a plain program's by a relative error of at most 0.023.
Values may be sent and summed in bfloat16 or wider, within the bound.
No kernel may reach another device: no remote copies, remote signals or barrier semaphores. Data moves between devices by JAX's collectives and lax.ppermute only.
A program may use at most 128 MiB of HBM per device.

v0:
```python
import jax
import jax.numpy as jnp
from jax import lax
from jax.sharding import PartitionSpec as P


def gated_part(rows, row_grads, weight_gate, weight_up, weight_down):
    gate_pre = jnp.dot(rows, weight_gate, preferred_element_type=jnp.float32)
    up_pre = jnp.dot(rows, weight_up, preferred_element_type=jnp.float32)
    sigmoid_a = jax.nn.sigmoid(gate_pre)
    activated = gate_pre * sigmoid_a
    hidden = (activated * up_pre).astype(jnp.bfloat16)
    out_term = jnp.dot(hidden, weight_down, preferred_element_type=jnp.float32)
    hidden_grad = lax.dot_general(
        row_grads, weight_down, (((1,), (1,)), ((), ())), preferred_element_type=jnp.float32
    )
    grad_gate = (hidden_grad * up_pre * sigmoid_a * (1.0 + gate_pre * (1.0 - sigmoid_a))).astype(
        jnp.bfloat16
    )
    grad_up = (hidden_grad * activated).astype(jnp.bfloat16)
    grad_term = lax.dot_general(
        grad_gate, weight_gate, (((1,), (1,)), ((), ())), preferred_element_type=jnp.float32
    )
    grad_term = grad_term + lax.dot_general(
        grad_up, weight_up, (((1,), (1,)), ((), ())), preferred_element_type=jnp.float32
    )
    return (out_term, grad_term)


def pack_rows(source, slot_table, token_of, gates, grads, experts, capacity):
    width = source.shape[1]
    source_ext = jnp.concatenate([source, jnp.zeros((1, width), jnp.bfloat16)], axis=0)
    sent_rows = source_ext[token_of].reshape(experts, capacity, width)
    scaled = (gates[:, :, None] * grads.astype(jnp.float32)[:, None, :]).astype(jnp.bfloat16)
    scaled_ext = jnp.concatenate(
        [scaled.reshape(-1, width), jnp.zeros((1, width), jnp.bfloat16)], axis=0
    )
    sent_grads = scaled_ext[slot_table].reshape(experts, capacity, width)
    return (sent_rows, sent_grads)


def local(
    tokens,
    cotangent,
    gates,
    routes,
    dense_gate,
    dense_up,
    dense_down,
    expert_gate,
    expert_up,
    expert_down,
):
    rows_dev = tokens.shape[0]
    picks = routes.shape[1]
    experts = lax.axis_size("dp")
    capacity = 2 * rows_dev * picks // experts
    pair_count = rows_dev * picks
    full_tokens, full_cotan = (
        lax.all_gather(tokens, "tensor", axis=1, tiled=True),
        lax.all_gather(cotangent, "tensor", axis=1, tiled=True),
    )
    flat_ids = routes.reshape(-1)
    one_hot = (flat_ids[:, None] == jnp.arange(experts, dtype=jnp.int32)[None, :]).astype(jnp.int32)
    earlier = jnp.cumsum(one_hot, axis=0) - one_hot
    slot_pos = jnp.sum(earlier * one_hot, axis=1)
    slot_index = flat_ids * capacity + slot_pos
    slot_table = jnp.full((experts * capacity,), pair_count, jnp.int32)
    slot_table = slot_table.at[slot_index].set(jnp.arange(pair_count, dtype=jnp.int32))
    token_of = jnp.where(slot_table < pair_count, slot_table // picks, rows_dev)
    sent_rows, sent_grads = pack_rows(
        full_tokens, slot_table, token_of, gates, full_cotan, experts, capacity
    )
    got_rows, got_grads = (
        lax.all_to_all(sent_rows, "dp", split_axis=0, concat_axis=0, tiled=True),
        lax.all_to_all(sent_grads, "dp", split_axis=0, concat_axis=0, tiled=True),
    )
    dense_out, dense_grad = gated_part(full_tokens, full_cotan, dense_gate, dense_up, dense_down)
    total_rows = experts * capacity
    recv_rows = got_rows.reshape(total_rows, -1)
    recv_grads = got_grads.reshape(total_rows, -1)
    expert_out, expert_grad = gated_part(
        recv_rows, recv_grads, expert_gate[0], expert_up[0], expert_down[0]
    )
    out_share, grad_share = (
        lax.psum_scatter(
            expert_out.astype(jnp.bfloat16), "tensor", scatter_dimension=1, tiled=True
        ).astype(jnp.float32),
        lax.psum_scatter(
            expert_grad.astype(jnp.bfloat16), "tensor", scatter_dimension=1, tiled=True
        ).astype(jnp.float32),
    )
    dense_share, dense_grad_share = (
        lax.psum_scatter(
            dense_out.astype(jnp.bfloat16), "tensor", scatter_dimension=1, tiled=True
        ).astype(jnp.float32),
        lax.psum_scatter(
            dense_grad.astype(jnp.bfloat16), "tensor", scatter_dimension=1, tiled=True
        ).astype(jnp.float32),
    )
    width_part = out_share.shape[1]
    back_out, back_grad = (
        lax.all_to_all(
            out_share.astype(jnp.bfloat16).reshape(experts, capacity, width_part),
            "dp",
            split_axis=0,
            concat_axis=0,
            tiled=True,
        ),
        lax.all_to_all(
            grad_share.astype(jnp.bfloat16).reshape(experts, capacity, width_part),
            "dp",
            split_axis=0,
            concat_axis=0,
            tiled=True,
        ),
    )
    pair_out = (
        back_out.reshape(experts * capacity, width_part)[slot_index]
        .reshape(rows_dev, picks, width_part)
        .astype(jnp.float32)
    )
    pair_grad = (
        back_grad.reshape(experts * capacity, width_part)[slot_index]
        .reshape(rows_dev, picks, width_part)
        .astype(jnp.float32)
    )
    mixed = (dense_share + jnp.sum(gates[:, :, None] * pair_out, axis=1)).astype(jnp.bfloat16)
    token_grad = (dense_grad_share + jnp.sum(pair_grad, axis=1)).astype(jnp.bfloat16)
    partial_inner = jnp.sum(cotangent.astype(jnp.float32)[:, None, :] * pair_out, axis=2)
    gate_grad = lax.psum(partial_inner, "tensor")
    return (mixed, token_grad, gate_grad)


def solution(mesh):
    in_specs = (
        P("dp", "tensor"),
        P("dp", "tensor"),
        P("dp", None),
        P("dp", None),
        P(None, "tensor"),
        P(None, "tensor"),
        P("tensor", None),
        P("dp", None, "tensor"),
        P("dp", None, "tensor"),
        P("dp", "tensor", None),
    )
    out_specs = (P("dp", "tensor"), P("dp", "tensor"), P("dp", None))
    return jax.shard_map(local, mesh=mesh, in_specs=in_specs, out_specs=out_specs, check_vma=False)
```

profile of v0, /device:TPU:2, one launch (start us, length us, event | category | flops | bytes accessed | tf_op | source)
XLA Modules:
  0.0 336.4 jit_solution(4575299899588716809)
XLA Ops:
  7.2 0.0 all-gather.3.cloned.1.call-start
  7.2 0.7 all-gather.3.cloned.1.call-update
  7.9 1.0 copy.22
  8.9 0.1 eq.29
  9.0 0.1 eq.25
  9.2 0.7 broadcast_multiply_fusion
  9.9 0.1 copy.21
  10.0 0.1 mul.104
  10.1 0.6 reduce-window.6
  10.7 0.2 slice_reduce_fusion
  11.0 0.1 fusion.22
  11.1 1.4 scatter_custom_fusion
  12.5 23.0 %all-gather.3.cloned.1.call-done = bf16[128,4096]{1,0:T(8,128)(2,1)} async-done(((bf16[128,512]{1,0:T(8,128)(2,1)}), bf16[128,4096]{1,0:T(8,128)(2,1)}) %all-gather.3.cloned.1.call-update) | async-done | bytes 1048592 | tf_op jit(solution)/shard_map/all_gather | solution.py:60
  35.5 2.3 concatenate.6
  37.8 10.0 %gather_fusion = bf16[512,4096]{1,0:T(8,128)(2,1)} fusion(bf16[129,4096]{1,0:T(8,128)(2,1)} %concatenate.6, s32[1024]{0:T(1024)S(1)} %pad_clamp_fusion.2), kind=kCustom, calls=%fused_computation | custom fusion | bytes 8390656 | tf_op jit(solution)/shard_map/gather | solution.py:33
  47.8 7.4 %all-to-all-start = ((bf16[16,32,4096]{2,1,0:T(8,128)(2,1)}), bf16[16,32,4096]{2,1,0:T(8,128)(2,1)}, u32[]{:S(2)}, u32[]{:S(2)}) async-start(bf16[16,32,4096]{2,1,0:T(8,128)(2,1)} %bitcast.57), calls=%async_computation.1 | async-start | bytes 8388608 | tf_op jit(solution)/shard_map/all_to_all | solution.py:75
  55.2 0.0 all-gather.5.cloned.1.call-start
  55.3 0.7 all-gather.5.cloned.1.call-update
  56.0 0.0 reduce-scatter.7.cloned.1.call-start
  56.0 54.1 %all-to-all-done = bf16[16,32,4096]{2,1,0:T(8,128)(2,1)} async-done(((bf16[16,32,4096]{2,1,0:T(8,128)(2,1)}), bf16[16,32,4096]{2,1,0:T(8,128)(2,1)}, u32[]{:S(2)}, u32[]{:S(2)}) %all-to-all-start) | async-done | bytes 4194336 | tf_op jit(solution)/shard_map/all_to_all | solution.py:75
  110.1 5.6 %fusion.9 = f32[512,384]{1,0:T(8,128)S(1)} fusion(bf16[512,4096]{1,0:T(8,128)(2,1)} %bitcast.4, bf16[1,4096,384]{2,1,0:T(8,128)(2,1)} %param.17), kind=kOutput, calls=%fused_computation.19 | convolution fusion | flops 1610612736 | bytes 8126464 | tf_op jit(solution)/shard_map/dot_general | solution.py:8
  115.8 4.8 %fusion.5 = f32[512,384]{1,0:T(8,128)S(1)} fusion(bf16[512,4096]{1,0:T(8,128)(2,1)} %bitcast.4, bf16[1,4096,384]{2,1,0:T(8,128)(2,1)S(1)} %copy-done.8), kind=kOutput, calls=%fused_computation.15 | convolution fusion | flops 1610612736 | bytes 8126464 | tf_op jit(solution)/shard_map/dot_general | solution.py:9
  120.6 0.9 copy-done.12
  121.5 4.3 %convolution_convert_fusion = bf16[512,4096]{1,0:T(8,128)(2,1)} fusion(bf16[1,384,4096]{2,1,0:T(8,128)(2,1)S(1)} %copy-done, f32[512,384]{1,0:T(8,128)S(1)} %fusion.5, f32[512,384]{1,0:T(8,128)S(1)} %fusion.9), kind=kOutput, calls=%fused_computation.6 | convolution fusion | flops 1613889536 | bytes 8912896 | tf_op jit(solution)/shard_map/dot_general | solution.py:13
  125.9 0.2 reduce-scatter.11.cloned.1.call-start
  126.1 0.4 copy-done.14
  126.5 0.1 copy.20
  126.6 0.1 mul.114
  126.8 0.0 all-gather.5.cloned.1.call-done
  126.8 5.3 %mul.116 = f32[128,2,4096]{2,1,0:T(2,128)} broadcast(bf16[128,4096]{1,0:T(8,128)(2,1)} %all-gather.5.cloned.1.call-done), dimensions={0,2} | broadcast | bytes 5242880 | tf_op jit(solution)/shard_map/mul | solution.py:34
  132.1 6.0 %mul.117 = f32[256,4096]{1,0:T(8,128)} reshape(f32[128,2,4096]{2,1,0:T(2,128)} %mul.116) | data formatting | bytes 8388608 | tf_op jit(solution)/shard_map/mul | solution.py:34
  138.2 2.6 multiply_convert_fusion
  140.8 1.6 concatenate.7
  142.4 10.6 %gather_fusion.2 = bf16[512,4096]{1,0:T(8,128)(2,1)} fusion(bf16[257,4096]{1,0:T(8,128)(2,1)} %concatenate.7, s32[1024]{0:T(1024)S(1)} %pad_clamp_fusion), kind=kCustom, calls=%fused_computation.2 | custom fusion | bytes 8390656 | tf_op jit(solution)/shard_map/gather | solution.py:38
  152.9 63.4 %all_to_all.20 = bf16[16,32,4096]{2,1,0:T(8,128)(2,1)S(1)} all-to-all(bf16[16,32,4096]{2,1,0:T(8,128)(2,1)} %bitcast.58), channel_id=1, replica_groups=mesh['dp'=16,'tensor'=8] {'dp'}, dimensions={0} | all-to-all | bytes 8388608 | tf_op jit(solution)/shard_map/all_to_all | solution.py:76
  216.3 2.4 fusion.1
  218.7 2.5 fusion.7
  221.2 4.4 %add_convert_fusion = bf16[512,4096]{1,0:T(8,128)(2,1)} fusion(f32[512,4096]{1,0:T(8,128)S(1)} %fusion.7, bf16[1,4096,384]{2,1,0:T(8,128)(2,1)S(1)} %copy-done.9, f32[512,384]{1,0:T(8,128)S(1)} %fusion.1, f32[512,384]{1,0:T(8,128)S(1)} %copy-done.6), kind=kOutput, calls=%fused_computation.5 | convolution fusion | flops 1615986688 | bytes 17301504 | tf_op jit(solution)/shard_map/dot_general | solution.py:24
  225.6 0.0 reduce-scatter.5.cloned.1.call-start
  225.7 3.4 %fusion.35 = f32[128,512]{1,0:T(8,128)S(1)} fusion(bf16[128,4096]{1,0:T(8,128)(2,1)} %all-gather.3.cloned.1.call-done, bf16[4096,512]{1,0:T(8,128)(2,1)} %param.14), kind=kOutput, calls=%fused_computation.70 | convolution fusion | flops 536870912 | bytes 5505024 | tf_op jit(solution)/shard_map/dot_general | solution.py:8
  229.1 3.0 fusion.36
  232.1 0.7 copy-done.10
  232.8 1.8 convolution_convert_fusion.1
  234.6 0.0 reduce-scatter.9.cloned.1.call-start
  234.7 4.2 %fusion.37 = f32[128,512]{1,0:T(8,128)S(1)} fusion(bf16[128,4096]{1,0:T(8,128)(2,1)} %all-gather.5.cloned.1.call-done, bf16[512,4096]{1,0:T(8,128)(2,1)} %param.16), kind=kOutput, calls=%fused_computation.72 | convolution fusion | flops 536870912 | bytes 5505024 | tf_op jit(solution)/shard_map/dot_general | solution.py:14
  238.9 1.5 fusion.16
  240.4 0.8 copy-done.3
  241.2 2.5 fusion
  243.7 6.8 %all-to-all-start.1 = ((bf16[16,32,512]{2,1,0:T(8,128)(2,1)}), bf16[16,32,512]{2,1,0:T(8,128)(2,1)}, u32[]{:S(2)}, u32[]{:S(2)}) async-start(bf16[16,32,512]{2,1,0:T(8,128)(2,1)} %bitcast.60), calls=%async_computation.3 | async-start | bytes 1048576 | tf_op jit(solution)/shard_map/all_to_all | solution.py:103
  250.5 11.3 %reduce-scatter.11.cloned.1.call-done = bf16[512,512]{1,0:T(8,128)(2,1)} async-done(((bf16[512,4096]{1,0:T(8,128)(2,1)}), bf16[512,512]{1,0:T(8,128)(2,1)}) %reduce-scatter.11.cloned.1.call-update) | async-done | bytes 524304 | tf_op jit(solution)/shard_map/reduce_scatter | solution.py:89
  261.8 7.2 %all-to-all-start.3 = ((bf16[16,32,512]{2,1,0:T(8,128)(2,1)}), bf16[16,32,512]{2,1,0:T(8,128)(2,1)}, u32[]{:S(2)}, u32[]{:S(2)}) async-start(bf16[16,32,512]{2,1,0:T(8,128)(2,1)} %bitcast.61), calls=%async_computation.7 | async-start | bytes 1048576 | tf_op jit(solution)/shard_map/all_to_all | solution.py:110
  269.0 1.6 convert_element_type.101
  270.6 2.3 gather_fusion.1
  272.9 1.1 reshape.107
  274.1 2.8 multiply_reduce_fusion
  276.9 24.2 %psum.7 = f32[128,2]{1,0:T(8,128)S(1)} all-reduce(f32[128,2]{1,0:T(8,128)S(1)} %get-tuple-element.6), channel_id=1, replica_groups=mesh['dp'=16,'tensor'=8] {'tensor'}, use_global_device_ids=true, to_apply=%region_11.12 | all-reduce | flops 256 | bytes 2048 | tf_op jit(solution)/shard_map/psum | solution.py:131
  301.1 0.6 copy.26
  301.7 2.3 gather_fusion.3
  304.1 1.1 reshape.108
  305.2 1.7 reduce_sum.41
  306.9 0.0 reduce-scatter.5.cloned.1.call-done
  306.9 1.7 add_convert_fusion.2
  308.6 19.4 %reduce-scatter.9.cloned.1.call-done = bf16[128,512]{1,0:T(8,128)(2,1)} async-done(((bf16[128,4096]{1,0:T(8,128)(2,1)}), bf16[128,512]{1,0:T(8,128)(2,1)}) %reduce-scatter.9.cloned.1.call-update) | async-done | bytes 131088 | tf_op jit(solution)/shard_map/reduce_scatter | solution.py:97
  328.0 1.6 add_convert_fusion.1
  (42 shorter events, 0.2 us)
Async XLA Ops:
  7.2 114.3 %copy-start = (bf16[1,384,4096]{2,1,0:T(8,128)(2,1)S(1)}, bf16[1,384,4096]{2,1,0:T(8,128)(2,1)}, u32[]{:S(2)}) copy-start(bf16[1,384,4096]{2,1,0:T(8,128)(2,1)} %param.19) | copy-start | bytes 9437188
  7.2 28.3 %all-gather.3.cloned.1.call-start = ((), (), s32[]{:S(2)}) async-start(), calls=%async_computation.8 | async-start | bytes 1179648 | tf_op jit(solution)/shard_map/all_gather | solution.py:60
  47.8 62.3 %all-to-all-start = ((bf16[16,32,4096]{2,1,0:T(8,128)(2,1)}), bf16[16,32,4096]{2,1,0:T(8,128)(2,1)}, u32[]{:S(2)}, u32[]{:S(2)}) async-start(bf16[16,32,4096]{2,1,0:T(8,128)(2,1)} %bitcast.57), calls=%async_computation.1 | async-start | bytes 8388608 | tf_op jit(solution)/shard_map/all_to_all | solution.py:75
  55.2 71.6 %all-gather.5.cloned.1.call-start = ((), (), s32[]{:S(2)}) async-start(), calls=%async_computation.11 | async-start | bytes 1179648 | tf_op jit(solution)/shard_map/all_gather | solution.py:61
  56.0 187.7 %reduce-scatter.7.cloned.1.call-start = ((), (), s32[]{:S(2)}) async-start(), calls=%async_computation.10 | async-start | bytes 4718592 | tf_op jit(solution)/shard_map/reduce_scatter | solution.py:86
  110.1 5.6 %copy-start.8 = (bf16[1,4096,384]{2,1,0:T(8,128)(2,1)S(1)}, bf16[1,4096,384]{2,1,0:T(8,128)(2,1)}, u32[]{:S(2)}) copy-start(bf16[1,4096,384]{2,1,0:T(8,128)(2,1)} %param.18) | copy-start | bytes 9437188
  115.8 4.8 %copy-start.5 = (f32[512,384]{1,0:T(8,128)}, f32[512,384]{1,0:T(8,128)S(1)}, u32[]{:S(2)}) copy-start(f32[512,384]{1,0:T(8,128)S(1)} %fusion.9) | copy-start | bytes 2359300
  120.6 0.9 copy-start.12
  125.8 0.7 copy-start.14
  125.9 135.9 %reduce-scatter.11.cloned.1.call-start = ((), (), s32[]{:S(2)}) async-start(), calls=%async_computation.13 | async-start | bytes 4718592 | tf_op jit(solution)/shard_map/reduce_scatter | solution.py:89
  216.3 2.4 copy-start.6
  216.3 2.4 copy-start.7
  216.3 2.4 copy-start.13
  218.7 2.5 copy-start.9
  225.6 81.3 %reduce-scatter.5.cloned.1.call-start = ((), (), s32[]{:S(2)}) async-start(), calls=%async_computation.9 | async-start | bytes 1179648 | tf_op jit(solution)/shard_map/reduce_scatter | solution.py:94
  225.7 3.4 %copy-start.4 = (bf16[128,4096]{1,0:T(8,128)(2,1)S(1)}, bf16[128,4096]{1,0:T(8,128)(2,1)}, u32[]{:S(2)}) copy-start(bf16[128,4096]{1,0:T(8,128)(2,1)} %all-gather.3.cloned.1.call-done) | copy-start | bytes 3145732
  225.7 7.1 %copy-start.2 = (bf16[512,4096]{1,0:T(8,128)(2,1)S(1)}, bf16[512,4096]{1,0:T(8,128)(2,1)}, u32[]{:S(2)}) copy-start(bf16[512,4096]{1,0:T(8,128)(2,1)} %param.16) | copy-start | bytes 12582916
  232.1 0.7 copy-start.10
  234.6 93.4 %reduce-scatter.9.cloned.1.call-start = ((), (), s32[]{:S(2)}) async-start(), calls=%async_computation.12 | async-start | bytes 1179648 | tf_op jit(solution)/shard_map/reduce_scatter | solution.py:97
  234.7 4.2 %copy-start.1 = (bf16[4096,512]{1,0:T(8,128)(2,1)S(1)}, bf16[4096,512]{1,0:T(8,128)(2,1)}, u32[]{:S(2)}) copy-start(bf16[4096,512]{1,0:T(8,128)(2,1)} %param.14) | copy-start | bytes 12582916
  234.7 4.2 %copy-start.11 = (f32[128,512]{1,0:T(8,128)S(1)}, f32[128,512]{1,0:T(8,128)}, u32[]{:S(2)}) copy-start(f32[128,512]{1,0:T(8,128)} %copy-done.10) | copy-start | bytes 786436
  238.9 2.3 copy-start.3
  243.7 18.1 %all-to-all-start.1 = ((bf16[16,32,512]{2,1,0:T(8,128)(2,1)}), bf16[16,32,512]{2,1,0:T(8,128)(2,1)}, u32[]{:S(2)}, u32[]{:S(2)}) async-start(bf16[16,32,512]{2,1,0:T(8,128)(2,1)} %bitcast.60), calls=%async_computation.3 | async-start | bytes 1048576 | tf_op jit(solution)/shard_map/all_to_all | solution.py:103
  261.8 39.9 %all-to-all-start.3 = ((bf16[16,32,512]{2,1,0:T(8,128)(2,1)}), bf16[16,32,512]{2,1,0:T(8,128)(2,1)}, u32[]{:S(2)}, u32[]{:S(2)}) async-start(bf16[16,32,512]{2,1,0:T(8,128)(2,1)} %bitcast.61), calls=%async_computation.7 | async-start | bytes 1048576 | tf_op jit(solution)/shard_map/all_to_all | solution.py:110
Sparse Core Ops, SparseCore 0:
  9.7 25.7 all-gather.2
  57.8 23.0 all-gather.4
  126.0 45.6 reduce-scatter.6
  225.7 36.0 reduce-scatter.10
  264.0 30.8 reduce-scatter.4
  297.1 30.8 reduce-scatter.8
where the time goes:
time: 338 us; the launch traced here: 336 us
  waiting for transfers between devices  109 us (32%)
  blocking collectives  87.6 us (26%)
  local copies, waits for them, and re-layouts  49.6 us (15%)
  matrix products  40.2 us (12%)
  starting transfers between devices  21.8 us (6%)
  between operations  14.4 us (4%)
  other arithmetic  13.4 us (4%)
    all_to_all x1, blocking collectives, local(): lax.all_to_all(sent_grads, 'dp', split_axis=0, concat_axis=0, tiled=True)  63.4 us
    all_to_all x1, waiting for transfers between devices, local(): lax.all_to_all(sent_rows, 'dp', split_axis=0, concat_axis=0, tiled=True)  54.1 us
    psum x1, blocking collectives, local(): gate_grad = lax.psum(partial_inner, 'tensor')  24.2 us
    all_gather x1, waiting for transfers between devices, local(): lax.all_gather(tokens, 'tensor', axis=1, tiled=True)  23 us
    reduce_scatter x1, waiting for transfers between devices, local(): lax.psum_scatter(dense_grad.astype(jnp.bfloat16), 'tensor', scatter_dimen...  19.4 us
    mul x3, local copies, waits for them, and re-layouts, pack_rows(): gates[:, :, None] * grads.astype(jnp.float32)[:, None, :]  11.5 us
    reduce_scatter x1, waiting for transfers between devices, local(): lax.psum_scatter(expert_grad.astype(jnp.bfloat16), 'tensor', scatter_dime...  11.3 us
    gather x1, local copies, waits for them, and re-layouts, pack_rows(): sent_grads = scaled_ext[slot_table].reshape(experts, capacity, width)  10.6 us
  transfers between devices with their start and end apart: 9, of which 4 were waited for; matrix products, arithmetic and copies ran while one was open for 26% of the time, Pallas kernels for 0%

commit v1 on v0

v1 whole, which is shorter than its diff:
```python
import functools

import jax
import jax.numpy as jnp
from jax import lax
from jax.experimental import pallas as pl
from jax.experimental.pallas import tpu as pltpu
from jax.sharding import PartitionSpec as P

F32 = jnp.float32
BF16 = jnp.bfloat16
MIB = 1 << 20
CAPACITY = 32
SIDES = 4


def dot(a, b, contract=((1,), (0,))):
    return lax.dot_general(a, b, (contract, ((), ())), preferred_element_type=F32)


def dot_nt(a, b):
    return dot(a, b, ((1,), (1,)))


def dot_tn(a, b):
    return dot(a, b, ((0,), (0,)))


def gate_terms(a, b):
    s = jax.nn.sigmoid(a)
    act = a * s
    return act, (act * b).astype(BF16), b * s * (1.0 + a * (1.0 - s))


def plan_kernel(routes_ref, gates_ref, cotan_ref, pick_ref, send_ref):
    rows = routes_ref.shape[0]
    slots = pick_ref.shape[1]
    lane = lax.broadcasted_iota(jnp.int32, (rows, 128), 1)
    one = [(routes_ref[:, k : k + 1] == lane).astype(F32) for k in range(2)]
    lower = (
        lax.broadcasted_iota(jnp.int32, (rows, rows), 1)
        < lax.broadcasted_iota(jnp.int32, (rows, rows), 0)
    ).astype(BF16)
    earlier = dot(lower, (one[0] + one[1]).astype(BF16))
    place = lax.broadcasted_iota(jnp.int32, (rows, slots), 1)
    cotan = cotan_ref[...].astype(F32)
    total = None
    for k in range(2):
        pos = jnp.sum(earlier * one[k], axis=1, keepdims=True).astype(jnp.int32)
        slot = routes_ref[:, k : k + 1] * CAPACITY + pos
        pick = (slot == place).astype(BF16)
        pick_ref[k * rows : (k + 1) * rows, :] = pick
        scaled = (gates_ref[:, k : k + 1] * cotan).astype(BF16)
        term = dot_tn(pick, scaled)
        total = term if total is None else total + term
    send_ref[...] = total.astype(BF16)


def rows_kernel(pick_ref, p0, p1, p2, p3, after, send_ref):
    rows = p0.shape[0] // 2
    width = p0.shape[1]
    pick = pick_ref[:rows, :] + pick_ref[rows:, :]
    for d, piece in enumerate((p0, p1, p2, p3)):
        send_ref[:, d * width : (d + 1) * width] = dot_tn(pick, piece[:rows, :]).astype(BF16)


def block_at(offs, i, width):
    return pl.ds(pl.multiple_of(offs[i], 512), width)


def dense_kernel(offs, *refs):
    pieces, (wg, wu, wd), outs = refs[:8], refs[9:12], refs[12:]
    rows = pieces[0].shape[0] // 2
    width = pieces[0].shape[1]
    a = b = g = None
    for i in range(8):
        at = block_at(offs, i, width)
        x, c = pieces[i][:rows, :], pieces[i][rows:, :]
        ta, tb, tg = dot(x, wg[at, :]), dot(x, wu[at, :]), dot_nt(c, wd[:, at])
        a, b, g = (ta, tb, tg) if a is None else (a + ta, b + tb, g + tg)
    act, hidden, slope = gate_terms(a, b)
    da, du = (g * slope).astype(BF16), (g * act).astype(BF16)
    for i in range(8):
        at = block_at(offs, i, width)
        out, d = outs[i // 4], i % 4
        out[:rows, d * width : (d + 1) * width] = dot(hidden, wd[:, at]).astype(BF16)
        out[rows:, d * width : (d + 1) * width] = (
            dot_nt(da, wg[at, :]) + dot_nt(du, wu[at, :])
        ).astype(BF16)


def dense_sum_kernel(mine, got, out_ref, g0, g1, g2, g3):
    rows = out_ref.shape[0]
    width = g0.shape[1]
    out_ref[...] = mine[:rows, :].astype(F32) + got[:rows, :].astype(F32)
    for d, ref in enumerate((g0, g1, g2, g3)):
        at = slice(d * width, (d + 1) * width)
        ref[...] = (mine[rows:, at].astype(F32) + got[rows:, at].astype(F32)).astype(ref.dtype)


def back_kernel(offs, *refs):
    pieces, wd, g_ref = refs[:8], refs[8], refs[9]
    width = pieces[0].shape[1]
    g = None
    for i in range(8):
        term = dot_nt(pieces[i][...], wd[:, block_at(offs, i, width)])
        g = term if g is None else g + term
    g_ref[...] = g


def forth_kernel(offs, xm, xo, g_ref, wg, wu, wd, oo, hid_ref, dadu_ref, ab):
    width = 512
    units = wg.shape[1]
    for i in range(8):
        at = block_at(offs, i, width)
        ref, d = (xm, xo)[i // 4], i % 4
        w = jnp.concatenate([wg[at, :], wu[at, :]], axis=1)
        term = dot(ref[:, d * width : (d + 1) * width], w)
        if i == 0:
            ab[...] = term
        else:
            ab[...] += term
    act, hidden, slope = gate_terms(ab[:, :units], ab[:, units:])
    g = g_ref[...]
    hid_ref[...] = hidden
    dadu_ref[:, :units] = (g * slope).astype(BF16)
    dadu_ref[:, units:] = (g * act).astype(BF16)
    for d in range(4):
        oo[:, d * width : (d + 1) * width] = dot(
            hidden, wd[:, block_at(offs, 4 + d, width)]
        ).astype(BF16)


def out_kernel(offs, hid_ref, wd, om):
    width = 512
    for d in range(4):
        om[:, d * width : (d + 1) * width] = dot(
            hid_ref[...], wd[:, block_at(offs, d, width)]
        ).astype(BF16)


def down_kernel(first, offs, dadu_ref, wg, wu, after, out):
    width = 512
    for d in range(4):
        at = block_at(offs, first + d, width)
        w = jnp.concatenate([wg[at, :], wu[at, :]], axis=1)
        out[:, d * width : (d + 1) * width] = dot_nt(dadu_ref[...], w).astype(BF16)


def add_kernel(mine, got, out):
    out[...] = (mine[...].astype(F32) + got[...].astype(F32)).astype(BF16)


def split_kernel(mine, got, *outs):
    width = outs[0].shape[1]
    for d, ref in enumerate(outs):
        at = slice(d * width, (d + 1) * width)
        ref[...] = (mine[:, at].astype(F32) + got[:, at].astype(F32)).astype(ref.dtype)


def sum_kernel(p0, p1, p2, p3, after, out):
    out[...] = (
        p0[...] + p1[...].astype(F32) + p2[...].astype(F32) + p3[...].astype(F32)
    ).astype(BF16)


def mix_kernel(back, pick, gates, dense, c0, c1, c2, c3, m0, m1, m2, m3, inner_ref):
    rows = gates.shape[0]
    width = 512
    inner = [None, None]
    for d, (cot, out) in enumerate(((c0, m0), (c1, m1), (c2, m2), (c3, m3))):
        cotan = cot[rows:, :].astype(F32)
        y = dot(pick[...], back[:, d * width : (d + 1) * width])
        total = dense[:, d * width : (d + 1) * width]
        for k in range(2):
            yk = y[k * rows : (k + 1) * rows, :]
            total = total + gates[:, k : k + 1] * yk
            term = jnp.sum(cotan * yk, axis=1, keepdims=True)
            inner[k] = term if inner[k] is None else inner[k] + term
        out[...] = total.astype(BF16)
    lane = lax.broadcasted_iota(jnp.int32, (rows, 128), 1)
    inner_ref[...] = jnp.where(lane == 0, inner[0], jnp.where(lane == 1, inner[1], 0.0))


def grad_kernel(back, pick, d0, d1, d2, d3, out):
    rows = out.shape[0]
    z = dot(pick[:rows, :] + pick[rows:, :], back[...])
    dense = d0[...] + d1[...].astype(F32) + d2[...].astype(F32) + d3[...].astype(F32)
    out[...] = (dense + z).astype(BF16)


def call(kernel, outs, limit, flops, prefetch, args, name, after=None, scratch=()):
    vmem = pl.BlockSpec(memory_space=pltpu.VMEM)
    smem = pl.BlockSpec(memory_space=pltpu.SMEM)
    moved = sum(a.size * a.dtype.itemsize for a in args)
    return pl.pallas_call(
        kernel,
        out_shape=[jax.ShapeDtypeStruct(*o) for o in outs],
        in_specs=[
            smem if i < prefetch else pl.BlockSpec(memory_space=pl.ANY) if i == after else vmem
            for i in range(len(args))
        ],
        out_specs=[vmem] * len(outs),
        compiler_params=pltpu.CompilerParams(vmem_limit_bytes=limit * MIB),
        cost_estimate=pl.CostEstimate(flops=flops, bytes_accessed=moved, transcendentals=0),
        scratch_shapes=list(scratch),
        name=name,
    )(*args)


def local(
    tokens,
    cotangent,
    gates,
    routes,
    dense_gate,
    dense_up,
    dense_down,
    expert_gate,
    expert_up,
    expert_down,
):
    devices = lax.axis_size("tensor")
    rows, width = tokens.shape
    experts = lax.axis_size("dp")
    slots = experts * CAPACITY
    half = SIDES * width
    hidden = expert_gate.shape[2]
    dense_hidden = dense_gate.shape[1]
    me = lax.axis_index("tensor")
    chip, core = me // 2, me % 2

    def along(v, d):
        return lax.ppermute(
            v, "tensor", [(i, (i + 2 * d) % devices) for i in range(devices)]
        )

    def swap(v):
        return lax.ppermute(v, "tensor", [(i, i ^ 1) for i in range(devices)])

    def spread(v):
        return lax.all_to_all(v, "dp", split_axis=0, concat_axis=0, tiled=True)

    steps = jnp.arange(SIDES, dtype=jnp.int32)
    chips = lax.rem(chip + SIDES - steps, SIDES)
    offs = jnp.concatenate([2 * chips + core, 2 * chips + 1 - core]) * width

    wg, wu, wd = expert_gate[0], expert_up[0], expert_down[0]
    both = jnp.concatenate([tokens, cotangent], axis=0)
    own = [both, along(both, 1), along(both, 2), along(both, 3)]
    pick, grads_send = call(
        plan_kernel,
        [((2 * rows, slots), BF16), ((slots, width), BF16)],
        16,
        2 * 2 * rows * slots * width,
        0,
        (routes, gates, cotangent),
        "plan",
    )
    got_grads = spread(grads_send)
    other = [swap(v) for v in own]
    (rows_send,) = call(
        rows_kernel,
        [((slots, half), BF16)],
        12,
        2 * rows * slots * half,
        0,
        (pick, *own, got_grads),
        "rows",
        after=5,
    )
    got_rows = spread(rows_send)
    grads_own = [got_grads] + [along(got_grads, d) for d in (1, 2, 3)]
    dense_m, dense_o = call(
        dense_kernel,
        [((2 * rows, half), BF16)] * 2,
        28,
        12 * rows * dense_hidden * half * 2,
        1,
        (offs, *own, *other, rows_send, dense_gate, dense_up, dense_down),
        "dense",
        after=9,
    )
    dense_out, *dense_part = call(
        dense_sum_kernel,
        [((rows, half), F32), ((rows, width), F32)] + [((rows, width), BF16)] * 3,
        12,
        2 * rows * half,
        0,
        (dense_m, swap(dense_o)),
        "dense_sum",
    )
    dense_got = [dense_part[0]] + [along(dense_part[d], SIDES - d) for d in (1, 2, 3)]
    grads_other = [swap(v) for v in grads_own]
    (g,) = call(
        back_kernel,
        [((slots, hidden), F32)],
        16,
        2 * slots * hidden * half * 2,
        1,
        (offs, *grads_own, *grads_other, wd),
        "back",
    )
    got_rows, g, dense_out, dense_got = lax.optimization_barrier(
        (got_rows, g, dense_out, dense_got)
    )
    rows_other = swap(got_rows)
    out_o, hid, dadu = call(
        forth_kernel,
        [((slots, half), BF16), ((slots, hidden), BF16), ((slots, 2 * hidden), BF16)],
        28,
        5 * slots * hidden * half * 2,
        1,
        (offs, got_rows, rows_other, g, wg, wu, wd),
        "forth",
        scratch=[pltpu.VMEM((slots, 2 * hidden), F32)],
    )
    out_got = swap(out_o)
    (out_m,) = call(
        out_kernel,
        [((slots, half), BF16)],
        12,
        2 * slots * hidden * half,
        1,
        (offs, hid, wd),
        "out",
    )
    (grad_o,) = call(
        functools.partial(down_kernel, 4),
        [((slots, half), BF16)],
        16,
        4 * slots * hidden * half,
        1,
        (offs, dadu, wg, wu, out_m),
        "down_o",
        after=4,
    )
    grad_got = swap(grad_o)
    (out_chip,) = call(
        add_kernel,
        [((slots, half), BF16)],
        12,
        slots * half,
        0,
        (out_m, out_got),
        "add",
    )
    out_back = spread(out_chip)
    (grad_m,) = call(
        functools.partial(down_kernel, 0),
        [((slots, half), BF16)],
        16,
        4 * slots * hidden * half,
        1,
        (offs, dadu, wg, wu, grad_o),
        "down_m",
        after=4,
    )
    grad_part = call(
        split_kernel,
        [((slots, width), F32)] + [((slots, width), BF16)] * 3,
        16,
        slots * half,
        0,
        (grad_m, grad_got),
        "split",
    )
    grad_all = [grad_part[0]] + [along(grad_part[d], SIDES - d) for d in (1, 2, 3)]
    m0, m1, m2, m3, inner = call(
        mix_kernel,
        [((rows, width), BF16)] * 4 + [((rows, 128), F32)],
        16,
        4 * rows * slots * half,
        0,
        (out_back, pick, gates, dense_out, *own),
        "mix",
    )
    (grad_sum,) = call(
        sum_kernel,
        [((slots, width), BF16)],
        12,
        3 * slots * width,
        0,
        (*grad_all, inner),
        "sum",
        after=4,
    )
    grad_back = spread(grad_sum)
    mixed = m0.astype(F32)
    for d, part in ((1, m1), (2, m2), (3, m3)):
        mixed = mixed + along(part, SIDES - d).astype(F32)
    inner = inner[:, :2]
    inner = inner + swap(inner)
    gate_grad = inner + along(inner, 1) + along(inner, 2) + along(inner, 3)
    (token_grad,) = call(
        grad_kernel,
        [((rows, width), BF16)],
        12,
        2 * rows * slots * width,
        0,
        (grad_back, pick, *dense_got),
        "grad",
    )
    return (mixed.astype(BF16), token_grad, gate_grad)


def solution(mesh):
    in_specs = (
        P("dp", "tensor"),
        P("dp", "tensor"),
        P("dp", None),
        P("dp", None),
        P(None, "tensor"),
        P(None, "tensor"),
        P("tensor", None),
        P("dp", None, "tensor"),
        P("dp", None, "tensor"),
        P("dp", "tensor", None),
    )
    out_specs = (P("dp", "tensor"), P("dp", "tensor"), P("dp", None))
    return jax.shard_map(local, mesh=mesh, in_specs=in_specs, out_specs=out_specs, check_vma=False)
```

time: 338 us -> 202 us (0.60)
  blocking collectives: 87.6 us -> 0 us
  waiting for transfers between devices: 109 us -> 66.6 us
  matrix products: 40.2 us -> 0 us
  Pallas kernels: 0 us -> 39.2 us
  starting transfers between devices: 21.8 us -> 57.5 us
  local copies, waits for them, and re-layouts: 49.6 us -> 34.9 us
  between operations: 14.4 us -> 1.02 us
  other arithmetic: 13.4 us -> 1.74 us
    all_to_all x1 -> x0, blocking collectives: 63.4 us -> none  [local(): lax.all_to_all(sent_grads, 'dp', split_axis=0, concat_axis=0, tiled=True)]
    ppermute x0 -> x31, waiting for transfers between devices: none -> 49.8 us  [the longest x18 45 us: along(): lax.ppermute(v, 'tensor', [(i, (i + 2 * d) % devices) for i in range(devi...]
    dot_general x12 -> x0, matrix products: 40.2 us -> none  [the longest x2 8.99 us: gated_part(): gate_pre = jnp.dot(rows, weight_gate, preferred_element_type=jnp.float32)]
    pallas_call x0 -> x14, Pallas kernels: none -> 39.2 us  [call(): pl.pallas_call(kernel, out_shape=[jax.ShapeDtypeStruct(*o) for o in outs]...]
    all_to_all x3 -> x4, waiting for transfers between devices: 54.1 us -> 16.8 us  [spread(): return lax.all_to_all(v, 'dp', split_axis=0, concat_axis=0, tiled=True)]
    reduce_scatter x4 -> x0, waiting for transfers between devices: 30.8 us -> none  [the longest x1 19.4 us: local(): lax.psum_scatter(dense_grad.astype(jnp.bfloat16), 'tensor', scatter_dimen...]
    unnamed x33 -> x102, local copies, waits for them, and re-layouts: 4.6 us -> 34 us
    ppermute x0 -> x31, starting transfers between devices: none -> 27.2 us  [the longest x18 25 us: along(): lax.ppermute(v, 'tensor', [(i, (i + 2 * d) % devices) for i in range(devi...]
  transfers between devices with their start and end apart: 9 -> 35, of which waited for: 4 -> 16; matrix products, arithmetic and copies ran while one was open for 26% -> 2% of each run, Pallas kernels for 0% -> 13%
where the time goes in v1:
time: 202 us; the launch traced here: 201 us
  waiting for transfers between devices  66.6 us (33%)
  starting transfers between devices  57.5 us (28%)
  Pallas kernels  39.2 us (19%)
  local copies, waits for them, and re-layouts  34.9 us (17%)
    ppermute x18, waiting for transfers between devices, along(): lax.ppermute(v, 'tensor', [(i, (i + 2 * d) % devices) for i in range(devi...  45 us
    pallas_call x14, Pallas kernels, call(): pl.pallas_call(kernel, out_shape=[jax.ShapeDtypeStruct(*o) for o in outs]...  39.2 us
    unnamed x102, local copies, waits for them, and re-layouts  34 us
    all_to_all x4, starting transfers between devices, spread(): return lax.all_to_all(v, 'dp', split_axis=0, concat_axis=0, tiled=True)  30.3 us
    ppermute x18, starting transfers between devices, along(): lax.ppermute(v, 'tensor', [(i, (i + 2 * d) % devices) for i in range(devi...  25 us
    all_to_all x4, waiting for transfers between devices, spread(): return lax.all_to_all(v, 'dp', split_axis=0, concat_axis=0, tiled=True)  16.8 us
    ppermute x13, waiting for transfers between devices, swap(): return lax.ppermute(v, 'tensor', [(i, i ^ 1) for i in range(devices)])  4.8 us
  transfers between devices with their start and end apart: 35, of which 16 were waited for; matrix products, arithmetic and copies ran while one was open for 2% of the time, Pallas kernels for 13%

profile of v1, /device:TPU:2, one launch (start us, length us, event | category | flops | bytes accessed | tf_op | source)
XLA Modules:
  0.0 201.0 jit_solution(4878157377933973589)
XLA Ops:
  2.2 0.9 copy-done.45
  3.1 1.8 plan.1
  4.9 8.3 %all-to-all-start = ((bf16[16,32,512]{2,1,0:T(8,128)(2,1)}), bf16[16,32,512]{2,1,0:T(8,128)(2,1)S(1)}, u32[]{:S(2)}, u32[]{:S(2)}) async-start(bf16[16,32,512]{2,1,0:T(8,128)(2,1)} %bitcast), calls=%async_computation | async-start | bytes 1048576 | tf_op jit(solution)/shard_map/all_to_all | solution.py:242
  13.2 0.9 constant_dynamic-update-slice_fusion.1
  14.1 0.9 constant_dynamic-update-slice_fusion.p0.refs_0_.c0
  15.1 1.6 collective-permute-start
  16.7 2.9 %collective-permute-start.1 = (bf16[256,512]{1,0:T(8,128)(2,1)S(1)}, bf16[256,512]{1,0:T(8,128)(2,1)S(1)}, u32[]{:S(2)}, u32[]{:S(2)}) collective-permute-start(bf16[256,512]{1,0:T(8,128)(2,1)S(1)} %constant_dynamic-update-slice_fusion.p0.refs_0_.c0), channel_id=1, source_target_pairs={{0,4},{1,5},{2,6},{3,7},{4,0},{5,1},{6,2},{7,3},{8,12},{9,13},{10,... | collective-permute-start | bytes 786440 | tf_op jit(solution)/shard_map/ppermute | solution.py:234
  19.6 1.3 collective-permute-start.2
  20.9 3.5 %collective-permute-done.p1.refs_1_.c1 = bf16[256,512]{1,0:T(8,128)(2,1)S(1)} collective-permute-done((bf16[256,512]{1,0:T(8,128)(2,1)S(1)}, bf16[256,512]{1,0:T(8,128)(2,1)S(1)}, u32[]{:S(2)}, u32[]{:S(2)}) %collective-permute-start) | collective-permute-done | bytes 262176 | tf_op jit(solution)/shard_map/ppermute | solution.py:234
  24.4 6.2 %collective-permute-done.1.p2.refs_2_.c2 = bf16[256,512]{1,0:T(8,128)(2,1)S(1)} collective-permute-done((bf16[256,512]{1,0:T(8,128)(2,1)S(1)}, bf16[256,512]{1,0:T(8,128)(2,1)S(1)}, u32[]{:S(2)}, u32[]{:S(2)}) %collective-permute-start.1) | collective-permute-done | bytes 262176 | tf_op jit(solution)/shard_map/ppermute | solution.py:234
  30.7 2.1 %rows.1.refs_8_ = bf16[512,2048]{1,0:T(8,128)(2,1)} custom-call(bf16[256,512]{1,0:T(8,128)(2,1)S(1)} %get-tuple-element.31.pick_ref.pick, bf16[256,512]{1,0:T(8,128)(2,1)S(1)} %constant_dynamic-update-slice_fusion.p0.refs_0_.c0, bf16[256,512]{1,0:T(8,128)(2,1)S(1)} %collective-permute-done.p1.refs_1_.c1, ...), custom_call_target="tpu_custom_call" | custom-call | flops 268435456 | bytes 1835008 | tf_op jit(solution)/shard_map/rows/pallas_call | solution.py:196
  32.8 7.2 %all-to-all-start.1 = ((bf16[16,32,2048]{2,1,0:T(8,128)(2,1)}), bf16[16,32,2048]{2,1,0:T(8,128)(2,1)}, u32[]{:S(2)}, u32[]{:S(2)}) async-start(bf16[16,32,2048]{2,1,0:T(8,128)(2,1)} %bitcast.2), calls=%async_computation.1 | async-start | bytes 4194304 | tf_op jit(solution)/shard_map/all_to_all | solution.py:242
  44.4 2.2 %copy-done.8 = bf16[4096,512]{1,0:T(8,128)(2,1)S(1)} copy-done((bf16[4096,512]{1,0:T(8,128)(2,1)S(1)}, bf16[4096,512]{1,0:T(8,128)(2,1)}, u32[]{:S(2)}) %copy-start.8) | copy-done | bytes 4194328
  46.6 2.2 %copy-done.9 = bf16[4096,512]{1,0:T(8,128)(2,1)S(1)} copy-done((bf16[4096,512]{1,0:T(8,128)(2,1)S(1)}, bf16[4096,512]{1,0:T(8,128)(2,1)}, u32[]{:S(2)}) %copy-start.9) | copy-done | bytes 4194328
  48.7 2.2 %copy-done.10 = bf16[512,4096]{1,0:T(8,128)(2,1)S(1)} copy-done((bf16[512,4096]{1,0:T(8,128)(2,1)S(1)}, bf16[512,4096]{1,0:T(8,128)(2,1)}, u32[]{:S(2)}) %copy-start.10) | copy-done | bytes 4194328
  50.9 0.9 copy-done.14
  51.9 0.9 copy-done.17
  52.8 0.9 copy-done.20
  53.8 0.9 copy-done.29
  54.7 0.9 copy-done.31
  55.7 0.9 copy-done.33
  56.6 0.9 copy-done.35
  57.6 6.6 %dense.1 = (bf16[256,2048]{1,0:T(8,128)(2,1)S(1)}, bf16[256,2048]{1,0:T(8,128)(2,1)S(1)}) custom-call(s32[8]{0:T(128)S(1)} %add_multiply_fusion.offs, bf16[256,512]{1,0:T(8,128)(2,1)S(1)} %constant_dynamic-update-slice_fusion.p0.refs_0_.c0, bf16[256,512]{1,0:T(8,128)(2,1)S(1)} %copy-done.14, bf16[256,512]{1,0:T(8,128)(2,1)S(1)} %copy-done.17, ...), custom_call_target="tpu_custom_call" | custom-call | flops 3221225472 | bytes 16777248 | tf_op jit(solution)/shard_map/dense/pallas_call | solution.py:196
  64.4 1.2 collective-permute-start.3
  65.7 2.4 %collective-permute-start.4 = (bf16[512,512]{1,0:T(8,128)(2,1)S(1)}, bf16[512,512]{1,0:T(8,128)(2,1)S(1)}, u32[]{:S(2)}, u32[]{:S(2)}) collective-permute-start(bf16[512,512]{1,0:T(8,128)(2,1)S(1)} %bitcast.24), channel_id=1, source_target_pairs={{0,4},{1,5},{2,6},{3,7},{4,0},{5,1},{6,2},{7,3},{8,12},{9,13},{10,... | collective-permute-start | bytes 1572872 | tf_op jit(solution)/shard_map/ppermute | solution.py:234
  68.1 1.6 collective-permute-start.5
  69.7 10.4 %collective-permute-done.3.refs_1_ = bf16[512,512]{1,0:T(8,128)(2,1)S(1)} collective-permute-done((bf16[512,512]{1,0:T(8,128)(2,1)S(1)}, bf16[512,512]{1,0:T(8,128)(2,1)S(1)}, u32[]{:S(2)}, u32[]{:S(2)}) %collective-permute-start.3) | collective-permute-done | bytes 524320 | tf_op jit(solution)/shard_map/ppermute | solution.py:234
  80.0 11.4 %collective-permute-done.4.refs_2_ = bf16[512,512]{1,0:T(8,128)(2,1)S(1)} collective-permute-done((bf16[512,512]{1,0:T(8,128)(2,1)S(1)}, bf16[512,512]{1,0:T(8,128)(2,1)S(1)}, u32[]{:S(2)}, u32[]{:S(2)}) %collective-permute-start.4) | collective-permute-done | bytes 524320 | tf_op jit(solution)/shard_map/ppermute | solution.py:234
  92.2 1.0 copy-done.24
  93.9 2.4 %collective-permute-start.15 = (bf16[128,512]{1,0:T(8,128)(2,1)S(1)}, bf16[128,512]{1,0:T(8,128)(2,1)S(1)}, u32[]{:S(2)}, u32[]{:S(2)}) collective-permute-start(bf16[128,512]{1,0:T(8,128)(2,1)S(1)} %get-tuple-element.37), channel_id=1, source_target_pairs={{0,6},{1,7},{2,0},{3,1},{4,2},{5,3},{6,4},{7,5},{8,14},{9,15},{10,... | collective-permute-start | bytes 393224 | tf_op jit(solution)/shard_map/ppermute | solution.py:234
  96.3 1.1 collective-permute-start.16
  97.6 2.9 %back.1.g_ref = f32[512,384]{1,0:T(8,128)S(1)} custom-call(s32[8]{0:T(128)S(1)} %add_multiply_fusion.offs, bf16[512,512]{1,0:T(8,128)(2,1)S(1)} %bitcast.27, bf16[512,512]{1,0:T(8,128)(2,1)S(1)} %collective-permute-done.3.refs_1_, bf16[512,512]{1,0:T(8,128)(2,1)S(1)} %collective-permute-done.4.refs_2_, bf16[512,512]{1,0:T(8,128)(2,1)S(1)} %collective-permute-done.5.refs_3_, ...), custom_call_target="tpu_custom_call" | custom-call | flops 1610612736 | bytes 7340064 | tf_op jit(solution)/shard_map/back/pallas_call | solution.py:196
  101.4 1.1 collective-permute-done.15.d1
  103.2 0.9 collective-permute-done.16.d2
  104.8 1.4 collective-permute-done.17.d3
  106.9 4.4 %collective-permute-done.18.xo = bf16[512,2048]{1,0:T(8,128)(2,1)S(1)} collective-permute-done((bf16[512,2048]{1,0:T(8,128)(2,1)}, bf16[512,2048]{1,0:T(8,128)(2,1)S(1)}, u32[]{:S(2)}, u32[]{:S(2)}) %collective-permute-start.18) | collective-permute-done | bytes 2097184 | tf_op jit(solution)/shard_map/ppermute | solution.py:239
  111.3 1.9 copy-done.1
  113.1 1.9 copy-done.3
  115.0 1.1 copy-done.27
  116.2 8.3 %forth.1 = (bf16[512,2048]{1,0:T(8,128)(2,1)S(1)}, bf16[512,384]{1,0:T(8,128)(2,1)S(1)}, bf16[512,768]{1,0:T(8,128)(2,1)S(1)}) custom-call(s32[8]{0:T(128)S(1)} %add_multiply_fusion.offs, bf16[512,2048]{1,0:T(8,128)(2,1)} %bitcast.3.xm, bf16[512,2048]{1,0:T(8,128)(2,1)S(1)} %collective-permute-done.18.xo, f32[512,384]{1,0:T(8,128)S(1)} %copy-done.27, ...), custom_call_target="tpu_custom_call" | custom-call | flops 4026531840 | bytes 14417952 | tf_op jit(solution)/shard_map/forth/pallas_call | solution.py:196
  124.7 1.8 out.1.mine.after
  126.5 3.8 %down_o.1.after = bf16[512,2048]{1,0:T(8,128)(2,1)} custom-call(s32[8]{0:T(128)S(1)} %add_multiply_fusion.offs, bf16[512,768]{1,0:T(8,128)(2,1)S(1)} %get-tuple-element.49.dadu_ref, bf16[4096,384]{1,0:T(8,128)(2,1)S(1)} %bitcast.16, bf16[4096,384]{1,0:T(8,128)(2,1)S(1)} %bitcast.19, bf16[512,2048]{1,0:T(8,128)(2,1)S(1)} %out.1.mine.after), custom_call_target="tpu_custom_call" | custom-call | flops 1610612736 | bytes 9175072 | tf_op jit(solution)/shard_map/down_o/pallas_call | solution.py:196
  131.2 1.3 copy-done.5
  132.5 7.5 %all-to-all-start.2 = ((bf16[16,32,2048]{2,1,0:T(8,128)(2,1)}), bf16[16,32,2048]{2,1,0:T(8,128)(2,1)}, u32[]{:S(2)}, u32[]{:S(2)}) async-start(bf16[16,32,2048]{2,1,0:T(8,128)(2,1)} %bitcast.21), calls=%async_computation.2 | async-start | bytes 4194304 | tf_op jit(solution)/shard_map/all_to_all | solution.py:242
  140.0 1.9 copy-done.4
  141.9 1.1 copy-done.12
  143.0 2.4 %down_m.1.mine = bf16[512,2048]{1,0:T(8,128)(2,1)S(1)} custom-call(s32[8]{0:T(128)S(1)} %add_multiply_fusion.offs, bf16[512,768]{1,0:T(8,128)(2,1)S(1)} %copy-done.12, bf16[4096,384]{1,0:T(8,128)(2,1)S(1)} %bitcast.17, bf16[4096,384]{1,0:T(8,128)(2,1)S(1)} %bitcast.20, bf16[512,2048]{1,0:T(8,128)(2,1)} %down_o.1.after), custom_call_target="tpu_custom_call" | custom-call | flops 1610612736 | bytes 9175072 | tf_op jit(solution)/shard_map/down_m/pallas_call | solution.py:196
  145.5 3.1 %split.1 = (f32[512,512]{1,0:T(8,128)S(1)}, bf16[512,512]{1,0:T(8,128)(2,1)}, bf16[512,512]{1,0:T(8,128)(2,1)}, bf16[512,512]{1,0:T(8,128)(2,1)}) custom-call(bf16[512,2048]{1,0:T(8,128)(2,1)S(1)} %down_m.1.mine, bf16[512,2048]{1,0:T(8,128)(2,1)} %collective-permute-done.23.got), custom_call_target="tpu_custom_call" | custom-call | flops 1048576 | bytes 4194304 | tf_op jit(solution)/shard_map/split/pallas_call | solution.py:196
  148.5 1.3 collective-permute-start.24
  151.1 16.8 %all-to-all-done.2 = bf16[16,32,2048]{2,1,0:T(8,128)(2,1)} async-done(((bf16[16,32,2048]{2,1,0:T(8,128)(2,1)}), bf16[16,32,2048]{2,1,0:T(8,128)(2,1)}, u32[]{:S(2)}, u32[]{:S(2)}) %all-to-all-start.2) | async-done | bytes 2097184 | tf_op jit(solution)/shard_map/all_to_all | solution.py:242
  167.9 2.5 %mix.1 = (bf16[128,512]{1,0:T(8,128)(2,1)S(1)}, bf16[128,512]{1,0:T(8,128)(2,1)S(1)}, bf16[128,512]{1,0:T(8,128)(2,1)S(1)}, bf16[128,512]{1,0:T(8,128)(2,1)S(1)}, f32[128,128]{1,0:T(8,128)S(1)}) custom-call(bf16[512,2048]{1,0:T(8,128)(2,1)} %bitcast.8.back, bf16[256,512]{1,0:T(8,128)(2,1)S(1)} %copy-done.23, f32[128,2]{1,0:T(8,128)S(1)} %copy.14.gates_ref.gates, ...), custom_call_target="tpu_custom_call" | custom-call | flops 536870912 | bytes 4457472 | tf_op jit(solution)/shard_map/mix/pallas_call | solution.py:196
  170.6 5.3 %collective-permute-done.26.p3 = bf16[512,512]{1,0:T(8,128)(2,1)} collective-permute-done((bf16[512,512]{1,0:T(8,128)(2,1)}, bf16[512,512]{1,0:T(8,128)(2,1)}, u32[]{:S(2)}, u32[]{:S(2)}) %collective-permute-start.26) | collective-permute-done | bytes 524320 | tf_op jit(solution)/shard_map/ppermute | solution.py:234
  175.9 2.5 %sum.1 = bf16[512,512]{1,0:T(8,128)(2,1)} custom-call(f32[512,512]{1,0:T(8,128)S(1)} %get-tuple-element.50.p0, bf16[512,512]{1,0:T(8,128)(2,1)} %collective-permute-done.24.p1, bf16[512,512]{1,0:T(8,128)(2,1)} %collective-permute-done.25.p2, bf16[512,512]{1,0:T(8,128)(2,1)} %collective-permute-done.26.p3, f32[128,128]{1,0:T(8,128)S(1)} %get-tuple-element.54.after), custom_call_target="tpu_custom_call" | custom-call | flops 786432 | bytes 2686976 | tf_op jit(solution)/shard_map/sum/pallas_call | solution.py:196
  178.4 7.2 %all-to-all-start.3 = ((bf16[16,32,512]{2,1,0:T(8,128)(2,1)}), bf16[16,32,512]{2,1,0:T(8,128)(2,1)S(1)}, u32[]{:S(2)}, u32[]{:S(2)}) async-start(bf16[16,32,512]{2,1,0:T(8,128)(2,1)} %bitcast.9), calls=%async_computation.3 | async-start | bytes 1048576 | tf_op jit(solution)/shard_map/all_to_all | solution.py:242
  185.7 2.2 %collective-permute-start.29 = (f32[128,2]{1,0:T(8,128)S(1)}, f32[128,2]{1,0:T(8,128)S(1)}, u32[]{:S(2)}, u32[]{:S(2)}) collective-permute-start(f32[128,2]{1,0:T(8,128)S(1)} %slice_add_fusion), channel_id=1, source_target_pairs={{0,4},{1,5},{2,6},{3,7},{4,0},{5,1},{6,2},{7,3},{8,12},{9,13},{10,... | collective-permute-start | bytes 3080 | tf_op jit(solution)/shard_map/ppermute | solution.py:234
  187.9 1.0 collective-permute-start.30
  188.9 0.9 collective-permute-start.20
  189.9 2.1 %collective-permute-start.21 = (bf16[128,512]{1,0:T(8,128)(2,1)}, bf16[128,512]{1,0:T(8,128)(2,1)S(1)}, u32[]{:S(2)}, u32[]{:S(2)}) collective-permute-start(bf16[128,512]{1,0:T(8,128)(2,1)} %copy-done.47), channel_id=1, source_target_pairs={{0,4},{1,5},{2,6},{3,7},{4,0},{5,1},{6,2},{7,3},{8,12},{9,13},{10,... | collective-permute-start | bytes 393224 | tf_op jit(solution)/shard_map/ppermute | solution.py:234
  192.0 1.3 collective-permute-start.22
  193.3 0.9 collective-permute-done.30
  194.9 1.6 collective-permute-done.20
  197.0 1.4 collective-permute-done.22
  198.4 1.6 add_convert_fusion
  200.1 0.9 grad.1
  (128 shorter events, 14.6 us)
Async XLA Ops:
  4.9 27.9 %copy-start.22 = (bf16[256,512]{1,0:T(8,128)(2,1)}, bf16[256,512]{1,0:T(8,128)(2,1)S(1)}, u32[]{:S(2)}) copy-start(bf16[256,512]{1,0:T(8,128)(2,1)S(1)} %get-tuple-element.31.pick_ref.pick) | copy-start | bytes 786436
  4.9 25.8 %all-to-all-start = ((bf16[16,32,512]{2,1,0:T(8,128)(2,1)}), bf16[16,32,512]{2,1,0:T(8,128)(2,1)S(1)}, u32[]{:S(2)}, u32[]{:S(2)}) async-start(bf16[16,32,512]{2,1,0:T(8,128)(2,1)} %bitcast), calls=%async_computation | async-start | bytes 1048576 | tf_op jit(solution)/shard_map/all_to_all | solution.py:242
  15.1 9.4 %collective-permute-start = (bf16[256,512]{1,0:T(8,128)(2,1)S(1)}, bf16[256,512]{1,0:T(8,128)(2,1)S(1)}, u32[]{:S(2)}, u32[]{:S(2)}) collective-permute-start(bf16[256,512]{1,0:T(8,128)(2,1)S(1)} %constant_dynamic-update-slice_fusion.p0.refs_0_.c0), channel_id=1, source_target_pairs={{0,2},{1,3},{2,4},{3,5},{4,6},{5,7},{6,0},{7,1},{8,10},{9,11},{10,... | collective-permute-start | bytes 786440 | tf_op jit(solution)/shard_map/ppermute | solution.py:234
  16.7 14.0 %collective-permute-start.1 = (bf16[256,512]{1,0:T(8,128)(2,1)S(1)}, bf16[256,512]{1,0:T(8,128)(2,1)S(1)}, u32[]{:S(2)}, u32[]{:S(2)}) collective-permute-start(bf16[256,512]{1,0:T(8,128)(2,1)S(1)} %constant_dynamic-update-slice_fusion.p0.refs_0_.c0), channel_id=1, source_target_pairs={{0,4},{1,5},{2,6},{3,7},{4,0},{5,1},{6,2},{7,3},{8,12},{9,13},{10,... | collective-permute-start | bytes 786440 | tf_op jit(solution)/shard_map/ppermute | solution.py:234
  19.6 11.1 %collective-permute-start.2 = (bf16[256,512]{1,0:T(8,128)(2,1)S(1)}, bf16[256,512]{1,0:T(8,128)(2,1)S(1)}, u32[]{:S(2)}, u32[]{:S(2)}) collective-permute-start(bf16[256,512]{1,0:T(8,128)(2,1)S(1)} %constant_dynamic-update-slice_fusion.p0.refs_0_.c0), channel_id=1, source_target_pairs={{0,6},{1,7},{2,0},{3,1},{4,2},{5,3},{6,4},{7,5},{8,14},{9,15},{10,... | collective-permute-start | bytes 786440 | tf_op jit(solution)/shard_map/ppermute | solution.py:234
  24.4 15.6 %copy-start.13 = (bf16[256,512]{1,0:T(8,128)(2,1)}, bf16[256,512]{1,0:T(8,128)(2,1)S(1)}, u32[]{:S(2)}) copy-start(bf16[256,512]{1,0:T(8,128)(2,1)S(1)} %collective-permute-done.p1.refs_1_.c1) | copy-start | bytes 786436
  30.7 9.9 %copy-start.16 = (bf16[256,512]{1,0:T(8,128)(2,1)}, bf16[256,512]{1,0:T(8,128)(2,1)S(1)}, u32[]{:S(2)}) copy-start(bf16[256,512]{1,0:T(8,128)(2,1)S(1)} %collective-permute-done.1.p2.refs_2_.c2) | copy-start | bytes 786436
  30.7 10.0 %copy-start.19 = (bf16[256,512]{1,0:T(8,128)(2,1)}, bf16[256,512]{1,0:T(8,128)(2,1)S(1)}, u32[]{:S(2)}) copy-start(bf16[256,512]{1,0:T(8,128)(2,1)S(1)} %collective-permute-done.2.p3.refs_3_.c3) | copy-start | bytes 786436
  30.7 2.1 %copy-start.6 = (bf16[16,32,512]{2,1,0:T(8,128)(2,1)}, bf16[16,32,512]{2,1,0:T(8,128)(2,1)S(1)}, u32[]{:S(2)}) copy-start(bf16[16,32,512]{2,1,0:T(8,128)(2,1)S(1)} %all-to-all-done) | copy-start | bytes 1572868
  32.8 74.1 %all-to-all-start.1 = ((bf16[16,32,2048]{2,1,0:T(8,128)(2,1)}), bf16[16,32,2048]{2,1,0:T(8,128)(2,1)}, u32[]{:S(2)}, u32[]{:S(2)}) async-start(bf16[16,32,2048]{2,1,0:T(8,128)(2,1)} %bitcast.2), calls=%async_computation.1 | async-start | bytes 4194304 | tf_op jit(solution)/shard_map/all_to_all | solution.py:242
  40.0 1.5 collective-permute-start.10
  40.0 2.2 %collective-permute-start.11 = (bf16[256,512]{1,0:T(8,128)(2,1)S(1)}, bf16[256,512]{1,0:T(8,128)(2,1)S(1)}, u32[]{:S(2)}, u32[]{:S(2)}) collective-permute-start(bf16[256,512]{1,0:T(8,128)(2,1)S(1)} %collective-permute-done.p1.refs_1_.c1), channel_id=1, source_target_pairs={{0,1},{1,0},{2,3},{3,2},{4,5},{5,4},{6,7},{7,6},{8,9},{9,8},{10,11... | collective-permute-start | bytes 786440 | tf_op jit(solution)/shard_map/ppermute | solution.py:239
  40.5 2.4 %collective-permute-start.12 = (bf16[256,512]{1,0:T(8,128)(2,1)S(1)}, bf16[256,512]{1,0:T(8,128)(2,1)S(1)}, u32[]{:S(2)}, u32[]{:S(2)}) collective-permute-start(bf16[256,512]{1,0:T(8,128)(2,1)S(1)} %collective-permute-done.1.p2.refs_2_.c2), channel_id=1, source_target_pairs={{0,1},{1,0},{2,3},{3,2},{4,5},{5,4},{6,7},{7,6},{8,9},{9,8},{10,11... | collective-permute-start | bytes 786440 | tf_op jit(solution)/shard_map/ppermute | solution.py:239
  40.6 3.0 %collective-permute-start.13 = (bf16[256,512]{1,0:T(8,128)(2,1)S(1)}, bf16[256,512]{1,0:T(8,128)(2,1)S(1)}, u32[]{:S(2)}, u32[]{:S(2)}) collective-permute-start(bf16[256,512]{1,0:T(8,128)(2,1)S(1)} %collective-permute-done.2.p3.refs_3_.c3), channel_id=1, source_target_pairs={{0,1},{1,0},{2,3},{3,2},{4,5},{5,4},{6,7},{7,6},{8,9},{9,8},{10,11... | collective-permute-start | bytes 786440 | tf_op jit(solution)/shard_map/ppermute | solution.py:239
  41.1 23.3 %copy-start.7 = (bf16[16,32,512]{2,1,0:T(8,128)(2,1)S(1)}, bf16[16,32,512]{2,1,0:T(8,128)(2,1)}, u32[]{:S(2)}) copy-start(bf16[16,32,512]{2,1,0:T(8,128)(2,1)} %copy-done.6) | copy-start | bytes 1572868
  44.4 2.2 %copy-start.8 = (bf16[4096,512]{1,0:T(8,128)(2,1)S(1)}, bf16[4096,512]{1,0:T(8,128)(2,1)}, u32[]{:S(2)}) copy-start(bf16[4096,512]{1,0:T(8,128)(2,1)} %refs_9_.1) | copy-start | bytes 12582916
  46.6 2.2 %copy-start.9 = (bf16[4096,512]{1,0:T(8,128)(2,1)S(1)}, bf16[4096,512]{1,0:T(8,128)(2,1)}, u32[]{:S(2)}) copy-start(bf16[4096,512]{1,0:T(8,128)(2,1)} %refs_10_.1) | copy-start | bytes 12582916
  48.7 2.2 %copy-start.10 = (bf16[512,4096]{1,0:T(8,128)(2,1)S(1)}, bf16[512,4096]{1,0:T(8,128)(2,1)}, u32[]{:S(2)}) copy-start(bf16[512,4096]{1,0:T(8,128)(2,1)} %refs_11_.1) | copy-start | bytes 12582916
  57.6 40.1 %copy-start = (bf16[1,384,4096]{2,1,0:T(8,128)(2,1)S(1)}, bf16[1,384,4096]{2,1,0:T(8,128)(2,1)}, u32[]{:S(2)}) copy-start(bf16[1,384,4096]{2,1,0:T(8,128)(2,1)} %param.19) | copy-start | bytes 9437188
  64.2 27.8 %collective-permute-start.14 = (bf16[256,2048]{1,0:T(8,128)(2,1)S(1)}, bf16[256,2048]{1,0:T(8,128)(2,1)S(1)}, u32[]{:S(2)}, u32[]{:S(2)}) collective-permute-start(bf16[256,2048]{1,0:T(8,128)(2,1)S(1)} %get-tuple-element.34), channel_id=1, source_target_pairs={{0,1},{1,0},{2,3},{3,2},{4,5},{5,4},{6,7},{7,6},{8,9},{9,8},{10,11... | collective-permute-start | bytes 3145736 | tf_op jit(solution)/shard_map/ppermute | solution.py:239
  64.4 15.6 %collective-permute-start.3 = (bf16[512,512]{1,0:T(8,128)(2,1)S(1)}, bf16[512,512]{1,0:T(8,128)(2,1)S(1)}, u32[]{:S(2)}, u32[]{:S(2)}) collective-permute-start(bf16[512,512]{1,0:T(8,128)(2,1)S(1)} %bitcast.23), channel_id=1, source_target_pairs={{0,2},{1,3},{2,4},{3,5},{4,6},{5,7},{6,0},{7,1},{8,10},{9,11},{10,... | collective-permute-start | bytes 1572872 | tf_op jit(solution)/shard_map/ppermute | solution.py:234
  65.7 25.8 %collective-permute-start.4 = (bf16[512,512]{1,0:T(8,128)(2,1)S(1)}, bf16[512,512]{1,0:T(8,128)(2,1)S(1)}, u32[]{:S(2)}, u32[]{:S(2)}) collective-permute-start(bf16[512,512]{1,0:T(8,128)(2,1)S(1)} %bitcast.24), channel_id=1, source_target_pairs={{0,4},{1,5},{2,6},{3,7},{4,0},{5,1},{6,2},{7,3},{8,12},{9,13},{10,... | collective-permute-start | bytes 1572872 | tf_op jit(solution)/shard_map/ppermute | solution.py:234
  68.1 23.6 %collective-permute-start.5 = (bf16[512,512]{1,0:T(8,128)(2,1)S(1)}, bf16[512,512]{1,0:T(8,128)(2,1)S(1)}, u32[]{:S(2)}, u32[]{:S(2)}) collective-permute-start(bf16[512,512]{1,0:T(8,128)(2,1)S(1)} %bitcast.25), channel_id=1, source_target_pairs={{0,6},{1,7},{2,0},{3,1},{4,2},{5,3},{6,4},{7,5},{8,14},{9,15},{10,... | collective-permute-start | bytes 1572872 | tf_op jit(solution)/shard_map/ppermute | solution.py:234
  69.7 26.6 %collective-permute-start.6 = (bf16[512,512]{1,0:T(8,128)(2,1)S(1)}, bf16[512,512]{1,0:T(8,128)(2,1)S(1)}, u32[]{:S(2)}, u32[]{:S(2)}) collective-permute-start(bf16[512,512]{1,0:T(8,128)(2,1)S(1)} %bitcast.26), channel_id=1, source_target_pairs={{0,1},{1,0},{2,3},{3,2},{4,5},{5,4},{6,7},{7,6},{8,9},{9,8},{10,11... | collective-permute-start | bytes 1572872 | tf_op jit(solution)/shard_map/ppermute | solution.py:239
  80.0 17.4 %collective-permute-start.7 = (bf16[512,512]{1,0:T(8,128)(2,1)S(1)}, bf16[512,512]{1,0:T(8,128)(2,1)S(1)}, u32[]{:S(2)}, u32[]{:S(2)}) collective-permute-start(bf16[512,512]{1,0:T(8,128)(2,1)S(1)} %collective-permute-done.3.refs_1_), channel_id=1, source_target_pairs={{0,1},{1,0},{2,3},{3,2},{4,5},{5,4},{6,7},{7,6},{8,9},{9,8},{10,11... | collective-permute-start | bytes 1572872 | tf_op jit(solution)/shard_map/ppermute | solution.py:239
  91.5 6.2 %collective-permute-start.8 = (bf16[512,512]{1,0:T(8,128)(2,1)S(1)}, bf16[512,512]{1,0:T(8,128)(2,1)S(1)}, u32[]{:S(2)}, u32[]{:S(2)}) collective-permute-start(bf16[512,512]{1,0:T(8,128)(2,1)S(1)} %collective-permute-done.4.refs_2_), channel_id=1, source_target_pairs={{0,1},{1,0},{2,3},{3,2},{4,5},{5,4},{6,7},{7,6},{8,9},{9,8},{10,11... | collective-permute-start | bytes 1572872 | tf_op jit(solution)/shard_map/ppermute | solution.py:239
  91.7 5.9 %collective-permute-start.9 = (bf16[512,512]{1,0:T(8,128)(2,1)S(1)}, bf16[512,512]{1,0:T(8,128)(2,1)S(1)}, u32[]{:S(2)}, u32[]{:S(2)}) collective-permute-start(bf16[512,512]{1,0:T(8,128)(2,1)S(1)} %collective-permute-done.5.refs_3_), channel_id=1, source_target_pairs={{0,1},{1,0},{2,3},{3,2},{4,5},{5,4},{6,7},{7,6},{8,9},{9,8},{10,11... | collective-permute-start | bytes 1572872 | tf_op jit(solution)/shard_map/ppermute | solution.py:239
  93.9 8.6 %collective-permute-start.15 = (bf16[128,512]{1,0:T(8,128)(2,1)S(1)}, bf16[128,512]{1,0:T(8,128)(2,1)S(1)}, u32[]{:S(2)}, u32[]{:S(2)}) collective-permute-start(bf16[128,512]{1,0:T(8,128)(2,1)S(1)} %get-tuple-element.37), channel_id=1, source_target_pairs={{0,6},{1,7},{2,0},{3,1},{4,2},{5,3},{6,4},{7,5},{8,14},{9,15},{10,... | collective-permute-start | bytes 393224 | tf_op jit(solution)/shard_map/ppermute | solution.py:234
  96.3 7.8 %collective-permute-start.16 = (bf16[128,512]{1,0:T(8,128)(2,1)S(1)}, bf16[128,512]{1,0:T(8,128)(2,1)S(1)}, u32[]{:S(2)}, u32[]{:S(2)}) collective-permute-start(bf16[128,512]{1,0:T(8,128)(2,1)S(1)} %get-tuple-element.38), channel_id=1, source_target_pairs={{0,4},{1,5},{2,6},{3,7},{4,0},{5,1},{6,2},{7,3},{8,12},{9,13},{10,... | collective-permute-start | bytes 393224 | tf_op jit(solution)/shard_map/ppermute | solution.py:234
  97.4 8.8 %collective-permute-start.17 = (bf16[128,512]{1,0:T(8,128)(2,1)S(1)}, bf16[128,512]{1,0:T(8,128)(2,1)S(1)}, u32[]{:S(2)}, u32[]{:S(2)}) collective-permute-start(bf16[128,512]{1,0:T(8,128)(2,1)S(1)} %get-tuple-element.39), channel_id=1, source_target_pairs={{0,2},{1,3},{2,4},{3,5},{4,6},{5,7},{6,0},{7,1},{8,10},{9,11},{10,... | collective-permute-start | bytes 393224 | tf_op jit(solution)/shard_map/ppermute | solution.py:234
  106.9 4.4 %collective-permute-start.18 = (bf16[512,2048]{1,0:T(8,128)(2,1)}, bf16[512,2048]{1,0:T(8,128)(2,1)S(1)}, u32[]{:S(2)}, u32[]{:S(2)}) collective-permute-start(bf16[512,2048]{1,0:T(8,128)(2,1)} %bitcast.3.xm), channel_id=1, source_target_pairs={{0,1},{1,0},{2,3},{3,2},{4,5},{5,4},{6,7},{7,6},{8,9},{9,8},{10,11... | collective-permute-start | bytes 6291464 | tf_op jit(solution)/shard_map/ppermute | solution.py:239
  111.3 1.9 copy-start.1
  113.1 1.9 copy-start.3
  124.5 2.0 %copy-start.11 = (bf16[512,768]{1,0:T(8,128)(2,1)}, bf16[512,768]{1,0:T(8,128)(2,1)S(1)}, u32[]{:S(2)}) copy-start(bf16[512,768]{1,0:T(8,128)(2,1)S(1)} %get-tuple-element.49.dadu_ref) | copy-start | bytes 2359300
  124.5 6.2 %collective-permute-start.19 = (bf16[512,2048]{1,0:T(8,128)(2,1)S(1)}, bf16[512,2048]{1,0:T(8,128)(2,1)S(1)}, u32[]{:S(2)}, u32[]{:S(2)}) collective-permute-start(bf16[512,2048]{1,0:T(8,128)(2,1)S(1)} %get-tuple-element.43), channel_id=1, source_target_pairs={{0,1},{1,0},{2,3},{3,2},{4,5},{5,4},{6,7},{7,6},{8,9},{9,8},{10,11... | collective-permute-start | bytes 6291464 | tf_op jit(solution)/shard_map/ppermute | solution.py:239
  130.3 15.2 %collective-permute-start.23 = (bf16[512,2048]{1,0:T(8,128)(2,1)}, bf16[512,2048]{1,0:T(8,128)(2,1)}, u32[]{:S(2)}, u32[]{:S(2)}) collective-permute-start(bf16[512,2048]{1,0:T(8,128)(2,1)} %down_o.1.after), channel_id=1, source_target_pairs={{0,1},{1,0},{2,3},{3,2},{4,5},{5,4},{6,7},{7,6},{8,9},{9,8},{10,11... | collective-permute-start | bytes 6291464 | tf_op jit(solution)/shard_map/ppermute | solution.py:239
  131.1 1.4 copy-start.5
  132.5 7.5 %copy-start.2 = (bf16[1,4096,384]{2,1,0:T(8,128)(2,1)S(1)}, bf16[1,4096,384]{2,1,0:T(8,128)(2,1)}, u32[]{:S(2)}) copy-start(bf16[1,4096,384]{2,1,0:T(8,128)(2,1)} %param.17) | copy-start | bytes 9437188
  132.5 35.4 %all-to-all-start.2 = ((bf16[16,32,2048]{2,1,0:T(8,128)(2,1)}), bf16[16,32,2048]{2,1,0:T(8,128)(2,1)}, u32[]{:S(2)}, u32[]{:S(2)}) async-start(bf16[16,32,2048]{2,1,0:T(8,128)(2,1)} %bitcast.21), calls=%async_computation.2 | async-start | bytes 4194304 | tf_op jit(solution)/shard_map/all_to_all | solution.py:242
  140.0 1.9 copy-start.4
  145.4 22.5 %copy-start.15 = (bf16[256,512]{1,0:T(8,128)(2,1)S(1)}, bf16[256,512]{1,0:T(8,128)(2,1)}, u32[]{:S(2)}) copy-start(bf16[256,512]{1,0:T(8,128)(2,1)} %copy-done.13) | copy-start | bytes 786436
  145.4 22.5 %copy-start.18 = (bf16[256,512]{1,0:T(8,128)(2,1)S(1)}, bf16[256,512]{1,0:T(8,128)(2,1)}, u32[]{:S(2)}) copy-start(bf16[256,512]{1,0:T(8,128)(2,1)} %copy-done.16) | copy-start | bytes 786436
  145.4 22.5 %copy-start.21 = (bf16[256,512]{1,0:T(8,128)(2,1)S(1)}, bf16[256,512]{1,0:T(8,128)(2,1)}, u32[]{:S(2)}) copy-start(bf16[256,512]{1,0:T(8,128)(2,1)} %copy-done.19) | copy-start | bytes 786436
  145.4 22.5 %copy-start.23 = (bf16[256,512]{1,0:T(8,128)(2,1)S(1)}, bf16[256,512]{1,0:T(8,128)(2,1)}, u32[]{:S(2)}) copy-start(bf16[256,512]{1,0:T(8,128)(2,1)} %copy-done.22) | copy-start | bytes 786436
  145.4 22.5 %copy-start.25 = (f32[128,2048]{1,0:T(8,128)S(1)}, f32[128,2048]{1,0:T(8,128)}, u32[]{:S(2)}) copy-start(f32[128,2048]{1,0:T(8,128)} %copy-done.24) | copy-start | bytes 3145732
  148.5 22.0 %collective-permute-start.24 = (bf16[512,512]{1,0:T(8,128)(2,1)}, bf16[512,512]{1,0:T(8,128)(2,1)}, u32[]{:S(2)}, u32[]{:S(2)}) collective-permute-start(bf16[512,512]{1,0:T(8,128)(2,1)} %get-tuple-element.51), channel_id=1, source_target_pairs={{0,6},{1,7},{2,0},{3,1},{4,2},{5,3},{6,4},{7,5},{8,14},{9,15},{10,... | collective-permute-start | bytes 1572872 | tf_op jit(solution)/shard_map/ppermute | solution.py:234
  149.9 20.7 %collective-permute-start.25 = (bf16[512,512]{1,0:T(8,128)(2,1)}, bf16[512,512]{1,0:T(8,128)(2,1)}, u32[]{:S(2)}, u32[]{:S(2)}) collective-permute-start(bf16[512,512]{1,0:T(8,128)(2,1)} %get-tuple-element.52), channel_id=1, source_target_pairs={{0,4},{1,5},{2,6},{3,7},{4,0},{5,1},{6,2},{7,3},{8,12},{9,13},{10,... | collective-permute-start | bytes 1572872 | tf_op jit(solution)/shard_map/ppermute | solution.py:234
  150.2 25.6 %collective-permute-start.26 = (bf16[512,512]{1,0:T(8,128)(2,1)}, bf16[512,512]{1,0:T(8,128)(2,1)}, u32[]{:S(2)}, u32[]{:S(2)}) collective-permute-start(bf16[512,512]{1,0:T(8,128)(2,1)} %get-tuple-element.53), channel_id=1, source_target_pairs={{0,2},{1,3},{2,4},{3,5},{4,6},{5,7},{6,0},{7,1},{8,10},{9,11},{10,... | collective-permute-start | bytes 1572872 | tf_op jit(solution)/shard_map/ppermute | solution.py:234
  170.4 7.9 %copy-start.44 = (bf16[128,512]{1,0:T(8,128)(2,1)}, bf16[128,512]{1,0:T(8,128)(2,1)S(1)}, u32[]{:S(2)}) copy-start(bf16[128,512]{1,0:T(8,128)(2,1)S(1)} %get-tuple-element.45) | copy-start | bytes 393220
  170.4 7.9 %copy-start.46 = (bf16[128,512]{1,0:T(8,128)(2,1)}, bf16[128,512]{1,0:T(8,128)(2,1)S(1)}, u32[]{:S(2)}) copy-start(bf16[128,512]{1,0:T(8,128)(2,1)S(1)} %get-tuple-element.48) | copy-start | bytes 393220
  170.4 7.9 %copy-start.47 = (bf16[128,512]{1,0:T(8,128)(2,1)}, bf16[128,512]{1,0:T(8,128)(2,1)S(1)}, u32[]{:S(2)}) copy-start(bf16[128,512]{1,0:T(8,128)(2,1)S(1)} %get-tuple-element.47) | copy-start | bytes 393220
  170.5 7.9 %copy-start.48 = (bf16[128,512]{1,0:T(8,128)(2,1)}, bf16[128,512]{1,0:T(8,128)(2,1)S(1)}, u32[]{:S(2)}) copy-start(bf16[128,512]{1,0:T(8,128)(2,1)S(1)} %get-tuple-element.46) | copy-start | bytes 393220
  170.5 15.1 %collective-permute-start.27 = (f32[128,2]{1,0:T(8,128)S(1)}, f32[128,2]{1,0:T(8,128)S(1)}, u32[]{:S(2)}, u32[]{:S(2)}) collective-permute-start(f32[128,2]{1,0:T(8,128)S(1)} %bitcast.29), channel_id=1, source_target_pairs={{0,1},{1,0},{2,3},{3,2},{4,5},{5,4},{6,7},{7,6},{8,9},{9,8},{10,11... | collective-permute-start | bytes 3080 | tf_op jit(solution)/shard_map/ppermute | solution.py:239
  175.9 24.2 %copy-start.37 = (f32[128,512]{1,0:T(8,128)S(1)}, f32[128,512]{1,0:T(8,128)}, u32[]{:S(2)}) copy-start(f32[128,512]{1,0:T(8,128)} %copy-done.36) | copy-start | bytes 786436
  175.9 24.2 %copy-start.39 = (bf16[128,512]{1,0:T(8,128)(2,1)S(1)}, bf16[128,512]{1,0:T(8,128)(2,1)}, u32[]{:S(2)}) copy-start(bf16[128,512]{1,0:T(8,128)(2,1)} %copy-done.38) | copy-start | bytes 393220
  175.9 24.2 %copy-start.41 = (bf16[128,512]{1,0:T(8,128)(2,1)S(1)}, bf16[128,512]{1,0:T(8,128)(2,1)}, u32[]{:S(2)}) copy-start(bf16[128,512]{1,0:T(8,128)(2,1)} %copy-done.40) | copy-start | bytes 393220
  175.9 24.2 %copy-start.43 = (bf16[128,512]{1,0:T(8,128)(2,1)S(1)}, bf16[128,512]{1,0:T(8,128)(2,1)}, u32[]{:S(2)}) copy-start(bf16[128,512]{1,0:T(8,128)(2,1)} %copy-done.42) | copy-start | bytes 393220
  178.4 21.7 %all-to-all-start.3 = ((bf16[16,32,512]{2,1,0:T(8,128)(2,1)}), bf16[16,32,512]{2,1,0:T(8,128)(2,1)S(1)}, u32[]{:S(2)}, u32[]{:S(2)}) async-start(bf16[16,32,512]{2,1,0:T(8,128)(2,1)} %bitcast.9), calls=%async_computation.3 | async-start | bytes 1048576 | tf_op jit(solution)/shard_map/all_to_all | solution.py:242
  185.6 6.4 %collective-permute-start.28 = (f32[128,2]{1,0:T(8,128)S(1)}, f32[128,2]{1,0:T(8,128)S(1)}, u32[]{:S(2)}, u32[]{:S(2)}) collective-permute-start(f32[128,2]{1,0:T(8,128)S(1)} %slice_add_fusion), channel_id=1, source_target_pairs={{0,2},{1,3},{2,4},{3,5},{4,6},{5,7},{6,0},{7,1},{8,10},{9,11},{10,... | collective-permute-start | bytes 3080 | tf_op jit(solution)/shard_map/ppermute | solution.py:234
  185.7 7.6 %collective-permute-start.29 = (f32[128,2]{1,0:T(8,128)S(1)}, f32[128,2]{1,0:T(8,128)S(1)}, u32[]{:S(2)}, u32[]{:S(2)}) collective-permute-start(f32[128,2]{1,0:T(8,128)S(1)} %slice_add_fusion), channel_id=1, source_target_pairs={{0,4},{1,5},{2,6},{3,7},{4,0},{5,1},{6,2},{7,3},{8,12},{9,13},{10,... | collective-permute-start | bytes 3080 | tf_op jit(solution)/shard_map/ppermute | solution.py:234
  187.9 6.3 %collective-permute-start.30 = (f32[128,2]{1,0:T(8,128)S(1)}, f32[128,2]{1,0:T(8,128)S(1)}, u32[]{:S(2)}, u32[]{:S(2)}) collective-permute-start(f32[128,2]{1,0:T(8,128)S(1)} %slice_add_fusion), channel_id=1, source_target_pairs={{0,6},{1,7},{2,0},{3,1},{4,2},{5,3},{6,4},{7,5},{8,14},{9,15},{10,... | collective-permute-start | bytes 3080 | tf_op jit(solution)/shard_map/ppermute | solution.py:234
  188.9 7.5 %collective-permute-start.20 = (bf16[128,512]{1,0:T(8,128)(2,1)}, bf16[128,512]{1,0:T(8,128)(2,1)S(1)}, u32[]{:S(2)}, u32[]{:S(2)}) collective-permute-start(bf16[128,512]{1,0:T(8,128)(2,1)} %copy-done.48), channel_id=1, source_target_pairs={{0,6},{1,7},{2,0},{3,1},{4,2},{5,3},{6,4},{7,5},{8,14},{9,15},{10,... | collective-permute-start | bytes 393224 | tf_op jit(solution)/shard_map/ppermute | solution.py:234
  189.9 7.1 %collective-permute-start.21 = (bf16[128,512]{1,0:T(8,128)(2,1)}, bf16[128,512]{1,0:T(8,128)(2,1)S(1)}, u32[]{:S(2)}, u32[]{:S(2)}) collective-permute-start(bf16[128,512]{1,0:T(8,128)(2,1)} %copy-done.47), channel_id=1, source_target_pairs={{0,4},{1,5},{2,6},{3,7},{4,0},{5,1},{6,2},{7,3},{8,12},{9,13},{10,... | collective-permute-start | bytes 393224 | tf_op jit(solution)/shard_map/ppermute | solution.py:234
  192.0 6.4 %collective-permute-start.22 = (bf16[128,512]{1,0:T(8,128)(2,1)}, bf16[128,512]{1,0:T(8,128)(2,1)S(1)}, u32[]{:S(2)}, u32[]{:S(2)}) collective-permute-start(bf16[128,512]{1,0:T(8,128)(2,1)} %copy-done.46), channel_id=1, source_target_pairs={{0,2},{1,3},{2,4},{3,5},{4,6},{5,7},{6,0},{7,1},{8,10},{9,11},{10,... | collective-permute-start | bytes 393224 | tf_op jit(solution)/shard_map/ppermute | solution.py:234
  (20 other events, 17.2 us)

commit v2 on v1

v2 whole, which is shorter than its diff:
```python
import functools

import jax
import jax.numpy as jnp
from jax import lax
from jax.experimental import pallas as pl
from jax.experimental.pallas import tpu as pltpu
from jax.sharding import PartitionSpec as P

F32 = jnp.float32
BF16 = jnp.bfloat16
MIB = 1 << 20
CAPACITY = 32
SIDES = 4


def dot(a, b, contract=((1,), (0,))):
    return lax.dot_general(a, b, (contract, ((), ())), preferred_element_type=F32)


def dot_nt(a, b):
    return dot(a, b, ((1,), (1,)))


def dot_tn(a, b):
    return dot(a, b, ((0,), (0,)))


def gate_terms(a, b):
    s = jax.nn.sigmoid(a)
    act = a * s
    return act, (act * b).astype(BF16), b * s * (1.0 + a * (1.0 - s))


def plan_kernel(routes_ref, gates_ref, cotan_ref, pick_ref, send_ref):
    rows = routes_ref.shape[0]
    slots = pick_ref.shape[1]
    lane = lax.broadcasted_iota(jnp.int32, (rows, 128), 1)
    one = [(routes_ref[:, k : k + 1] == lane).astype(F32) for k in range(2)]
    lower = (
        lax.broadcasted_iota(jnp.int32, (rows, rows), 1)
        < lax.broadcasted_iota(jnp.int32, (rows, rows), 0)
    ).astype(BF16)
    earlier = dot(lower, (one[0] + one[1]).astype(BF16))
    place = lax.broadcasted_iota(jnp.int32, (rows, slots), 1)
    cotan = cotan_ref[...].astype(F32)
    total = None
    for k in range(2):
        pos = jnp.sum(earlier * one[k], axis=1, keepdims=True).astype(jnp.int32)
        slot = routes_ref[:, k : k + 1] * CAPACITY + pos
        pick = (slot == place).astype(BF16)
        pick_ref[k * rows : (k + 1) * rows, :] = pick
        scaled = (gates_ref[:, k : k + 1] * cotan).astype(BF16)
        term = dot_tn(pick, scaled)
        total = term if total is None else total + term
    send_ref[...] = total.astype(BF16)


def rows_kernel(pick_ref, p0, p1, p2, p3, after, send_ref, pack_ref):
    rows = p0.shape[0] // 2
    width = p0.shape[1]
    pick = pick_ref[:rows, :] + pick_ref[rows:, :]
    for d, piece in enumerate((p0, p1, p2, p3)):
        pack_ref[d] = piece[...]
        send_ref[:, d * width : (d + 1) * width] = dot_tn(pick, piece[:rows, :]).astype(BF16)


def starts(width):
    me = lax.axis_index("tensor")
    chip, core = me // 2, lax.rem(me, 2)
    chips = [lax.rem(chip + SIDES - d, SIDES) for d in range(SIDES)]
    mine = [pl.multiple_of((2 * c + core) * width, width) for c in chips]
    other = [pl.multiple_of((2 * c + 1 - core) * width, width) for c in chips]
    return mine + other


class Loads:
    def __init__(self, sems):
        self.sems = sems
        self.count = 0

    def __call__(self, src, dst):
        copy = pltpu.make_async_copy(src, dst, self.sems.at[self.count])
        copy.start()
        self.count += 1
        return copy


def wait(copies):
    for copy in copies:
        copy.wait()


def dense_kernel(*refs):
    sides, (wg, wu, wd), outs = refs[:2], refs[2:5], refs[5:7]
    xs, ws, vs, sems = refs[7:]
    rows = xs.shape[1] // 2
    width = xs.shape[2]
    units = wg.shape[1]
    load = Loads(sems)
    copies = []
    for i, at in enumerate(starts(width)):
        copies.append(
            [
                load(sides[i // 4].at[i % 4], xs.at[i]),
                load(wg.at[pl.ds(at, width), :], ws.at[i, :, pl.ds(0, units)]),
                load(wu.at[pl.ds(at, width), :], ws.at[i, :, pl.ds(units, units)]),
                load(wd.at[:, pl.ds(at, width)], vs.at[i]),
            ]
        )
    ab = g = None
    for i in range(8):
        wait(copies[i])
        tab = dot(xs[i, :rows, :], ws[i])
        tg = dot_nt(xs[i, rows:, :], vs[i])
        ab, g = (tab, tg) if ab is None else (ab + tab, g + tg)
    act, hidden, slope = gate_terms(ab[:, :units], ab[:, units:])
    dadu = jnp.concatenate([(g * slope).astype(BF16), (g * act).astype(BF16)], axis=1)
    for i in range(8):
        out, d = outs[i // 4], i % 4
        out[:rows, d * width : (d + 1) * width] = dot(hidden, vs[i]).astype(BF16)
        out[rows:, d * width : (d + 1) * width] = dot_nt(dadu, ws[i]).astype(BF16)


def dense_sum_kernel(mine, got, out_ref, g0, g1, g2, g3):
    rows = out_ref.shape[0]
    width = g0.shape[1]
    out_ref[...] = (mine[:rows, :].astype(F32) + got[:rows, :].astype(F32)).astype(BF16)
    for d, ref in enumerate((g0, g1, g2, g3)):
        at = slice(d * width, (d + 1) * width)
        ref[...] = (mine[rows:, at].astype(F32) + got[rows:, at].astype(F32)).astype(ref.dtype)


def back_kernel(*refs):
    pieces, wd, g_ref, xs, vs, sems = refs[:8], refs[8], *refs[10:]
    width = pieces[0].shape[1]
    load = Loads(sems)
    copies = [
        [load(pieces[i], xs.at[i]), load(wd.at[:, pl.ds(at, width)], vs.at[i])]
        for i, at in enumerate(starts(width))
    ]
    for i in range(8):
        wait(copies[i])
        term = dot_nt(xs[i], vs[i])
        if i == 0:
            g_ref[...] = term
        else:
            g_ref[...] += term


def half_kernel(side, x, wg, wu, ab, xs, ws, sems):
    width = xs.shape[2]
    units = wg.shape[1]
    load = Loads(sems)
    at = starts(width)[4 * side :]
    copies = [
        [
            load(x.at[:, pl.ds(d * width, width)], xs.at[d]),
            load(wg.at[pl.ds(at[d], width), :], ws.at[d, :, pl.ds(0, units)]),
            load(wu.at[pl.ds(at[d], width), :], ws.at[d, :, pl.ds(units, units)]),
        ]
        for d in range(4)
    ]
    for d in range(4):
        wait(copies[d])
        term = dot(xs[d], ws[d])
        if d == 0 and side == 0:
            ab[...] = term
        else:
            ab[...] += term


def forth_kernel(x, part, g_ref, wg, wu, wd, a1, a2, a3, oo, hid_ref, dadu_ref, ab, xs, ws, vs, gs, sems):
    width = xs.shape[2]
    units = wg.shape[1]
    load = Loads(sems)
    at = starts(width)
    first = load(part, ab)
    more = [load(wd.at[:, pl.ds(at[4 + d], width)], vs.at[d]) for d in range(4)]
    copy_g = load(g_ref, gs)
    first.wait()
    half_kernel(1, x, wg, wu, ab, xs, ws, sems.at[pl.ds(6, 12)])
    act, hidden, slope = gate_terms(ab[:, :units], ab[:, units:])
    copy_g.wait()
    g = gs[...]
    hid_ref[...] = hidden
    dadu_ref[:, :units] = (g * slope).astype(BF16)
    dadu_ref[:, units:] = (g * act).astype(BF16)
    for d in range(4):
        more[d].wait()
        oo[:, d * width : (d + 1) * width] = dot(hidden, vs[d]).astype(BF16)


def cross_kernel(hid_ref, dadu_ref, wg, wu, wd, om, ro, ws, vs, sems):
    width = ws.shape[1]
    units = wg.shape[1]
    load = Loads(sems)
    at = starts(width)
    copies = [
        [
            load(wg.at[pl.ds(at[4 + d], width), :], ws.at[d, :, pl.ds(0, units)]),
            load(wu.at[pl.ds(at[4 + d], width), :], ws.at[d, :, pl.ds(units, units)]),
        ]
        for d in range(4)
    ]
    more = [load(wd.at[:, pl.ds(at[d], width)], vs.at[d]) for d in range(4)]
    for d in range(4):
        wait(copies[d])
        ro[:, d * width : (d + 1) * width] = dot_nt(dadu_ref[...], ws[d]).astype(BF16)
    for d in range(4):
        more[d].wait()
        om[:, d * width : (d + 1) * width] = dot(hid_ref[...], vs[d]).astype(BF16)


def down_kernel(dadu_ref, wg, wu, got, *refs):
    outs, (ws, gs, sems) = refs[:SIDES], refs[SIDES:]
    width = ws.shape[1]
    units = wg.shape[1]
    load = Loads(sems)
    at = starts(width)
    copies = [
        [
            load(wg.at[pl.ds(at[d], width), :], ws.at[d, :, pl.ds(0, units)]),
            load(wu.at[pl.ds(at[d], width), :], ws.at[d, :, pl.ds(units, units)]),
            load(got.at[:, pl.ds(d * width, width)], gs.at[d]),
        ]
        for d in range(SIDES)
    ]
    for d in range(SIDES):
        wait(copies[d])
        outs[d][...] = (dot_nt(dadu_ref[...], ws[d]) + gs[d].astype(F32)).astype(BF16)


def add_kernel(mine, got, out):
    out[...] = (mine[...].astype(F32) + got[...].astype(F32)).astype(BF16)


def sum_kernel(p0, p1, p2, p3, after, out):
    out[...] = (
        p0[...].astype(F32)
        + p1[...].astype(F32)
        + p2[...].astype(F32)
        + p3[...].astype(F32)
    ).astype(BF16)


def mix_kernel(back, pick, gates, dense, pack, m0, m1, m2, m3, inner_ref):
    rows = gates.shape[0]
    width = pack.shape[2]
    inner = [None, None]
    for d, out in enumerate((m0, m1, m2, m3)):
        cotan = pack[d, rows:, :].astype(F32)
        y = dot(pick[...], back[:, d * width : (d + 1) * width])
        total = dense[:, d * width : (d + 1) * width].astype(F32)
        for k in range(2):
            yk = y[k * rows : (k + 1) * rows, :]
            total = total + gates[:, k : k + 1] * yk
            term = jnp.sum(cotan * yk, axis=1, keepdims=True)
            inner[k] = term if inner[k] is None else inner[k] + term
        out[...] = total.astype(BF16)
    lane = lax.broadcasted_iota(jnp.int32, (rows, 128), 1)
    inner_ref[...] = jnp.where(lane == 0, inner[0], jnp.where(lane == 1, inner[1], 0.0))


def grad_kernel(back, pick, d0, d1, d2, d3, out):
    rows = out.shape[0]
    z = dot(pick[:rows, :] + pick[rows:, :], back[...])
    dense = d0[...].astype(F32) + d1[...].astype(F32)
    dense = dense + d2[...].astype(F32) + d3[...].astype(F32)
    out[...] = (dense + z).astype(BF16)


def call(kernel, outs, limit, flops, args, name, far_args=(), scratch=()):
    vmem = pl.BlockSpec(memory_space=pltpu.VMEM)
    far = pl.BlockSpec(memory_space=pl.ANY)
    moved = sum(a.size * a.dtype.itemsize for a in args)
    return pl.pallas_call(
        kernel,
        out_shape=[jax.ShapeDtypeStruct(*o) for o in outs],
        in_specs=[far if i in far_args else vmem for i in range(len(args))],
        out_specs=[vmem] * len(outs),
        compiler_params=pltpu.CompilerParams(vmem_limit_bytes=limit * MIB),
        cost_estimate=pl.CostEstimate(flops=flops, bytes_accessed=moved, transcendentals=0),
        scratch_shapes=list(scratch),
        name=name,
    )(*args)


def local(
    tokens,
    cotangent,
    gates,
    routes,
    dense_gate,
    dense_up,
    dense_down,
    expert_gate,
    expert_up,
    expert_down,
):
    devices = lax.axis_size("tensor")
    rows, width = tokens.shape
    experts = lax.axis_size("dp")
    slots = experts * CAPACITY
    half = SIDES * width
    hidden = expert_gate.shape[2]
    dense_hidden = dense_gate.shape[1]

    def along(v, d):
        return lax.ppermute(
            v, "tensor", [(i, (i + 2 * d) % devices) for i in range(devices)]
        )

    def swap(v):
        return lax.ppermute(v, "tensor", [(i, i ^ 1) for i in range(devices)])

    def spread(v):
        return lax.all_to_all(v, "dp", split_axis=0, concat_axis=0, tiled=True)

    def pin(v):
        return pltpu.with_memory_space_constraint(v, pltpu.HBM)

    wg, wu, wd = pin(expert_gate[0]), pin(expert_up[0]), pin(expert_down[0])
    both = jnp.concatenate([tokens, cotangent], axis=0)
    own = [both] + [along(both, d) for d in (1, 2, 3)]
    sems = pltpu.SemaphoreType.DMA
    pick, grads_send = call(
        plan_kernel,
        [((2 * rows, slots), BF16), ((slots, width), BF16)],
        12,
        2 * 2 * rows * slots * width,
        (routes, gates, cotangent),
        "plan",
    )
    got_grads, own = lax.optimization_barrier((spread(grads_send), own))
    rows_send, pack = call(
        rows_kernel,
        [((slots, half), BF16), ((SIDES, 2 * rows, width), BF16)],
        12,
        2 * rows * slots * half,
        (pick, *own, got_grads),
        "rows",
        far_args=(5,),
    )
    got_rows = spread(rows_send)
    grads_own = [got_grads] + [along(got_grads, d) for d in (1, 2, 3)]
    grads_other = [swap(got_grads)]
    dense_m, dense_o = call(
        dense_kernel,
        [((2 * rows, half), BF16)] * 2,
        24,
        12 * rows * dense_hidden * half * 2,
        (pack, swap(pack), pin(dense_gate), pin(dense_up), pin(dense_down)),
        "dense",
        far_args=range(5),
        scratch=[
            pltpu.VMEM((8, 2 * rows, width), BF16),
            pltpu.VMEM((8, width, 2 * dense_hidden), BF16),
            pltpu.VMEM((8, dense_hidden, width), BF16),
            sems((32,)),
        ],
    )
    grads_own[1:], dense_m = lax.optimization_barrier((grads_own[1:], dense_m))
    grads_other += [swap(v) for v in grads_own[1:]]
    dense_out, *dense_part = call(
        dense_sum_kernel,
        [((rows, half), BF16)] + [((rows, width), BF16)] * SIDES,
        12,
        2 * rows * half,
        (dense_m, swap(dense_o)),
        "dense_sum",
    )
    dense_got = [dense_part[0]] + [along(dense_part[d], SIDES - d) for d in (1, 2, 3)]
    (g,) = call(
        back_kernel,
        [((slots, hidden), F32)],
        16,
        2 * slots * hidden * half * 2,
        (*grads_own, *grads_other, wd, dense_part[0]),
        "back",
        far_args=range(10),
        scratch=[
            pltpu.VMEM((8, slots, width), BF16),
            pltpu.VMEM((8, hidden, width), BF16),
            sems((16,)),
        ],
    )
    got_rows, g, dense_m = lax.optimization_barrier((got_rows, g, dense_m))
    rows_other = swap(got_rows)
    half_scratch = [pltpu.VMEM((4, slots, width), BF16), pltpu.VMEM((4, width, 2 * hidden), BF16)]
    (part,) = call(
        functools.partial(half_kernel, 0),
        [((slots, 2 * hidden), F32)],
        16,
        4 * slots * hidden * half,
        (got_rows, wg, wu),
        "half",
        far_args=(0, 1, 2),
        scratch=[*half_scratch, sems((12,))],
    )
    out_o, hid, dadu = call(
        forth_kernel,
        [((slots, half), BF16), ((slots, hidden), BF16), ((slots, 2 * hidden), BF16)],
        24,
        6 * slots * hidden * half,
        (rows_other, part, g, wg, wu, wd, *dense_got[1:]),
        "forth",
        far_args=range(9),
        scratch=[
            pltpu.VMEM((slots, 2 * hidden), F32),
            *half_scratch,
            pltpu.VMEM((4, hidden, width), BF16),
            pltpu.VMEM((slots, hidden), F32),
            sems((18,)),
        ],
    )
    out_got = swap(out_o)
    out_m, grad_o = call(
        cross_kernel,
        [((slots, half), BF16)] * 2,
        20,
        6 * slots * hidden * half,
        (hid, dadu, wg, wu, wd),
        "cross",
        far_args=range(2, 5),
        scratch=[half_scratch[1], pltpu.VMEM((4, hidden, width), BF16), sems((12,))],
    )
    grad_got = swap(grad_o)
    (out_chip,) = call(
        add_kernel,
        [((slots, half), BF16)],
        12,
        slots * half,
        (out_m, out_got),
        "add",
    )
    out_back = spread(out_chip)
    grad_part = call(
        down_kernel,
        [((slots, width), BF16)] * SIDES,
        20,
        4 * slots * hidden * half,
        (dadu, wg, wu, grad_got),
        "down",
        far_args=(1, 2, 3),
        scratch=[half_scratch[1], pltpu.VMEM((SIDES, slots, width), BF16), sems((12,))],
    )
    grad_all = [grad_part[0]] + [along(grad_part[d], SIDES - d) for d in (1, 2, 3)]
    m0, m1, m2, m3, inner = call(
        mix_kernel,
        [((rows, width), BF16)] * 4 + [((rows, 128), F32)],
        16,
        4 * rows * slots * half,
        (out_back, pick, gates, dense_out, pack),
        "mix",
    )
    (grad_sum,) = call(
        sum_kernel,
        [((slots, width), BF16)],
        12,
        3 * slots * width,
        (*grad_all, inner),
        "sum",
        far_args=(4,),
    )
    grad_back = spread(grad_sum)
    mixed = m0.astype(F32)
    for d, part in ((1, m1), (2, m2), (3, m3)):
        mixed = mixed + along(part, SIDES - d).astype(F32)
    inner = inner[:, :2]
    inner = inner + swap(inner)
    gate_grad = inner + along(inner, 1) + along(inner, 2) + along(inner, 3)
    (token_grad,) = call(
        grad_kernel,
        [((rows, width), BF16)],
        12,
        2 * rows * slots * width,
        (grad_back, pick, *dense_got),
        "grad",
    )
    return (mixed.astype(BF16), token_grad, gate_grad)


def solution(mesh):
    in_specs = (
        P("dp", "tensor"),
        P("dp", "tensor"),
        P("dp", None),
        P("dp", None),
        P(None, "tensor"),
        P(None, "tensor"),
        P("tensor", None),
        P("dp", None, "tensor"),
        P("dp", None, "tensor"),
        P("dp", "tensor", None),
    )
    out_specs = (P("dp", "tensor"), P("dp", "tensor"), P("dp", None))
    return jax.shard_map(local, mesh=mesh, in_specs=in_specs, out_specs=out_specs, check_vma=False)
```

time: 202 us -> 174 us (0.86)
  local copies, waits for them, and re-layouts: 34.9 us -> 11.8 us
  Pallas kernels: 39.2 us -> 47.4 us
  waiting for transfers between devices: 66.6 us -> 59.6 us
  starting transfers between devices: 57.5 us -> 50.6 us
    unnamed x102 -> x56, local copies, waits for them, and re-layouts: 34 us -> 10.9 us
    pallas_call x14 -> x13, Pallas kernels: 39.2 us -> 47.4 us  [call(): pl.pallas_call(kernel, out_shape=[jax.ShapeDtypeStruct(*o) for o in outs]...]
    ppermute x18, waiting for transfers between devices: 45 us -> 37.8 us  [along(): lax.ppermute(v, 'tensor', [(i, (i + 2 * d) % devices) for i in range(devi...]
    ppermute x18, starting transfers between devices: 25 us -> 18.5 us  [along(): lax.ppermute(v, 'tensor', [(i, (i + 2 * d) % devices) for i in range(devi...]
    all_to_all x4, waiting for transfers between devices: 16.8 us -> 20.6 us  [spread(): return lax.all_to_all(v, 'dp', split_axis=0, concat_axis=0, tiled=True)]
    ppermute x13 -> x10, waiting for transfers between devices: 4.8 us -> 1.17 us  [swap(): return lax.ppermute(v, 'tensor', [(i, i ^ 1) for i in range(devices)])]
  transfers between devices with their start and end apart: 35 -> 32, of which waited for: 16 -> 15; matrix products, arithmetic and copies ran while one was open for 2% -> 3% of each run, Pallas kernels for 13% -> 21%
where the time goes in v2:
time: 174 us; the launch traced here: 173 us
  waiting for transfers between devices  59.6 us (34%)
  starting transfers between devices  50.6 us (29%)
  Pallas kernels  47.4 us (27%)
  local copies, waits for them, and re-layouts  11.8 us (7%)
  other arithmetic  2.49 us (1%)
    pallas_call x13, Pallas kernels, call(): pl.pallas_call(kernel, out_shape=[jax.ShapeDtypeStruct(*o) for o in outs]...  47.4 us
    ppermute x18, waiting for transfers between devices, along(): lax.ppermute(v, 'tensor', [(i, (i + 2 * d) % devices) for i in range(devi...  37.8 us
    all_to_all x4, starting transfers between devices, spread(): return lax.all_to_all(v, 'dp', split_axis=0, concat_axis=0, tiled=True)  30 us
    all_to_all x4, waiting for transfers between devices, spread(): return lax.all_to_all(v, 'dp', split_axis=0, concat_axis=0, tiled=True)  20.6 us
    ppermute x18, starting transfers between devices, along(): lax.ppermute(v, 'tensor', [(i, (i + 2 * d) % devices) for i in range(devi...  18.5 us
    unnamed x56, local copies, waits for them, and re-layouts  10.9 us
  transfers between devices with their start and end apart: 32, of which 15 were waited for; matrix products, arithmetic and copies ran while one was open for 3% of the time, Pallas kernels for 21%

profile of v2, /device:TPU:2, one launch (start us, length us, event | category | flops | bytes accessed | tf_op | source)
XLA Modules:
  0.0 172.8 jit_solution(1458868554025776999)
XLA Ops:
  0.6 0.8 copy.14.gates_ref.gates
  1.4 0.8 copy.13.routes_ref
  2.2 0.9 copy-done.18
  3.1 1.8 %plan.1 = (bf16[256,512]{1,0:T(8,128)(2,1)S(1)}, bf16[512,512]{1,0:T(8,128)(2,1)}) custom-call(s32[128,2]{1,0:T(8,128)S(1)} %copy.13.routes_ref, f32[128,2]{1,0:T(8,128)S(1)} %copy.14.gates_ref.gates, bf16[128,512]{1,0:T(8,128)(2,1)S(1)} %copy-done.18), custom_call_target="tpu_custom_call" | custom-call | flops 134217728 | bytes 133120 | tf_op jit(solution)/shard_map/plan/pallas_call | solution.py:277
  4.9 8.3 %all-to-all-start = ((bf16[16,32,512]{2,1,0:T(8,128)(2,1)}), bf16[16,32,512]{2,1,0:T(8,128)(2,1)S(1)}, u32[]{:S(2)}, u32[]{:S(2)}) async-start(bf16[16,32,512]{2,1,0:T(8,128)(2,1)} %bitcast), calls=%async_computation | async-start | bytes 1048576 | tf_op jit(solution)/shard_map/all_to_all | solution.py:318
  13.2 0.9 constant_dynamic-update-slice_fusion.1
  14.1 0.9 constant_dynamic-update-slice_fusion.p0
  15.1 3.1 %collective-permute-start.2 = (bf16[256,512]{1,0:T(8,128)(2,1)S(1)}, bf16[256,512]{1,0:T(8,128)(2,1)S(1)}, u32[]{:S(2)}, u32[]{:S(2)}) collective-permute-start(bf16[256,512]{1,0:T(8,128)(2,1)S(1)} %constant_dynamic-update-slice_fusion.p0), channel_id=1, source_target_pairs={{0,6},{1,7},{2,0},{3,1},{4,2},{5,3},{6,4},{7,5},{8,14},{9,15},{10,... | collective-permute-start | bytes 786440 | tf_op jit(solution)/shard_map/ppermute | solution.py:310
  18.1 0.6 collective-permute-start.1
  18.8 1.0 collective-permute-start
  19.7 9.0 %collective-permute-done.2.p3 = bf16[256,512]{1,0:T(8,128)(2,1)S(1)} collective-permute-done((bf16[256,512]{1,0:T(8,128)(2,1)S(1)}, bf16[256,512]{1,0:T(8,128)(2,1)S(1)}, u32[]{:S(2)}, u32[]{:S(2)}) %collective-permute-start.2) | collective-permute-done | bytes 262176 | tf_op jit(solution)/shard_map/ppermute | solution.py:310
  28.9 3.6 %collective-permute-done.p1 = bf16[256,512]{1,0:T(8,128)(2,1)S(1)} collective-permute-done((bf16[256,512]{1,0:T(8,128)(2,1)S(1)}, bf16[256,512]{1,0:T(8,128)(2,1)S(1)}, u32[]{:S(2)}, u32[]{:S(2)}) %collective-permute-start) | collective-permute-done | bytes 262176 | tf_op jit(solution)/shard_map/ppermute | solution.py:310
  32.5 1.7 %rows.1 = (bf16[512,2048]{1,0:T(8,128)(2,1)S(1)}, bf16[4,256,512]{2,1,0:T(8,128)(2,1)}) custom-call(bf16[256,512]{1,0:T(8,128)(2,1)S(1)} %get-tuple-element.39.pick_ref.pick, bf16[256,512]{1,0:T(8,128)(2,1)S(1)} %constant_dynamic-update-slice_fusion.p0, bf16[256,512]{1,0:T(8,128)(2,1)S(1)} %collective-permute-done.p1, ...), custom_call_target="tpu_custom_call" | custom-call | flops 268435456 | bytes 1835008 | tf_op jit(solution)/shard_map/rows/pallas_call | solution.py:277
  34.2 1.3 copy-done.4
  35.6 7.2 %all-to-all-start.1 = ((bf16[16,32,2048]{2,1,0:T(8,128)(2,1)}), bf16[16,32,2048]{2,1,0:T(8,128)(2,1)S(1)}, u32[]{:S(2)}, u32[]{:S(2)}) async-start(bf16[16,32,2048]{2,1,0:T(8,128)(2,1)} %bitcast.21), calls=%async_computation.1 | async-start | bytes 4194304 | tf_op jit(solution)/shard_map/all_to_all | solution.py:318
  42.8 0.6 collective-permute-start.5
  43.4 0.6 collective-permute-start.4
  44.0 0.8 collective-permute-start.3
  44.9 9.4 %dense.1 = (bf16[256,2048]{1,0:T(8,128)(2,1)S(1)}, bf16[256,2048]{1,0:T(8,128)(2,1)S(1)}) custom-call(bf16[4,256,512]{2,1,0:T(8,128)(2,1)} %get-tuple-element.47.refs_0_.pack, bf16[4,256,512]{2,1,0:T(8,128)(2,1)} %collective-permute-done.6.refs_1_, bf16[4096,512]{1,0:T(8,128)(2,1)} %refs_2_.1, bf16[4096,512]{1,0:T(8,128)(2,1)} %refs_3_.1, ...), custom_call_target="tpu_custom_call" | custom-call | flops 3221225472 | bytes 14680064 | tf_op jit(solution)/shard_map/dense/pallas_call | solution.py:277
  54.3 0.5 collective-permute-start.7
  54.8 2.8 %collective-permute-done.5.refs_3_ = bf16[512,512]{1,0:T(8,128)(2,1)S(1)} collective-permute-done((bf16[512,512]{1,0:T(8,128)(2,1)S(1)}, bf16[512,512]{1,0:T(8,128)(2,1)S(1)}, u32[]{:S(2)}, u32[]{:S(2)}) %collective-permute-start.5) | collective-permute-done | bytes 524320 | tf_op jit(solution)/shard_map/ppermute | solution.py:310
  57.6 2.2 %collective-permute-done.4.refs_2_ = bf16[512,512]{1,0:T(8,128)(2,1)S(1)} collective-permute-done((bf16[512,512]{1,0:T(8,128)(2,1)S(1)}, bf16[512,512]{1,0:T(8,128)(2,1)S(1)}, u32[]{:S(2)}, u32[]{:S(2)}) %collective-permute-start.4) | collective-permute-done | bytes 524320 | tf_op jit(solution)/shard_map/ppermute | solution.py:310
  59.8 9.9 %collective-permute-done.3.refs_1_ = bf16[512,512]{1,0:T(8,128)(2,1)S(1)} collective-permute-done((bf16[512,512]{1,0:T(8,128)(2,1)S(1)}, bf16[512,512]{1,0:T(8,128)(2,1)S(1)}, u32[]{:S(2)}, u32[]{:S(2)}) %collective-permute-start.3) | collective-permute-done | bytes 524320 | tf_op jit(solution)/shard_map/ppermute | solution.py:310
  69.6 0.5 collective-permute-start.9
  70.4 0.8 copy-done.11
  71.2 0.7 copy-done.25
  71.9 0.4 collective-permute-done.9.refs_6_
  72.3 0.7 collective-permute-done.10.refs_7_
  73.0 4.0 %back.1.g_ref = f32[512,384]{1,0:T(8,128)S(1)} custom-call(bf16[512,512]{1,0:T(8,128)(2,1)S(1)} %bitcast.20, bf16[512,512]{1,0:T(8,128)(2,1)S(1)} %collective-permute-done.3.refs_1_, bf16[512,512]{1,0:T(8,128)(2,1)S(1)} %collective-permute-done.4.refs_2_, bf16[512,512]{1,0:T(8,128)(2,1)S(1)} %collective-permute-done.5.refs_3_, ...), custom_call_target="tpu_custom_call" | custom-call | flops 1610612736 | bytes 7471104 | tf_op jit(solution)/shard_map/back/pallas_call | solution.py:277
  77.3 0.9 collective-permute-start.13
  78.2 0.4 collective-permute-start.14
  78.6 0.8 collective-permute-start.15
  79.4 4.1 %half.1.part = f32[512,768]{1,0:T(8,128)S(1)} custom-call(bf16[512,2048]{1,0:T(8,128)(2,1)S(1)} %bitcast.13, bf16[4096,384]{1,0:T(8,128)(2,1)} %bitcast.23, bf16[4096,384]{1,0:T(8,128)(2,1)} %bitcast.27), custom_call_target="tpu_custom_call" | custom-call | flops 1610612736 | bytes 8388608 | tf_op jit(solution)/shard_map/half/pallas_call | solution.py:277
  83.9 2.4 %collective-permute-done.14.a2.d2 = bf16[128,512]{1,0:T(8,128)(2,1)S(1)} collective-permute-done((bf16[128,512]{1,0:T(8,128)(2,1)}, bf16[128,512]{1,0:T(8,128)(2,1)S(1)}, u32[]{:S(2)}, u32[]{:S(2)}) %collective-permute-start.14) | collective-permute-done | bytes 131104 | tf_op jit(solution)/shard_map/ppermute | solution.py:310
  86.3 1.9 %collective-permute-done.15.a3.d3 = bf16[128,512]{1,0:T(8,128)(2,1)S(1)} collective-permute-done((bf16[128,512]{1,0:T(8,128)(2,1)}, bf16[128,512]{1,0:T(8,128)(2,1)S(1)}, u32[]{:S(2)}, u32[]{:S(2)}) %collective-permute-start.15) | collective-permute-done | bytes 131104 | tf_op jit(solution)/shard_map/ppermute | solution.py:310
  88.2 6.8 %forth.1 = (bf16[512,2048]{1,0:T(8,128)(2,1)S(1)}, bf16[512,384]{1,0:T(8,128)(2,1)S(1)}, bf16[512,768]{1,0:T(8,128)(2,1)S(1)}) custom-call(bf16[512,2048]{1,0:T(8,128)(2,1)S(1)} %collective-permute-done.12.x, f32[512,768]{1,0:T(8,128)S(1)} %half.1.part, f32[512,384]{1,0:T(8,128)S(1)} %back.1.g_ref, bf16[4096,384]{1,0:T(8,128)(2,1)} %bitcast.24, ...), custom_call_target="tpu_custom_call" | custom-call | flops 2415919104 | bytes 14286848 | tf_op jit(solution)/shard_map/forth/pallas_call | solution.py:277
  95.2 6.5 %cross.1 = (bf16[512,2048]{1,0:T(8,128)(2,1)S(1)}, bf16[512,2048]{1,0:T(8,128)(2,1)}) custom-call(bf16[512,384]{1,0:T(8,128)(2,1)S(1)} %get-tuple-element.60.hid_ref, bf16[512,768]{1,0:T(8,128)(2,1)S(1)} %get-tuple-element.61.dadu_ref, bf16[4096,384]{1,0:T(8,128)(2,1)} %bitcast.25, bf16[4096,384]{1,0:T(8,128)(2,1)} %bitcast.29, bf16[384,4096]{1,0:T(8,128)(2,1)} %bitcast.33), custom_call_target="tpu_custom_call" | custom-call | flops 2415919104 | bytes 10616832 | tf_op jit(solution)/shard_map/cross/pallas_call | solution.py:277
  101.7 0.6 collective-permute-start.20
  102.3 1.8 %add.36 = bf16[512,2048]{1,0:T(8,128)(2,1)} custom-call(bf16[512,2048]{1,0:T(8,128)(2,1)S(1)} %get-tuple-element.62.mine, bf16[512,2048]{1,0:T(8,128)(2,1)S(1)} %collective-permute-done.16.got), custom_call_target="tpu_custom_call" | custom-call | flops 1048576 | bytes 4194304 | tf_op jit(solution)/shard_map/add/pallas_call | solution.py:277
  104.2 7.4 %all-to-all-start.2 = ((bf16[16,32,2048]{2,1,0:T(8,128)(2,1)}), bf16[16,32,2048]{2,1,0:T(8,128)(2,1)S(1)}, u32[]{:S(2)}, u32[]{:S(2)}) async-start(bf16[16,32,2048]{2,1,0:T(8,128)(2,1)} %bitcast.7), calls=%async_computation.2 | async-start | bytes 4194304 | tf_op jit(solution)/shard_map/all_to_all | solution.py:318
  111.5 4.8 %down.1 = (bf16[512,512]{1,0:T(8,128)(2,1)S(1)}, bf16[512,512]{1,0:T(8,128)(2,1)}, bf16[512,512]{1,0:T(8,128)(2,1)}, bf16[512,512]{1,0:T(8,128)(2,1)}) custom-call(bf16[512,768]{1,0:T(8,128)(2,1)S(1)} %copy-done.1, bf16[4096,384]{1,0:T(8,128)(2,1)} %bitcast.26, bf16[4096,384]{1,0:T(8,128)(2,1)} %bitcast.30, bf16[512,2048]{1,0:T(8,128)(2,1)} %collective-permute-done.20.got), custom_call_target="tpu_custom_call" | custom-call | flops 1610612736 | bytes 9175040 | tf_op jit(solution)/shard_map/down/pallas_call | solution.py:277
  116.3 0.8 copy-done.13
  117.1 0.6 collective-permute-start.21
  118.1 1.1 collective-permute-start.23
  119.1 20.6 %all-to-all-done.2 = bf16[16,32,2048]{2,1,0:T(8,128)(2,1)S(1)} async-done(((bf16[16,32,2048]{2,1,0:T(8,128)(2,1)}), bf16[16,32,2048]{2,1,0:T(8,128)(2,1)S(1)}, u32[]{:S(2)}, u32[]{:S(2)}) %all-to-all-start.2) | async-done | bytes 2097184 | tf_op jit(solution)/shard_map/all_to_all | solution.py:318
  139.8 1.0 copy-done.12
  140.8 0.8 copy-done.16
  141.7 2.8 %mix.1 = (bf16[128,512]{1,0:T(8,128)(2,1)S(1)}, bf16[128,512]{1,0:T(8,128)(2,1)S(1)}, bf16[128,512]{1,0:T(8,128)(2,1)S(1)}, bf16[128,512]{1,0:T(8,128)(2,1)S(1)}, f32[128,128]{1,0:T(8,128)}) custom-call(bf16[512,2048]{1,0:T(8,128)(2,1)S(1)} %bitcast.14, bf16[256,512]{1,0:T(8,128)(2,1)S(1)} %copy-done.3, f32[128,2]{1,0:T(8,128)S(1)} %copy-done.16, ...), custom_call_target="tpu_custom_call" | custom-call | flops 536870912 | bytes 3933184 | tf_op jit(solution)/shard_map/mix/pallas_call | solution.py:277
  144.5 0.7 copy-done.19
  145.1 0.7 copy-done.21
  145.9 2.4 %sum.1 = bf16[512,512]{1,0:T(8,128)(2,1)} custom-call(bf16[512,512]{1,0:T(8,128)(2,1)S(1)} %copy-done.14, bf16[512,512]{1,0:T(8,128)(2,1)S(1)} %collective-permute-done.21.p1, bf16[512,512]{1,0:T(8,128)(2,1)} %collective-permute-done.22.p2, bf16[512,512]{1,0:T(8,128)(2,1)} %collective-permute-done.23.p3, f32[128,128]{1,0:T(8,128)} %get-tuple-element.74.after), custom_call_target="tpu_custom_call" | custom-call | flops 786432 | bytes 2162688 | tf_op jit(solution)/shard_map/sum/pallas_call | solution.py:277
  148.3 7.1 %all-to-all-start.3 = ((bf16[16,32,512]{2,1,0:T(8,128)(2,1)}), bf16[16,32,512]{2,1,0:T(8,128)(2,1)S(1)}, u32[]{:S(2)}, u32[]{:S(2)}) async-start(bf16[16,32,512]{2,1,0:T(8,128)(2,1)} %bitcast.9), calls=%async_computation.3 | async-start | bytes 1048576 | tf_op jit(solution)/shard_map/all_to_all | solution.py:318
  155.4 0.8 slice_add_fusion
  156.3 0.7 collective-permute-start.27
  157.3 1.1 collective-permute-start.25
  158.4 2.7 %collective-permute-start.17 = (bf16[128,512]{1,0:T(8,128)(2,1)S(1)}, bf16[128,512]{1,0:T(8,128)(2,1)S(1)}, u32[]{:S(2)}, u32[]{:S(2)}) collective-permute-start(bf16[128,512]{1,0:T(8,128)(2,1)S(1)} %copy-done.22), channel_id=1, source_target_pairs={{0,6},{1,7},{2,0},{3,1},{4,2},{5,3},{6,4},{7,5},{8,14},{9,15},{10,... | collective-permute-start | bytes 393224 | tf_op jit(solution)/shard_map/ppermute | solution.py:310
  161.0 1.5 collective-permute-start.18
  162.6 1.3 collective-permute-start.19
  164.0 0.6 copy.16
  164.6 2.1 %collective-permute-done.17 = bf16[128,512]{1,0:T(8,128)(2,1)S(1)} collective-permute-done((bf16[128,512]{1,0:T(8,128)(2,1)S(1)}, bf16[128,512]{1,0:T(8,128)(2,1)S(1)}, u32[]{:S(2)}, u32[]{:S(2)}) %collective-permute-start.17) | collective-permute-done | bytes 131104 | tf_op jit(solution)/shard_map/ppermute | solution.py:310
  166.7 2.2 %collective-permute-done.18 = bf16[128,512]{1,0:T(8,128)(2,1)S(1)} collective-permute-done((bf16[128,512]{1,0:T(8,128)(2,1)S(1)}, bf16[128,512]{1,0:T(8,128)(2,1)S(1)}, u32[]{:S(2)}, u32[]{:S(2)}) %collective-permute-start.18) | collective-permute-done | bytes 131104 | tf_op jit(solution)/shard_map/ppermute | solution.py:310
  169.0 1.2 collective-permute-done.19
  170.2 1.6 add_convert_fusion
  171.9 0.9 grad.1
  (73 shorter events, 1.9 us)
Async XLA Ops:
  1.4 3.5 %copy-start.15 = (f32[128,2]{1,0:T(8,128)}, f32[128,2]{1,0:T(8,128)S(1)}, u32[]{:S(2)}) copy-start(f32[128,2]{1,0:T(8,128)S(1)} %copy.14.gates_ref.gates) | copy-start | bytes 3076
  2.2 0.9 copy-start.18
  4.9 30.7 %copy-start.2 = (bf16[256,512]{1,0:T(8,128)(2,1)}, bf16[256,512]{1,0:T(8,128)(2,1)S(1)}, u32[]{:S(2)}) copy-start(bf16[256,512]{1,0:T(8,128)(2,1)S(1)} %get-tuple-element.39.pick_ref.pick) | copy-start | bytes 786436
  4.9 27.6 %all-to-all-start = ((bf16[16,32,512]{2,1,0:T(8,128)(2,1)}), bf16[16,32,512]{2,1,0:T(8,128)(2,1)S(1)}, u32[]{:S(2)}, u32[]{:S(2)}) async-start(bf16[16,32,512]{2,1,0:T(8,128)(2,1)} %bitcast), calls=%async_computation | async-start | bytes 1048576 | tf_op jit(solution)/shard_map/all_to_all | solution.py:318
  15.1 13.7 %collective-permute-start.2 = (bf16[256,512]{1,0:T(8,128)(2,1)S(1)}, bf16[256,512]{1,0:T(8,128)(2,1)S(1)}, u32[]{:S(2)}, u32[]{:S(2)}) collective-permute-start(bf16[256,512]{1,0:T(8,128)(2,1)S(1)} %constant_dynamic-update-slice_fusion.p0), channel_id=1, source_target_pairs={{0,6},{1,7},{2,0},{3,1},{4,2},{5,3},{6,4},{7,5},{8,14},{9,15},{10,... | collective-permute-start | bytes 786440 | tf_op jit(solution)/shard_map/ppermute | solution.py:310
  18.1 10.8 %collective-permute-start.1 = (bf16[256,512]{1,0:T(8,128)(2,1)S(1)}, bf16[256,512]{1,0:T(8,128)(2,1)S(1)}, u32[]{:S(2)}, u32[]{:S(2)}) collective-permute-start(bf16[256,512]{1,0:T(8,128)(2,1)S(1)} %constant_dynamic-update-slice_fusion.p0), channel_id=1, source_target_pairs={{0,4},{1,5},{2,6},{3,7},{4,0},{5,1},{6,2},{7,3},{8,12},{9,13},{10,... | collective-permute-start | bytes 786440 | tf_op jit(solution)/shard_map/ppermute | solution.py:310
  18.8 13.7 %collective-permute-start = (bf16[256,512]{1,0:T(8,128)(2,1)S(1)}, bf16[256,512]{1,0:T(8,128)(2,1)S(1)}, u32[]{:S(2)}, u32[]{:S(2)}) collective-permute-start(bf16[256,512]{1,0:T(8,128)(2,1)S(1)} %constant_dynamic-update-slice_fusion.p0), channel_id=1, source_target_pairs={{0,2},{1,3},{2,4},{3,5},{4,6},{5,7},{6,0},{7,1},{8,10},{9,11},{10,... | collective-permute-start | bytes 786440 | tf_op jit(solution)/shard_map/ppermute | solution.py:310
  34.2 1.3 copy-start.4
  35.6 9.3 %collective-permute-start.6 = (bf16[4,256,512]{2,1,0:T(8,128)(2,1)}, bf16[4,256,512]{2,1,0:T(8,128)(2,1)}, u32[]{:S(2)}, u32[]{:S(2)}) collective-permute-start(bf16[4,256,512]{2,1,0:T(8,128)(2,1)} %get-tuple-element.47.refs_0_.pack), channel_id=1, source_target_pairs={{0,1},{1,0},{2,3},{3,2},{4,5},{5,4},{6,7},{7,6},{8,9},{9,8},{10,11... | collective-permute-start | bytes 3145736 | tf_op jit(solution)/shard_map/ppermute | solution.py:315
  35.6 41.5 %all-to-all-start.1 = ((bf16[16,32,2048]{2,1,0:T(8,128)(2,1)}), bf16[16,32,2048]{2,1,0:T(8,128)(2,1)S(1)}, u32[]{:S(2)}, u32[]{:S(2)}) async-start(bf16[16,32,2048]{2,1,0:T(8,128)(2,1)} %bitcast.21), calls=%async_computation.1 | async-start | bytes 4194304 | tf_op jit(solution)/shard_map/all_to_all | solution.py:318
  42.8 14.8 %collective-permute-start.5 = (bf16[512,512]{1,0:T(8,128)(2,1)S(1)}, bf16[512,512]{1,0:T(8,128)(2,1)S(1)}, u32[]{:S(2)}, u32[]{:S(2)}) collective-permute-start(bf16[512,512]{1,0:T(8,128)(2,1)S(1)} %bitcast.16), channel_id=1, source_target_pairs={{0,6},{1,7},{2,0},{3,1},{4,2},{5,3},{6,4},{7,5},{8,14},{9,15},{10,... | collective-permute-start | bytes 1572872 | tf_op jit(solution)/shard_map/ppermute | solution.py:310
  43.4 16.4 %collective-permute-start.4 = (bf16[512,512]{1,0:T(8,128)(2,1)S(1)}, bf16[512,512]{1,0:T(8,128)(2,1)S(1)}, u32[]{:S(2)}, u32[]{:S(2)}) collective-permute-start(bf16[512,512]{1,0:T(8,128)(2,1)S(1)} %bitcast.17), channel_id=1, source_target_pairs={{0,4},{1,5},{2,6},{3,7},{4,0},{5,1},{6,2},{7,3},{8,12},{9,13},{10,... | collective-permute-start | bytes 1572872 | tf_op jit(solution)/shard_map/ppermute | solution.py:310
  44.0 25.6 %collective-permute-start.3 = (bf16[512,512]{1,0:T(8,128)(2,1)S(1)}, bf16[512,512]{1,0:T(8,128)(2,1)S(1)}, u32[]{:S(2)}, u32[]{:S(2)}) collective-permute-start(bf16[512,512]{1,0:T(8,128)(2,1)S(1)} %bitcast.18), channel_id=1, source_target_pairs={{0,2},{1,3},{2,4},{3,5},{4,6},{5,7},{6,0},{7,1},{8,10},{9,11},{10,... | collective-permute-start | bytes 1572872 | tf_op jit(solution)/shard_map/ppermute | solution.py:310
  54.2 15.9 %collective-permute-start.11 = (bf16[256,2048]{1,0:T(8,128)(2,1)S(1)}, bf16[256,2048]{1,0:T(8,128)(2,1)S(1)}, u32[]{:S(2)}, u32[]{:S(2)}) collective-permute-start(bf16[256,2048]{1,0:T(8,128)(2,1)S(1)} %get-tuple-element.53), channel_id=1, source_target_pairs={{0,1},{1,0},{2,3},{3,2},{4,5},{5,4},{6,7},{7,6},{8,9},{9,8},{10,11... | collective-permute-start | bytes 3145736 | tf_op jit(solution)/shard_map/ppermute | solution.py:315
  54.3 17.6 %collective-permute-start.7 = (bf16[512,512]{1,0:T(8,128)(2,1)S(1)}, bf16[512,512]{1,0:T(8,128)(2,1)S(1)}, u32[]{:S(2)}, u32[]{:S(2)}) collective-permute-start(bf16[512,512]{1,0:T(8,128)(2,1)S(1)} %bitcast.19), channel_id=1, source_target_pairs={{0,1},{1,0},{2,3},{3,2},{4,5},{5,4},{6,7},{7,6},{8,9},{9,8},{10,11... | collective-permute-start | bytes 1572872 | tf_op jit(solution)/shard_map/ppermute | solution.py:315
  69.6 2.3 %collective-permute-start.8 = (bf16[512,512]{1,0:T(8,128)(2,1)S(1)}, bf16[512,512]{1,0:T(8,128)(2,1)S(1)}, u32[]{:S(2)}, u32[]{:S(2)}) collective-permute-start(bf16[512,512]{1,0:T(8,128)(2,1)S(1)} %collective-permute-done.3.refs_1_), channel_id=1, source_target_pairs={{0,1},{1,0},{2,3},{3,2},{4,5},{5,4},{6,7},{7,6},{8,9},{9,8},{10,11... | collective-permute-start | bytes 1572872 | tf_op jit(solution)/shard_map/ppermute | solution.py:315
  69.6 2.6 %collective-permute-start.9 = (bf16[512,512]{1,0:T(8,128)(2,1)S(1)}, bf16[512,512]{1,0:T(8,128)(2,1)S(1)}, u32[]{:S(2)}, u32[]{:S(2)}) collective-permute-start(bf16[512,512]{1,0:T(8,128)(2,1)S(1)} %collective-permute-done.4.refs_2_), channel_id=1, source_target_pairs={{0,1},{1,0},{2,3},{3,2},{4,5},{5,4},{6,7},{7,6},{8,9},{9,8},{10,11... | collective-permute-start | bytes 1572872 | tf_op jit(solution)/shard_map/ppermute | solution.py:315
  70.1 2.9 %collective-permute-start.10 = (bf16[512,512]{1,0:T(8,128)(2,1)S(1)}, bf16[512,512]{1,0:T(8,128)(2,1)S(1)}, u32[]{:S(2)}, u32[]{:S(2)}) collective-permute-start(bf16[512,512]{1,0:T(8,128)(2,1)S(1)} %collective-permute-done.5.refs_3_), channel_id=1, source_target_pairs={{0,1},{1,0},{2,3},{3,2},{4,5},{5,4},{6,7},{7,6},{8,9},{9,8},{10,11... | collective-permute-start | bytes 1572872 | tf_op jit(solution)/shard_map/ppermute | solution.py:315
  70.4 0.8 copy-start.11
  71.2 0.7 copy-start.25
  71.9 1.2 copy-start.23
  71.9 1.2 copy-start.24
  77.1 11.1 %collective-permute-start.12 = (bf16[512,2048]{1,0:T(8,128)(2,1)S(1)}, bf16[512,2048]{1,0:T(8,128)(2,1)S(1)}, u32[]{:S(2)}, u32[]{:S(2)}) collective-permute-start(bf16[512,2048]{1,0:T(8,128)(2,1)S(1)} %bitcast.12), channel_id=1, source_target_pairs={{0,1},{1,0},{2,3},{3,2},{4,5},{5,4},{6,7},{7,6},{8,9},{9,8},{10,11... | collective-permute-start | bytes 6291464 | tf_op jit(solution)/shard_map/ppermute | solution.py:315
  77.3 6.5 %collective-permute-start.13 = (bf16[128,512]{1,0:T(8,128)(2,1)}, bf16[128,512]{1,0:T(8,128)(2,1)S(1)}, u32[]{:S(2)}, u32[]{:S(2)}) collective-permute-start(bf16[128,512]{1,0:T(8,128)(2,1)} %copy-done.25), channel_id=1, source_target_pairs={{0,6},{1,7},{2,0},{3,1},{4,2},{5,3},{6,4},{7,5},{8,14},{9,15},{10,... | collective-permute-start | bytes 393224 | tf_op jit(solution)/shard_map/ppermute | solution.py:310
  78.2 8.1 %collective-permute-start.14 = (bf16[128,512]{1,0:T(8,128)(2,1)}, bf16[128,512]{1,0:T(8,128)(2,1)S(1)}, u32[]{:S(2)}, u32[]{:S(2)}) collective-permute-start(bf16[128,512]{1,0:T(8,128)(2,1)} %copy-done.24), channel_id=1, source_target_pairs={{0,4},{1,5},{2,6},{3,7},{4,0},{5,1},{6,2},{7,3},{8,12},{9,13},{10,... | collective-permute-start | bytes 393224 | tf_op jit(solution)/shard_map/ppermute | solution.py:310
  78.6 9.6 %collective-permute-start.15 = (bf16[128,512]{1,0:T(8,128)(2,1)}, bf16[128,512]{1,0:T(8,128)(2,1)S(1)}, u32[]{:S(2)}, u32[]{:S(2)}) collective-permute-start(bf16[128,512]{1,0:T(8,128)(2,1)} %copy-done.23), channel_id=1, source_target_pairs={{0,2},{1,3},{2,4},{3,5},{4,6},{5,7},{6,0},{7,1},{8,10},{9,11},{10,... | collective-permute-start | bytes 393224 | tf_op jit(solution)/shard_map/ppermute | solution.py:310
  83.9 11.2 %copy-start.5 = (bf16[128,512]{1,0:T(8,128)(2,1)}, bf16[128,512]{1,0:T(8,128)(2,1)S(1)}, u32[]{:S(2)}) copy-start(bf16[128,512]{1,0:T(8,128)(2,1)S(1)} %collective-permute-done.13.a1.d1) | copy-start | bytes 393220
  86.3 8.8 %copy-start.7 = (bf16[128,512]{1,0:T(8,128)(2,1)}, bf16[128,512]{1,0:T(8,128)(2,1)S(1)}, u32[]{:S(2)}) copy-start(bf16[128,512]{1,0:T(8,128)(2,1)S(1)} %collective-permute-done.14.a2.d2) | copy-start | bytes 393220
  88.2 6.9 %copy-start.9 = (bf16[128,512]{1,0:T(8,128)(2,1)}, bf16[128,512]{1,0:T(8,128)(2,1)S(1)}, u32[]{:S(2)}) copy-start(bf16[128,512]{1,0:T(8,128)(2,1)S(1)} %collective-permute-done.15.a3.d3) | copy-start | bytes 393220
  95.1 6.7 %copy-start = (bf16[512,768]{1,0:T(8,128)(2,1)}, bf16[512,768]{1,0:T(8,128)(2,1)S(1)}, u32[]{:S(2)}) copy-start(bf16[512,768]{1,0:T(8,128)(2,1)S(1)} %get-tuple-element.61.dadu_ref) | copy-start | bytes 2359300
  95.1 7.3 %collective-permute-start.16 = (bf16[512,2048]{1,0:T(8,128)(2,1)S(1)}, bf16[512,2048]{1,0:T(8,128)(2,1)S(1)}, u32[]{:S(2)}, u32[]{:S(2)}) collective-permute-start(bf16[512,2048]{1,0:T(8,128)(2,1)S(1)} %get-tuple-element.63), channel_id=1, source_target_pairs={{0,1},{1,0},{2,3},{3,2},{4,5},{5,4},{6,7},{7,6},{8,9},{9,8},{10,11... | collective-permute-start | bytes 6291464 | tf_op jit(solution)/shard_map/ppermute | solution.py:315
  101.7 9.8 %collective-permute-start.20 = (bf16[512,2048]{1,0:T(8,128)(2,1)}, bf16[512,2048]{1,0:T(8,128)(2,1)}, u32[]{:S(2)}, u32[]{:S(2)}) collective-permute-start(bf16[512,2048]{1,0:T(8,128)(2,1)} %get-tuple-element.69), channel_id=1, source_target_pairs={{0,1},{1,0},{2,3},{3,2},{4,5},{5,4},{6,7},{7,6},{8,9},{9,8},{10,11... | collective-permute-start | bytes 6291464 | tf_op jit(solution)/shard_map/ppermute | solution.py:315
  104.2 7.4 %copy-start.1 = (bf16[512,768]{1,0:T(8,128)(2,1)S(1)}, bf16[512,768]{1,0:T(8,128)(2,1)}, u32[]{:S(2)}) copy-start(bf16[512,768]{1,0:T(8,128)(2,1)} %copy-done) | copy-start | bytes 2359300
  104.2 35.6 %all-to-all-start.2 = ((bf16[16,32,2048]{2,1,0:T(8,128)(2,1)}), bf16[16,32,2048]{2,1,0:T(8,128)(2,1)S(1)}, u32[]{:S(2)}, u32[]{:S(2)}) async-start(bf16[16,32,2048]{2,1,0:T(8,128)(2,1)} %bitcast.7), calls=%async_computation.2 | async-start | bytes 4194304 | tf_op jit(solution)/shard_map/all_to_all | solution.py:318
  111.5 28.2 %copy-start.3 = (bf16[256,512]{1,0:T(8,128)(2,1)S(1)}, bf16[256,512]{1,0:T(8,128)(2,1)}, u32[]{:S(2)}) copy-start(bf16[256,512]{1,0:T(8,128)(2,1)} %copy-done.2) | copy-start | bytes 786436
  116.3 0.8 copy-start.13
  117.1 28.7 %collective-permute-start.21 = (bf16[512,512]{1,0:T(8,128)(2,1)}, bf16[512,512]{1,0:T(8,128)(2,1)S(1)}, u32[]{:S(2)}, u32[]{:S(2)}) collective-permute-start(bf16[512,512]{1,0:T(8,128)(2,1)} %get-tuple-element.71), channel_id=1, source_target_pairs={{0,6},{1,7},{2,0},{3,1},{4,2},{5,3},{6,4},{7,5},{8,14},{9,15},{10,... | collective-permute-start | bytes 1572872 | tf_op jit(solution)/shard_map/ppermute | solution.py:310
  117.8 28.0 %collective-permute-start.22 = (bf16[512,512]{1,0:T(8,128)(2,1)}, bf16[512,512]{1,0:T(8,128)(2,1)}, u32[]{:S(2)}, u32[]{:S(2)}) collective-permute-start(bf16[512,512]{1,0:T(8,128)(2,1)} %get-tuple-element.72), channel_id=1, source_target_pairs={{0,4},{1,5},{2,6},{3,7},{4,0},{5,1},{6,2},{7,3},{8,12},{9,13},{10,... | collective-permute-start | bytes 1572872 | tf_op jit(solution)/shard_map/ppermute | solution.py:310
  118.1 27.7 %collective-permute-start.23 = (bf16[512,512]{1,0:T(8,128)(2,1)}, bf16[512,512]{1,0:T(8,128)(2,1)}, u32[]{:S(2)}, u32[]{:S(2)}) collective-permute-start(bf16[512,512]{1,0:T(8,128)(2,1)} %get-tuple-element.73), channel_id=1, source_target_pairs={{0,2},{1,3},{2,4},{3,5},{4,6},{5,7},{6,0},{7,1},{8,10},{9,11},{10,... | collective-permute-start | bytes 1572872 | tf_op jit(solution)/shard_map/ppermute | solution.py:310
  139.8 1.0 copy-start.12
  140.8 0.8 copy-start.16
  141.6 4.2 %copy-start.14 = (bf16[512,512]{1,0:T(8,128)(2,1)S(1)}, bf16[512,512]{1,0:T(8,128)(2,1)}, u32[]{:S(2)}) copy-start(bf16[512,512]{1,0:T(8,128)(2,1)} %copy-done.13) | copy-start | bytes 1572868
  144.5 0.7 copy-start.19
  145.1 0.7 copy-start.21
  145.8 2.5 %copy-start.17 = (bf16[128,512]{1,0:T(8,128)(2,1)}, bf16[128,512]{1,0:T(8,128)(2,1)S(1)}, u32[]{:S(2)}) copy-start(bf16[128,512]{1,0:T(8,128)(2,1)S(1)} %get-tuple-element.65) | copy-start | bytes 393220
  145.8 12.6 %copy-start.22 = (bf16[128,512]{1,0:T(8,128)(2,1)S(1)}, bf16[128,512]{1,0:T(8,128)(2,1)}, u32[]{:S(2)}) copy-start(bf16[128,512]{1,0:T(8,128)(2,1)} %copy-done.21) | copy-start | bytes 393220
  145.8 15.3 %copy-start.20 = (bf16[128,512]{1,0:T(8,128)(2,1)S(1)}, bf16[128,512]{1,0:T(8,128)(2,1)}, u32[]{:S(2)}) copy-start(bf16[128,512]{1,0:T(8,128)(2,1)} %copy-done.19) | copy-start | bytes 393220
  145.8 9.6 %collective-permute-start.24 = (f32[128,2]{1,0:T(8,128)}, f32[128,2]{1,0:T(8,128)S(1)}, u32[]{:S(2)}, u32[]{:S(2)}) collective-permute-start(f32[128,2]{1,0:T(8,128)} %bitcast.11), channel_id=1, source_target_pairs={{0,1},{1,0},{2,3},{3,2},{4,5},{5,4},{6,7},{7,6},{8,9},{9,8},{10,11... | collective-permute-start | bytes 3080 | tf_op jit(solution)/shard_map/ppermute | solution.py:315
  145.8 26.0 %copy-start.6 = (bf16[128,512]{1,0:T(8,128)(2,1)S(1)}, bf16[128,512]{1,0:T(8,128)(2,1)}, u32[]{:S(2)}) copy-start(bf16[128,512]{1,0:T(8,128)(2,1)} %copy-done.5) | copy-start | bytes 393220
  145.8 26.0 %copy-start.8 = (bf16[128,512]{1,0:T(8,128)(2,1)S(1)}, bf16[128,512]{1,0:T(8,128)(2,1)}, u32[]{:S(2)}) copy-start(bf16[128,512]{1,0:T(8,128)(2,1)} %copy-done.7) | copy-start | bytes 393220
  145.8 26.0 %copy-start.10 = (bf16[128,512]{1,0:T(8,128)(2,1)S(1)}, bf16[128,512]{1,0:T(8,128)(2,1)}, u32[]{:S(2)}) copy-start(bf16[128,512]{1,0:T(8,128)(2,1)} %copy-done.9) | copy-start | bytes 393220
  148.3 23.6 %all-to-all-start.3 = ((bf16[16,32,512]{2,1,0:T(8,128)(2,1)}), bf16[16,32,512]{2,1,0:T(8,128)(2,1)S(1)}, u32[]{:S(2)}, u32[]{:S(2)}) async-start(bf16[16,32,512]{2,1,0:T(8,128)(2,1)} %bitcast.9), calls=%async_computation.3 | async-start | bytes 1048576 | tf_op jit(solution)/shard_map/all_to_all | solution.py:318
  156.3 6.3 %collective-permute-start.27 = (f32[128,2]{1,0:T(8,128)S(1)}, f32[128,2]{1,0:T(8,128)S(1)}, u32[]{:S(2)}, u32[]{:S(2)}) collective-permute-start(f32[128,2]{1,0:T(8,128)S(1)} %slice_add_fusion), channel_id=1, source_target_pairs={{0,6},{1,7},{2,0},{3,1},{4,2},{5,3},{6,4},{7,5},{8,14},{9,15},{10,... | collective-permute-start | bytes 3080 | tf_op jit(solution)/shard_map/ppermute | solution.py:310
  157.0 7.0 %collective-permute-start.26 = (f32[128,2]{1,0:T(8,128)S(1)}, f32[128,2]{1,0:T(8,128)S(1)}, u32[]{:S(2)}, u32[]{:S(2)}) collective-permute-start(f32[128,2]{1,0:T(8,128)S(1)} %slice_add_fusion), channel_id=1, source_target_pairs={{0,4},{1,5},{2,6},{3,7},{4,0},{5,1},{6,2},{7,3},{8,12},{9,13},{10,... | collective-permute-start | bytes 3080 | tf_op jit(solution)/shard_map/ppermute | solution.py:310
  157.3 6.7 %collective-permute-start.25 = (f32[128,2]{1,0:T(8,128)S(1)}, f32[128,2]{1,0:T(8,128)S(1)}, u32[]{:S(2)}, u32[]{:S(2)}) collective-permute-start(f32[128,2]{1,0:T(8,128)S(1)} %slice_add_fusion), channel_id=1, source_target_pairs={{0,2},{1,3},{2,4},{3,5},{4,6},{5,7},{6,0},{7,1},{8,10},{9,11},{10,... | collective-permute-start | bytes 3080 | tf_op jit(solution)/shard_map/ppermute | solution.py:310
  158.4 8.3 %collective-permute-start.17 = (bf16[128,512]{1,0:T(8,128)(2,1)S(1)}, bf16[128,512]{1,0:T(8,128)(2,1)S(1)}, u32[]{:S(2)}, u32[]{:S(2)}) collective-permute-start(bf16[128,512]{1,0:T(8,128)(2,1)S(1)} %copy-done.22), channel_id=1, source_target_pairs={{0,6},{1,7},{2,0},{3,1},{4,2},{5,3},{6,4},{7,5},{8,14},{9,15},{10,... | collective-permute-start | bytes 393224 | tf_op jit(solution)/shard_map/ppermute | solution.py:310
  161.0 7.9 %collective-permute-start.18 = (bf16[128,512]{1,0:T(8,128)(2,1)S(1)}, bf16[128,512]{1,0:T(8,128)(2,1)S(1)}, u32[]{:S(2)}, u32[]{:S(2)}) collective-permute-start(bf16[128,512]{1,0:T(8,128)(2,1)S(1)} %copy-done.20), channel_id=1, source_target_pairs={{0,4},{1,5},{2,6},{3,7},{4,0},{5,1},{6,2},{7,3},{8,12},{9,13},{10,... | collective-permute-start | bytes 393224 | tf_op jit(solution)/shard_map/ppermute | solution.py:310
  162.6 7.6 %collective-permute-start.19 = (bf16[128,512]{1,0:T(8,128)(2,1)S(1)}, bf16[128,512]{1,0:T(8,128)(2,1)S(1)}, u32[]{:S(2)}, u32[]{:S(2)}) collective-permute-start(bf16[128,512]{1,0:T(8,128)(2,1)S(1)} %get-tuple-element.68), channel_id=1, source_target_pairs={{0,2},{1,3},{2,4},{3,5},{4,6},{5,7},{6,0},{7,1},{8,10},{9,11},{10,... | collective-permute-start | bytes 393224 | tf_op jit(solution)/shard_map/ppermute | solution.py:310

commit v3 on v2

--- a/solution.py
+++ b/solution.py
@@ -32,37 +32,61 @@
     return act, (act * b).astype(BF16), b * s * (1.0 + a * (1.0 - s))
 
 
-def plan_kernel(routes_ref, gates_ref, cotan_ref, pick_ref, send_ref):
-    rows = routes_ref.shape[0]
+def column(ref, k):
+    rows = ref.shape[1]
+    eye = lax.broadcasted_iota(jnp.int32, (rows, rows), 0) == lax.broadcasted_iota(
+        jnp.int32, (rows, rows), 1
+    )
+    return jnp.sum(jnp.where(eye, ref[k : k + 1, :].astype(F32), 0.0), axis=1, keepdims=True)
+
+
+def plan_kernel(routes, gates, tokens, cotangent, pick_ref, send_ref, both_ref, *scratch):
+    routes_ref, gates_ref, sems = scratch
+    rows = tokens.shape[0]
     slots = pick_ref.shape[1]
+    load = Loads(sems)
+    first = load(routes, routes_ref)
+    copies = [
+        load(gates, gates_ref),
+        load(cotangent, both_ref.at[pl.ds(rows, rows), :]),
+        load(tokens, both_ref.at[pl.ds(0, rows), :]),
+    ]
+    first.wait()
     lane = lax.broadcasted_iota(jnp.int32, (rows, 128), 1)
-    one = [(routes_ref[:, k : k + 1] == lane).astype(F32) for k in range(2)]
+    route = [column(routes_ref, k).astype(jnp.int32) for k in range(2)]
+    one = [(route[k] == lane).astype(F32) for k in range(2)]
     lower = (
         lax.broadcasted_iota(jnp.int32, (rows, rows), 1)
         < lax.broadcasted_iota(jnp.int32, (rows, rows), 0)
     ).astype(BF16)
     earlier = dot(lower, (one[0] + one[1]).astype(BF16))
     place = lax.broadcasted_iota(jnp.int32, (rows, slots), 1)
-    cotan = cotan_ref[...].astype(F32)
+    wait(copies)
+    cotan = both_ref[rows:, :].astype(F32)
     total = None
     for k in range(2):
         pos = jnp.sum(earlier * one[k], axis=1, keepdims=True).astype(jnp.int32)
-        slot = routes_ref[:, k : k + 1] * CAPACITY + pos
+        slot = route[k] * CAPACITY + pos
         pick = (slot == place).astype(BF16)
         pick_ref[k * rows : (k + 1) * rows, :] = pick
-        scaled = (gates_ref[:, k : k + 1] * cotan).astype(BF16)
+        scaled = (column(gates_ref, k) * cotan).astype(BF16)
         term = dot_tn(pick, scaled)
         total = term if total is None else total + term
     send_ref[...] = total.astype(BF16)
 
 
-def rows_kernel(pick_ref, p0, p1, p2, p3, after, send_ref, pack_ref):
+def rows_kernel(pick_ref, p0, p1, p2, p3, after, send_ref, pack_ref, out, sems):
     rows = p0.shape[0] // 2
     width = p0.shape[1]
+    load = Loads(sems)
     pick = pick_ref[:rows, :] + pick_ref[rows:, :]
+    copies = []
     for d, piece in enumerate((p0, p1, p2, p3)):
+        at = pl.ds(d * width, width)
+        out[:, at] = dot_tn(pick, piece[:rows, :]).astype(BF16)
+        copies.append(load(out.at[:, at], send_ref.at[:, at]))
         pack_ref[d] = piece[...]
-        send_ref[:, d * width : (d + 1) * width] = dot_tn(pick, piece[:rows, :]).astype(BF16)
+    wait(copies)
 
 
 def starts(width):
@@ -131,29 +155,11 @@
         ref[...] = (mine[rows:, at].astype(F32) + got[rows:, at].astype(F32)).astype(ref.dtype)
 
 
-def back_kernel(*refs):
-    pieces, wd, g_ref, xs, vs, sems = refs[:8], refs[8], *refs[10:]
-    width = pieces[0].shape[1]
-    load = Loads(sems)
-    copies = [
-        [load(pieces[i], xs.at[i]), load(wd.at[:, pl.ds(at, width)], vs.at[i])]
-        for i, at in enumerate(starts(width))
-    ]
-    for i in range(8):
-        wait(copies[i])
-        term = dot_nt(xs[i], vs[i])
-        if i == 0:
-            g_ref[...] = term
-        else:
-            g_ref[...] += term
-
-
-def half_kernel(side, x, wg, wu, ab, xs, ws, sems):
+def half_loads(side, load, x, wg, wu, xs, ws):
     width = xs.shape[2]
     units = wg.shape[1]
-    load = Loads(sems)
     at = starts(width)[4 * side :]
-    copies = [
+    return [
         [
             load(x.at[:, pl.ds(d * width, width)], xs.at[d]),
             load(wg.at[pl.ds(at[d], width), :], ws.at[d, :, pl.ds(0, units)]),
@@ -161,6 +167,9 @@
         ]
         for d in range(4)
     ]
+
+
+def half_dots(side, copies, ab, xs, ws):
     for d in range(4):
         wait(copies[d])
         term = dot(xs[d], ws[d])
@@ -170,16 +179,36 @@
             ab[...] += term
 
 
+def early_kernel(*refs):
+    pieces, (wd, x, wg, wu), (g_ref, ab, cs, vs, xs, ws, sems) = refs[:8], refs[8:12], refs[12:]
+    width = cs.shape[2]
+    load = Loads(sems)
+    copies = [
+        [load(pieces[i], cs.at[i]), load(wd.at[:, pl.ds(at, width)], vs.at[i])]
+        for i, at in enumerate(starts(width))
+    ]
+    more = half_loads(0, load, x, wg, wu, xs, ws)
+    for i in range(8):
+        wait(copies[i])
+        term = dot_nt(cs[i], vs[i])
+        if i == 0:
+            g_ref[...] = term
+        else:
+            g_ref[...] += term
+    half_dots(0, more, ab, xs, ws)
+
+
 def forth_kernel(x, part, g_ref, wg, wu, wd, a1, a2, a3, oo, hid_ref, dadu_ref, ab, xs, ws, vs, gs, sems):
     width = xs.shape[2]
     units = wg.shape[1]
     load = Loads(sems)
     at = starts(width)
     first = load(part, ab)
+    copies = half_loads(1, load, x, wg, wu, xs, ws)
     more = [load(wd.at[:, pl.ds(at[4 + d], width)], vs.at[d]) for d in range(4)]
     copy_g = load(g_ref, gs)
     first.wait()
-    half_kernel(1, x, wg, wu, ab, xs, ws, sems.at[pl.ds(6, 12)])
+    half_dots(1, copies, ab, xs, ws)
     act, hidden, slope = gate_terms(ab[:, :units], ab[:, units:])
     copy_g.wait()
     g = gs[...]
@@ -235,29 +264,44 @@
     out[...] = (mine[...].astype(F32) + got[...].astype(F32)).astype(BF16)
 
 
-def sum_kernel(p0, p1, p2, p3, after, out):
+def sum_kernel(p0, p1, p2, p3, after, out, parts, sems):
+    load = Loads(sems)
+    copies = [load(p, parts.at[d]) for d, p in enumerate((p0, p1, p2, p3))]
+    wait(copies)
     out[...] = (
-        p0[...].astype(F32)
-        + p1[...].astype(F32)
-        + p2[...].astype(F32)
-        + p3[...].astype(F32)
+        parts[0].astype(F32)
+        + parts[1].astype(F32)
+        + parts[2].astype(F32)
+        + parts[3].astype(F32)
     ).astype(BF16)
 
 
-def mix_kernel(back, pick, gates, dense, pack, m0, m1, m2, m3, inner_ref):
-    rows = gates.shape[0]
-    width = pack.shape[2]
+def mix_kernel(back, pick, gates, dense, pack, *refs):
+    outs, inner_ref, (bs, ps, gs, ds, cs, sems) = refs[:SIDES], refs[SIDES], refs[SIDES + 1 :]
+    rows, width = outs[0].shape
+    load = Loads(sems)
+    small = [load(pick, ps), load(gates, gs), load(dense, ds)]
+    copies = [
+        [
+            load(back.at[:, pl.ds(d * width, width)], bs.at[d]),
+            load(pack.at[d, pl.ds(rows, rows), :], cs.at[d]),
+        ]
+        for d in range(SIDES)
+    ]
+    wait(small)
+    gate = [column(gs, k) for k in range(2)]
     inner = [None, None]
-    for d, out in enumerate((m0, m1, m2, m3)):
-        cotan = pack[d, rows:, :].astype(F32)
-        y = dot(pick[...], back[:, d * width : (d + 1) * width])
-        total = dense[:, d * width : (d + 1) * width].astype(F32)
+    for d in range(SIDES):
+        wait(copies[d])
+        cotan = cs[d].astype(F32)
+        y = dot(ps[...], bs[d])
+        total = ds[:, d * width : (d + 1) * width].astype(F32)
         for k in range(2):
             yk = y[k * rows : (k + 1) * rows, :]
-            total = total + gates[:, k : k + 1] * yk
+            total = total + gate[k] * yk
             term = jnp.sum(cotan * yk, axis=1, keepdims=True)
             inner[k] = term if inner[k] is None else inner[k] + term
-        out[...] = total.astype(BF16)
+        outs[d][...] = total.astype(BF16)
     lane = lax.broadcasted_iota(jnp.int32, (rows, 128), 1)
     inner_ref[...] = jnp.where(lane == 0, inner[0], jnp.where(lane == 1, inner[1], 0.0))
 
@@ -270,15 +314,18 @@
     out[...] = (dense + z).astype(BF16)
 
 
-def call(kernel, outs, limit, flops, args, name, far_args=(), scratch=()):
+def call(kernel, outs, limit, flops, args, name, far_args=(), scratch=(), far_out=False):
     vmem = pl.BlockSpec(memory_space=pltpu.VMEM)
     far = pl.BlockSpec(memory_space=pl.ANY)
     moved = sum(a.size * a.dtype.itemsize for a in args)
     return pl.pallas_call(
         kernel,
-        out_shape=[jax.ShapeDtypeStruct(*o) for o in outs],
+        out_shape=[
+            pltpu.HBM(*o) if far_out and i == 0 else jax.ShapeDtypeStruct(*o)
+            for i, o in enumerate(outs)
+        ],
         in_specs=[far if i in far_args else vmem for i in range(len(args))],
-        out_specs=[vmem] * len(outs),
+        out_specs=[far if far_out and i == 0 else vmem for i in range(len(outs))],
         compiler_params=pltpu.CompilerParams(vmem_limit_bytes=limit * MIB),
         cost_estimate=pl.CostEstimate(flops=flops, bytes_accessed=moved, transcendentals=0),
         scratch_shapes=list(scratch),
@@ -321,17 +368,18 @@
         return pltpu.with_memory_space_constraint(v, pltpu.HBM)
 
     wg, wu, wd = pin(expert_gate[0]), pin(expert_up[0]), pin(expert_down[0])
-    both = jnp.concatenate([tokens, cotangent], axis=0)
-    own = [both] + [along(both, d) for d in (1, 2, 3)]
     sems = pltpu.SemaphoreType.DMA
-    pick, grads_send = call(
+    pick, grads_send, both = call(
         plan_kernel,
-        [((2 * rows, slots), BF16), ((slots, width), BF16)],
+        [((2 * rows, slots), BF16), ((slots, width), BF16), ((2 * rows, width), BF16)],
         12,
         2 * 2 * rows * slots * width,
-        (routes, gates, cotangent),
+        (routes.T, gates.T, tokens, cotangent),
         "plan",
-    )
+        far_args=range(4),
+        scratch=[pltpu.VMEM((2, rows), jnp.int32), pltpu.VMEM((2, rows), F32), sems((4,))],
+    )
+    own = [both] + [along(both, d) for d in (1, 2, 3)]
     got_grads, own = lax.optimization_barrier((spread(grads_send), own))
     rows_send, pack = call(
         rows_kernel,
@@ -341,6 +389,8 @@
         (pick, *own, got_grads),
         "rows",
         far_args=(5,),
+        scratch=[pltpu.VMEM((slots, half), BF16), sems((SIDES,))],
+        far_out=True,
     )
     got_rows = spread(rows_send)
     grads_own = [got_grads] + [along(got_grads, d) for d in (1, 2, 3)]
@@ -370,33 +420,24 @@
         (dense_m, swap(dense_o)),
         "dense_sum",
     )
+    got_rows, _ = lax.optimization_barrier((got_rows, (grads_other, dense_part)))
+    rows_other = swap(got_rows)
     dense_got = [dense_part[0]] + [along(dense_part[d], SIDES - d) for d in (1, 2, 3)]
-    (g,) = call(
-        back_kernel,
-        [((slots, hidden), F32)],
-        16,
-        2 * slots * hidden * half * 2,
-        (*grads_own, *grads_other, wd, dense_part[0]),
-        "back",
-        far_args=range(10),
+    half_scratch = [pltpu.VMEM((4, slots, width), BF16), pltpu.VMEM((4, width, 2 * hidden), BF16)]
+    g, part = call(
+        early_kernel,
+        [((slots, hidden), F32), ((slots, 2 * hidden), F32)],
+        24,
+        8 * slots * hidden * half,
+        (*[pin(v) for v in (*grads_own, *grads_other)], wd, got_rows, wg, wu),
+        "early",
+        far_args=range(12),
         scratch=[
             pltpu.VMEM((8, slots, width), BF16),
             pltpu.VMEM((8, hidden, width), BF16),
-            sems((16,)),
+            *half_scratch,
+            sems((28,)),
         ],
-    )
-    got_rows, g, dense_m = lax.optimization_barrier((got_rows, g, dense_m))
-    rows_other = swap(got_rows)
-    half_scratch = [pltpu.VMEM((4, slots, width), BF16), pltpu.VMEM((4, width, 2 * hidden), BF16)]
-    (part,) = call(
-        functools.partial(half_kernel, 0),
-        [((slots, 2 * hidden), F32)],
-        16,
-        4 * slots * hidden * half,
-        (got_rows, wg, wu),
-        "half",
-        far_args=(0, 1, 2),
-        scratch=[*half_scratch, sems((12,))],
     )
     out_o, hid, dadu = call(
         forth_kernel,
@@ -451,8 +492,17 @@
         [((rows, width), BF16)] * 4 + [((rows, 128), F32)],
         16,
         4 * rows * slots * half,
-        (out_back, pick, gates, dense_out, pack),
+        (out_back, pin(pick), gates.T, pin(dense_out), pin(pack)),
         "mix",
+        far_args=range(5),
+        scratch=[
+            pltpu.VMEM((SIDES, slots, width), BF16),
+            pltpu.VMEM((2 * rows, slots), BF16),
+            pltpu.VMEM((2, rows), F32),
+            pltpu.VMEM((rows, half), BF16),
+            pltpu.VMEM((SIDES, rows, width), BF16),
+            sems((11,)),
+        ],
     )
     (grad_sum,) = call(
         sum_kernel,
@@ -461,7 +511,8 @@
         3 * slots * width,
         (*grad_all, inner),
         "sum",
-        far_args=(4,),
+        far_args=range(5),
+        scratch=[pltpu.VMEM((SIDES, slots, width), BF16), sems((SIDES,))],
     )
     grad_back = spread(grad_sum)
     mixed = m0.astype(F32)

time: 174 us -> 165 us (0.948)
  local copies, waits for them, and re-layouts: 11.8 us -> 6.28 us
  waiting for transfers between devices: 59.6 us -> 56.5 us
  starting transfers between devices: 50.6 us -> 52.5 us
  other arithmetic: 2.49 us -> 0.75 us
    unnamed x56 -> x39, local copies, waits for them, and re-layouts: 10.9 us -> 6.28 us
    all_to_all x4, waiting for transfers between devices: 20.6 us -> 17.9 us  [spread(): return lax.all_to_all(v, 'dp', split_axis=0, concat_axis=0, tiled=True)]
    ppermute x18, starting transfers between devices: 18.5 us -> 20.4 us  [along(): lax.ppermute(v, 'tensor', [(i, (i + 2 * d) % devices) for i in range(devi...]
    pallas_call x13 -> x12, Pallas kernels: 47.4 us -> 47 us  [call(): pl.pallas_call(kernel, out_shape=[pltpu.HBM(*o) if far_out and i == 0 els...]
  transfers between devices with their start and end apart: 32 -> 32, of which waited for: 15 -> 15; matrix products, arithmetic and copies ran while one was open for 3% -> 1% of each run, Pallas kernels for 21% -> 21%
where the time goes in v3:
time: 165 us; the launch traced here: 164 us
  waiting for transfers between devices  56.5 us (34%)
  starting transfers between devices  52.5 us (32%)
  Pallas kernels  47 us (28%)
  local copies, waits for them, and re-layouts  6.28 us (4%)
    pallas_call x12, Pallas kernels, call(): pl.pallas_call(kernel, out_shape=[pltpu.HBM(*o) if far_out and i == 0 els...  47 us
    ppermute x18, waiting for transfers between devices, along(): lax.ppermute(v, 'tensor', [(i, (i + 2 * d) % devices) for i in range(devi...  36.8 us
    all_to_all x4, starting transfers between devices, spread(): return lax.all_to_all(v, 'dp', split_axis=0, concat_axis=0, tiled=True)  30 us
    ppermute x18, starting transfers between devices, along(): lax.ppermute(v, 'tensor', [(i, (i + 2 * d) % devices) for i in range(devi...  20.4 us
    all_to_all x4, waiting for transfers between devices, spread(): return lax.all_to_all(v, 'dp', split_axis=0, concat_axis=0, tiled=True)  17.9 us
    unnamed x39, local copies, waits for them, and re-layouts  6.28 us
  transfers between devices with their start and end apart: 32, of which 15 were waited for; matrix products, arithmetic and copies ran while one was open for 1% of the time, Pallas kernels for 21%

profile of v3, /device:TPU:2, one launch (start us, length us, event | category | flops | bytes accessed | tf_op | source)
XLA Modules:
  0.0 164.1 jit_solution(17730575672642492385)
XLA Ops:
  0.6 0.7 copy-done.6
  1.3 0.9 copy-done.8
  2.2 0.9 copy-done.9
  3.1 0.7 copy-done.12
  3.8 2.0 %plan.1 = (bf16[256,512]{1,0:T(8,128)(2,1)S(1)}, bf16[512,512]{1,0:T(8,128)(2,1)}, bf16[256,512]{1,0:T(8,128)(2,1)S(1)}) custom-call(s32[2,128]{1,0:T(2,128)S(1)} %bitcast.27, f32[2,128]{1,0:T(2,128)S(1)} %bitcast.25, bf16[128,512]{1,0:T(8,128)(2,1)S(1)} %copy-done.8, bf16[128,512]{1,0:T(8,128)(2,1)S(1)} %copy-done.9), custom_call_target="tpu_custom_call" | custom-call | flops 134217728 | bytes 264192 | tf_op jit(solution)/shard_map/plan/pallas_call | solution.py:321
  5.8 8.3 %all-to-all-start = ((bf16[16,32,512]{2,1,0:T(8,128)(2,1)}), bf16[16,32,512]{2,1,0:T(8,128)(2,1)S(1)}, u32[]{:S(2)}, u32[]{:S(2)}) async-start(bf16[16,32,512]{2,1,0:T(8,128)(2,1)} %bitcast.2), calls=%async_computation | async-start | bytes 1048576 | tf_op jit(solution)/shard_map/all_to_all | solution.py:365
  14.1 3.0 %collective-permute-start.2 = (bf16[256,512]{1,0:T(8,128)(2,1)S(1)}, bf16[256,512]{1,0:T(8,128)(2,1)S(1)}, u32[]{:S(2)}, u32[]{:S(2)}) collective-permute-start(bf16[256,512]{1,0:T(8,128)(2,1)S(1)} %get-tuple-element.44.p0), channel_id=1, source_target_pairs={{0,6},{1,7},{2,0},{3,1},{4,2},{5,3},{6,4},{7,5},{8,14},{9,15},{10,... | collective-permute-start | bytes 786440 | tf_op jit(solution)/shard_map/ppermute | solution.py:357
  17.1 0.6 collective-permute-start.1
  17.8 1.0 collective-permute-start
  18.8 9.0 %collective-permute-done.2.p3 = bf16[256,512]{1,0:T(8,128)(2,1)S(1)} collective-permute-done((bf16[256,512]{1,0:T(8,128)(2,1)S(1)}, bf16[256,512]{1,0:T(8,128)(2,1)S(1)}, u32[]{:S(2)}, u32[]{:S(2)}) %collective-permute-start.2) | collective-permute-done | bytes 262176 | tf_op jit(solution)/shard_map/ppermute | solution.py:357
  27.8 0.1 collective-permute-done.1.p2
  27.9 3.6 %collective-permute-done.p1 = bf16[256,512]{1,0:T(8,128)(2,1)S(1)} collective-permute-done((bf16[256,512]{1,0:T(8,128)(2,1)S(1)}, bf16[256,512]{1,0:T(8,128)(2,1)S(1)}, u32[]{:S(2)}, u32[]{:S(2)}) %collective-permute-start) | collective-permute-done | bytes 262176 | tf_op jit(solution)/shard_map/ppermute | solution.py:357
  31.5 2.7 %rows.1 = (bf16[512,2048]{1,0:T(8,128)(2,1)}, bf16[4,256,512]{2,1,0:T(8,128)(2,1)}) custom-call(bf16[256,512]{1,0:T(8,128)(2,1)S(1)} %get-tuple-element.41.pick_ref.pick, bf16[256,512]{1,0:T(8,128)(2,1)S(1)} %get-tuple-element.44.p0, bf16[256,512]{1,0:T(8,128)(2,1)S(1)} %collective-permute-done.p1, bf16[256,512]{1,0:T(8,128)(2,1)S(1)} %collective-permute-done.1.p2, ...), custom_call_target="tpu_custom_call" | custom-call | flops 268435456 | bytes 1835008 | tf_op jit(solution)/shard_map/rows/pallas_call | solution.py:321
  34.2 0.1 collective-permute-start.7
  34.3 7.2 %all-to-all-start.1 = ((bf16[16,32,2048]{2,1,0:T(8,128)(2,1)}), bf16[16,32,2048]{2,1,0:T(8,128)(2,1)S(1)}, u32[]{:S(2)}, u32[]{:S(2)}) async-start(bf16[16,32,2048]{2,1,0:T(8,128)(2,1)} %bitcast.39), calls=%async_computation.1 | async-start | bytes 4194304 | tf_op jit(solution)/shard_map/all_to_all | solution.py:365
  41.5 0.6 collective-permute-start.6
  42.1 0.6 collective-permute-start.5
  42.8 0.8 collective-permute-start.4
  43.6 9.4 %dense.1 = (bf16[256,2048]{1,0:T(8,128)(2,1)S(1)}, bf16[256,2048]{1,0:T(8,128)(2,1)S(1)}) custom-call(bf16[4,256,512]{2,1,0:T(8,128)(2,1)} %get-tuple-element.50.refs_0_.pack, bf16[4,256,512]{2,1,0:T(8,128)(2,1)} %collective-permute-done.7.refs_1_, bf16[4096,512]{1,0:T(8,128)(2,1)} %refs_2_.1, bf16[4096,512]{1,0:T(8,128)(2,1)} %refs_3_.1, ...), custom_call_target="tpu_custom_call" | custom-call | flops 3221225472 | bytes 14680064 | tf_op jit(solution)/shard_map/dense/pallas_call | solution.py:321
  53.0 0.5 collective-permute-start.3
  53.5 2.8 %collective-permute-done.6.refs_3_ = bf16[512,512]{1,0:T(8,128)(2,1)S(1)} collective-permute-done((bf16[512,512]{1,0:T(8,128)(2,1)S(1)}, bf16[512,512]{1,0:T(8,128)(2,1)S(1)}, u32[]{:S(2)}, u32[]{:S(2)}) %collective-permute-start.6) | collective-permute-done | bytes 524320 | tf_op jit(solution)/shard_map/ppermute | solution.py:357
  56.3 2.2 %collective-permute-done.5.refs_2_ = bf16[512,512]{1,0:T(8,128)(2,1)S(1)} collective-permute-done((bf16[512,512]{1,0:T(8,128)(2,1)S(1)}, bf16[512,512]{1,0:T(8,128)(2,1)S(1)}, u32[]{:S(2)}, u32[]{:S(2)}) %collective-permute-start.5) | collective-permute-done | bytes 524320 | tf_op jit(solution)/shard_map/ppermute | solution.py:357
  58.5 9.8 %collective-permute-done.4.refs_1_ = bf16[512,512]{1,0:T(8,128)(2,1)S(1)} collective-permute-done((bf16[512,512]{1,0:T(8,128)(2,1)S(1)}, bf16[512,512]{1,0:T(8,128)(2,1)S(1)}, u32[]{:S(2)}, u32[]{:S(2)}) %collective-permute-start.4) | collective-permute-done | bytes 524320 | tf_op jit(solution)/shard_map/ppermute | solution.py:357
  68.4 0.5 collective-permute-start.9
  68.9 0.2 dense_sum.1
  69.1 0.8 copy-done.3
  70.0 0.3 collective-permute-done.8.refs_5_
  70.2 1.5 collective-permute-done.9.refs_6_
  71.8 0.8 copy-done.18
  72.6 0.1 collective-permute-start.12
  72.7 0.9 collective-permute-start.13
  73.7 0.3 collective-permute-start.14
  74.0 0.8 collective-permute-start.15
  74.8 7.1 %early.1 = (f32[512,384]{1,0:T(8,128)S(1)}, f32[512,768]{1,0:T(8,128)S(1)}) custom-call(bf16[512,512]{1,0:T(8,128)(2,1)} %bitcast.22, bf16[512,512]{1,0:T(8,128)(2,1)} %copy-done.15, bf16[512,512]{1,0:T(8,128)(2,1)} %copy-done.14, bf16[512,512]{1,0:T(8,128)(2,1)} %copy-done.13, bf16[512,512]{1,0:T(8,128)(2,1)} %copy-done.16, bf16[512,512]{1,0:T(8,128)(2,1)} %copy-done.17, ...), custom_call_target="tpu_custom_call" | custom-call | flops 3221225472 | bytes 15728640 | tf_op jit(solution)/shard_map/early/pallas_call | solution.py:321
  82.0 1.5 collective-permute-done.15.a3.d3
  83.5 6.4 %forth.1 = (bf16[512,2048]{1,0:T(8,128)(2,1)S(1)}, bf16[512,384]{1,0:T(8,128)(2,1)S(1)}, bf16[512,768]{1,0:T(8,128)(2,1)S(1)}) custom-call(bf16[512,2048]{1,0:T(8,128)(2,1)S(1)} %collective-permute-done.12.x, f32[512,768]{1,0:T(8,128)S(1)} %get-tuple-element.62.part, f32[512,384]{1,0:T(8,128)S(1)} %get-tuple-element.63.g_ref, bf16[4096,384]{1,0:T(8,128)(2,1)} %bitcast.29, ...), custom_call_target="tpu_custom_call" | custom-call | flops 2415919104 | bytes 14286848 | tf_op jit(solution)/shard_map/forth/pallas_call | solution.py:321
  89.9 0.1 collective-permute-start.16
  90.0 6.4 %cross.1 = (bf16[512,2048]{1,0:T(8,128)(2,1)S(1)}, bf16[512,2048]{1,0:T(8,128)(2,1)}) custom-call(bf16[512,384]{1,0:T(8,128)(2,1)S(1)} %get-tuple-element.64.hid_ref, bf16[512,768]{1,0:T(8,128)(2,1)S(1)} %get-tuple-element.65.dadu_ref, bf16[4096,384]{1,0:T(8,128)(2,1)} %bitcast.30, bf16[4096,384]{1,0:T(8,128)(2,1)} %bitcast.34, bf16[384,4096]{1,0:T(8,128)(2,1)} %bitcast.38), custom_call_target="tpu_custom_call" | custom-call | flops 2415919104 | bytes 10616832 | tf_op jit(solution)/shard_map/cross/pallas_call | solution.py:321
  96.4 0.6 collective-permute-start.20
  96.9 1.8 %add.36 = bf16[512,2048]{1,0:T(8,128)(2,1)} custom-call(bf16[512,2048]{1,0:T(8,128)(2,1)S(1)} %get-tuple-element.66.mine, bf16[512,2048]{1,0:T(8,128)(2,1)S(1)} %collective-permute-done.16.got), custom_call_target="tpu_custom_call" | custom-call | flops 1048576 | bytes 4194304 | tf_op jit(solution)/shard_map/add/pallas_call | solution.py:321
  98.8 7.2 %all-to-all-start.2 = ((bf16[16,32,2048]{2,1,0:T(8,128)(2,1)}), bf16[16,32,2048]{2,1,0:T(8,128)(2,1)S(1)}, u32[]{:S(2)}, u32[]{:S(2)}) async-start(bf16[16,32,2048]{2,1,0:T(8,128)(2,1)} %bitcast.9), calls=%async_computation.2 | async-start | bytes 4194304 | tf_op jit(solution)/shard_map/all_to_all | solution.py:365
  106.0 4.7 %down.1 = (bf16[512,512]{1,0:T(8,128)(2,1)S(1)}, bf16[512,512]{1,0:T(8,128)(2,1)}, bf16[512,512]{1,0:T(8,128)(2,1)}, bf16[512,512]{1,0:T(8,128)(2,1)}) custom-call(bf16[512,768]{1,0:T(8,128)(2,1)S(1)} %get-tuple-element.65.dadu_ref, bf16[4096,384]{1,0:T(8,128)(2,1)} %bitcast.31, bf16[4096,384]{1,0:T(8,128)(2,1)} %bitcast.35, ...), custom_call_target="tpu_custom_call" | custom-call | flops 1610612736 | bytes 9175040 | tf_op jit(solution)/shard_map/down/pallas_call | solution.py:321
  110.7 0.8 copy-done.4
  111.5 1.2 collective-permute-start.21
  112.7 1.8 %collective-permute-start.22 = (bf16[512,512]{1,0:T(8,128)(2,1)}, bf16[512,512]{1,0:T(8,128)(2,1)}, u32[]{:S(2)}, u32[]{:S(2)}) collective-permute-start(bf16[512,512]{1,0:T(8,128)(2,1)} %get-tuple-element.76), channel_id=1, source_target_pairs={{0,4},{1,5},{2,6},{3,7},{4,0},{5,1},{6,2},{7,3},{8,12},{9,13},{10,... | collective-permute-start | bytes 1572872 | tf_op jit(solution)/shard_map/ppermute | solution.py:357
  114.5 1.1 collective-permute-start.23
  115.6 17.9 %all-to-all-done.2 = bf16[16,32,2048]{2,1,0:T(8,128)(2,1)S(1)} async-done(((bf16[16,32,2048]{2,1,0:T(8,128)(2,1)}), bf16[16,32,2048]{2,1,0:T(8,128)(2,1)S(1)}, u32[]{:S(2)}, u32[]{:S(2)}) %all-to-all-start.2) | async-done | bytes 2097184 | tf_op jit(solution)/shard_map/all_to_all | solution.py:365
  133.4 2.9 %mix.1 = (bf16[128,512]{1,0:T(8,128)(2,1)S(1)}, bf16[128,512]{1,0:T(8,128)(2,1)S(1)}, bf16[128,512]{1,0:T(8,128)(2,1)S(1)}, bf16[128,512]{1,0:T(8,128)(2,1)S(1)}, f32[128,128]{1,0:T(8,128)S(1)}) custom-call(bf16[512,2048]{1,0:T(8,128)(2,1)S(1)} %bitcast.16, bf16[256,512]{1,0:T(8,128)(2,1)} %copy-done.1, f32[2,128]{1,0:T(2,128)S(1)} %bitcast.26, ...), custom_call_target="tpu_custom_call" | custom-call | flops 536870912 | bytes 3933184 | tf_op jit(solution)/shard_map/mix/pallas_call | solution.py:321
  136.5 2.3 %collective-permute-done.23.p3 = bf16[512,512]{1,0:T(8,128)(2,1)} collective-permute-done((bf16[512,512]{1,0:T(8,128)(2,1)}, bf16[512,512]{1,0:T(8,128)(2,1)}, u32[]{:S(2)}, u32[]{:S(2)}) %collective-permute-start.23) | collective-permute-done | bytes 524320 | tf_op jit(solution)/shard_map/ppermute | solution.py:357
  138.8 2.5 %sum.1 = bf16[512,512]{1,0:T(8,128)(2,1)} custom-call(bf16[512,512]{1,0:T(8,128)(2,1)S(1)} %copy-done.5, bf16[512,512]{1,0:T(8,128)(2,1)} %collective-permute-done.21.p1, bf16[512,512]{1,0:T(8,128)(2,1)} %collective-permute-done.22.p2, bf16[512,512]{1,0:T(8,128)(2,1)} %collective-permute-done.23.p3, f32[128,128]{1,0:T(8,128)S(1)} %get-tuple-element.78.after), custom_call_target="tpu_custom_call" | custom-call | flops 786432 | bytes 2162688 | tf_op jit(solution)/shard_map/sum/pallas_call | solution.py:321
  141.3 7.2 %all-to-all-start.3 = ((bf16[16,32,512]{2,1,0:T(8,128)(2,1)}), bf16[16,32,512]{2,1,0:T(8,128)(2,1)S(1)}, u32[]{:S(2)}, u32[]{:S(2)}) async-start(bf16[16,32,512]{2,1,0:T(8,128)(2,1)} %bitcast.11), calls=%async_computation.3 | async-start | bytes 1048576 | tf_op jit(solution)/shard_map/all_to_all | solution.py:365
  148.6 0.7 collective-permute-start.27
  149.3 1.8 %collective-permute-start.26 = (f32[128,2]{1,0:T(8,128)S(1)}, f32[128,2]{1,0:T(8,128)S(1)}, u32[]{:S(2)}, u32[]{:S(2)}) collective-permute-start(f32[128,2]{1,0:T(8,128)S(1)} %slice_add_fusion), channel_id=1, source_target_pairs={{0,4},{1,5},{2,6},{3,7},{4,0},{5,1},{6,2},{7,3},{8,12},{9,13},{10,... | collective-permute-start | bytes 3080 | tf_op jit(solution)/shard_map/ppermute | solution.py:357
  151.0 0.8 collective-permute-start.25
  151.8 2.4 %collective-permute-start.17 = (bf16[128,512]{1,0:T(8,128)(2,1)}, bf16[128,512]{1,0:T(8,128)(2,1)S(1)}, u32[]{:S(2)}, u32[]{:S(2)}) collective-permute-start(bf16[128,512]{1,0:T(8,128)(2,1)} %copy-done.11), channel_id=1, source_target_pairs={{0,6},{1,7},{2,0},{3,1},{4,2},{5,3},{6,4},{7,5},{8,14},{9,15},{10,... | collective-permute-start | bytes 393224 | tf_op jit(solution)/shard_map/ppermute | solution.py:357
  154.3 0.5 collective-permute-start.18
  154.8 1.4 collective-permute-start.19
  156.3 0.3 collective-permute-done.25
  156.5 0.6 copy.13
  157.2 2.0 %collective-permute-done.17 = bf16[128,512]{1,0:T(8,128)(2,1)S(1)} collective-permute-done((bf16[128,512]{1,0:T(8,128)(2,1)}, bf16[128,512]{1,0:T(8,128)(2,1)S(1)}, u32[]{:S(2)}, u32[]{:S(2)}) %collective-permute-start.17) | collective-permute-done | bytes 131104 | tf_op jit(solution)/shard_map/ppermute | solution.py:357
  159.2 2.2 %collective-permute-done.18 = bf16[128,512]{1,0:T(8,128)(2,1)S(1)} collective-permute-done((bf16[128,512]{1,0:T(8,128)(2,1)}, bf16[128,512]{1,0:T(8,128)(2,1)S(1)}, u32[]{:S(2)}, u32[]{:S(2)}) %collective-permute-start.18) | collective-permute-done | bytes 131104 | tf_op jit(solution)/shard_map/ppermute | solution.py:357
  161.4 1.0 collective-permute-done.19
  162.4 0.7 add_convert_fusion
  163.2 0.9 grad.1
  (54 shorter events, 0.3 us)
Async XLA Ops:
  0.6 0.7 copy-start.6
  1.3 0.9 copy-start.8
  2.2 0.9 copy-start.9
  3.1 0.7 copy-start.12
  5.8 28.5 %copy-start.1 = (bf16[256,512]{1,0:T(8,128)(2,1)}, bf16[256,512]{1,0:T(8,128)(2,1)S(1)}, u32[]{:S(2)}) copy-start(bf16[256,512]{1,0:T(8,128)(2,1)S(1)} %get-tuple-element.41.pick_ref.pick) | copy-start | bytes 786436
  5.8 25.7 %all-to-all-start = ((bf16[16,32,512]{2,1,0:T(8,128)(2,1)}), bf16[16,32,512]{2,1,0:T(8,128)(2,1)S(1)}, u32[]{:S(2)}, u32[]{:S(2)}) async-start(bf16[16,32,512]{2,1,0:T(8,128)(2,1)} %bitcast.2), calls=%async_computation | async-start | bytes 1048576 | tf_op jit(solution)/shard_map/all_to_all | solution.py:365
  14.1 13.6 %collective-permute-start.2 = (bf16[256,512]{1,0:T(8,128)(2,1)S(1)}, bf16[256,512]{1,0:T(8,128)(2,1)S(1)}, u32[]{:S(2)}, u32[]{:S(2)}) collective-permute-start(bf16[256,512]{1,0:T(8,128)(2,1)S(1)} %get-tuple-element.44.p0), channel_id=1, source_target_pairs={{0,6},{1,7},{2,0},{3,1},{4,2},{5,3},{6,4},{7,5},{8,14},{9,15},{10,... | collective-permute-start | bytes 786440 | tf_op jit(solution)/shard_map/ppermute | solution.py:357
  17.1 10.7 %collective-permute-start.1 = (bf16[256,512]{1,0:T(8,128)(2,1)S(1)}, bf16[256,512]{1,0:T(8,128)(2,1)S(1)}, u32[]{:S(2)}, u32[]{:S(2)}) collective-permute-start(bf16[256,512]{1,0:T(8,128)(2,1)S(1)} %get-tuple-element.44.p0), channel_id=1, source_target_pairs={{0,4},{1,5},{2,6},{3,7},{4,0},{5,1},{6,2},{7,3},{8,12},{9,13},{10,... | collective-permute-start | bytes 786440 | tf_op jit(solution)/shard_map/ppermute | solution.py:357
  17.8 13.7 %collective-permute-start = (bf16[256,512]{1,0:T(8,128)(2,1)S(1)}, bf16[256,512]{1,0:T(8,128)(2,1)S(1)}, u32[]{:S(2)}, u32[]{:S(2)}) collective-permute-start(bf16[256,512]{1,0:T(8,128)(2,1)S(1)} %get-tuple-element.44.p0), channel_id=1, source_target_pairs={{0,2},{1,3},{2,4},{3,5},{4,6},{5,7},{6,0},{7,1},{8,10},{9,11},{10,... | collective-permute-start | bytes 786440 | tf_op jit(solution)/shard_map/ppermute | solution.py:357
  31.5 21.6 %copy-start = (bf16[16,32,512]{2,1,0:T(8,128)(2,1)}, bf16[16,32,512]{2,1,0:T(8,128)(2,1)S(1)}, u32[]{:S(2)}) copy-start(bf16[16,32,512]{2,1,0:T(8,128)(2,1)S(1)} %all-to-all-done) | copy-start | bytes 1572868
  34.2 9.4 %collective-permute-start.7 = (bf16[4,256,512]{2,1,0:T(8,128)(2,1)}, bf16[4,256,512]{2,1,0:T(8,128)(2,1)}, u32[]{:S(2)}, u32[]{:S(2)}) collective-permute-start(bf16[4,256,512]{2,1,0:T(8,128)(2,1)} %get-tuple-element.50.refs_0_.pack), channel_id=1, source_target_pairs={{0,1},{1,0},{2,3},{3,2},{4,5},{5,4},{6,7},{7,6},{8,9},{9,8},{10,11... | collective-permute-start | bytes 3145736 | tf_op jit(solution)/shard_map/ppermute | solution.py:362
  34.3 38.3 %all-to-all-start.1 = ((bf16[16,32,2048]{2,1,0:T(8,128)(2,1)}), bf16[16,32,2048]{2,1,0:T(8,128)(2,1)S(1)}, u32[]{:S(2)}, u32[]{:S(2)}) async-start(bf16[16,32,2048]{2,1,0:T(8,128)(2,1)} %bitcast.39), calls=%async_computation.1 | async-start | bytes 4194304 | tf_op jit(solution)/shard_map/all_to_all | solution.py:365
  41.5 14.8 %collective-permute-start.6 = (bf16[512,512]{1,0:T(8,128)(2,1)S(1)}, bf16[512,512]{1,0:T(8,128)(2,1)S(1)}, u32[]{:S(2)}, u32[]{:S(2)}) collective-permute-start(bf16[512,512]{1,0:T(8,128)(2,1)S(1)} %bitcast.18), channel_id=1, source_target_pairs={{0,6},{1,7},{2,0},{3,1},{4,2},{5,3},{6,4},{7,5},{8,14},{9,15},{10,... | collective-permute-start | bytes 1572872 | tf_op jit(solution)/shard_map/ppermute | solution.py:357
  42.1 16.4 %collective-permute-start.5 = (bf16[512,512]{1,0:T(8,128)(2,1)S(1)}, bf16[512,512]{1,0:T(8,128)(2,1)S(1)}, u32[]{:S(2)}, u32[]{:S(2)}) collective-permute-start(bf16[512,512]{1,0:T(8,128)(2,1)S(1)} %bitcast.19), channel_id=1, source_target_pairs={{0,4},{1,5},{2,6},{3,7},{4,0},{5,1},{6,2},{7,3},{8,12},{9,13},{10,... | collective-permute-start | bytes 1572872 | tf_op jit(solution)/shard_map/ppermute | solution.py:357
  42.8 25.6 %collective-permute-start.4 = (bf16[512,512]{1,0:T(8,128)(2,1)S(1)}, bf16[512,512]{1,0:T(8,128)(2,1)S(1)}, u32[]{:S(2)}, u32[]{:S(2)}) collective-permute-start(bf16[512,512]{1,0:T(8,128)(2,1)S(1)} %bitcast.20), channel_id=1, source_target_pairs={{0,2},{1,3},{2,4},{3,5},{4,6},{5,7},{6,0},{7,1},{8,10},{9,11},{10,... | collective-permute-start | bytes 1572872 | tf_op jit(solution)/shard_map/ppermute | solution.py:357
  52.9 15.9 %collective-permute-start.11 = (bf16[256,2048]{1,0:T(8,128)(2,1)S(1)}, bf16[256,2048]{1,0:T(8,128)(2,1)S(1)}, u32[]{:S(2)}, u32[]{:S(2)}) collective-permute-start(bf16[256,2048]{1,0:T(8,128)(2,1)S(1)} %get-tuple-element.56), channel_id=1, source_target_pairs={{0,1},{1,0},{2,3},{3,2},{4,5},{5,4},{6,7},{7,6},{8,9},{9,8},{10,11... | collective-permute-start | bytes 3145736 | tf_op jit(solution)/shard_map/ppermute | solution.py:362
  53.0 16.9 %collective-permute-start.3 = (bf16[512,512]{1,0:T(8,128)(2,1)S(1)}, bf16[512,512]{1,0:T(8,128)(2,1)S(1)}, u32[]{:S(2)}, u32[]{:S(2)}) collective-permute-start(bf16[512,512]{1,0:T(8,128)(2,1)S(1)} %bitcast.21), channel_id=1, source_target_pairs={{0,1},{1,0},{2,3},{3,2},{4,5},{5,4},{6,7},{7,6},{8,9},{9,8},{10,11... | collective-permute-start | bytes 1572872 | tf_op jit(solution)/shard_map/ppermute | solution.py:362
  56.3 15.4 %copy-start.13 = (bf16[512,512]{1,0:T(8,128)(2,1)}, bf16[512,512]{1,0:T(8,128)(2,1)S(1)}, u32[]{:S(2)}) copy-start(bf16[512,512]{1,0:T(8,128)(2,1)S(1)} %collective-permute-done.6.refs_3_) | copy-start | bytes 1572868
  58.5 13.2 %copy-start.14 = (bf16[512,512]{1,0:T(8,128)(2,1)}, bf16[512,512]{1,0:T(8,128)(2,1)S(1)}, u32[]{:S(2)}) copy-start(bf16[512,512]{1,0:T(8,128)(2,1)S(1)} %collective-permute-done.5.refs_2_) | copy-start | bytes 1572868
  68.3 3.4 %copy-start.15 = (bf16[512,512]{1,0:T(8,128)(2,1)}, bf16[512,512]{1,0:T(8,128)(2,1)S(1)}, u32[]{:S(2)}) copy-start(bf16[512,512]{1,0:T(8,128)(2,1)S(1)} %collective-permute-done.4.refs_1_) | copy-start | bytes 1572868
  68.3 1.9 %collective-permute-start.8 = (bf16[512,512]{1,0:T(8,128)(2,1)S(1)}, bf16[512,512]{1,0:T(8,128)(2,1)S(1)}, u32[]{:S(2)}, u32[]{:S(2)}) collective-permute-start(bf16[512,512]{1,0:T(8,128)(2,1)S(1)} %collective-permute-done.4.refs_1_), channel_id=1, source_target_pairs={{0,1},{1,0},{2,3},{3,2},{4,5},{5,4},{6,7},{7,6},{8,9},{9,8},{10,11... | collective-permute-start | bytes 1572872 | tf_op jit(solution)/shard_map/ppermute | solution.py:362
  68.4 3.4 %collective-permute-start.9 = (bf16[512,512]{1,0:T(8,128)(2,1)S(1)}, bf16[512,512]{1,0:T(8,128)(2,1)S(1)}, u32[]{:S(2)}, u32[]{:S(2)}) collective-permute-start(bf16[512,512]{1,0:T(8,128)(2,1)S(1)} %collective-permute-done.5.refs_2_), channel_id=1, source_target_pairs={{0,1},{1,0},{2,3},{3,2},{4,5},{5,4},{6,7},{7,6},{8,9},{9,8},{10,11... | collective-permute-start | bytes 1572872 | tf_op jit(solution)/shard_map/ppermute | solution.py:362
  68.8 3.8 %collective-permute-start.10 = (bf16[512,512]{1,0:T(8,128)(2,1)S(1)}, bf16[512,512]{1,0:T(8,128)(2,1)}, u32[]{:S(2)}, u32[]{:S(2)}) collective-permute-start(bf16[512,512]{1,0:T(8,128)(2,1)S(1)} %collective-permute-done.6.refs_3_), channel_id=1, source_target_pairs={{0,1},{1,0},{2,3},{3,2},{4,5},{5,4},{6,7},{7,6},{8,9},{9,8},{10,11... | collective-permute-start | bytes 1572872 | tf_op jit(solution)/shard_map/ppermute | solution.py:362
  69.1 0.8 copy-start.3
  70.0 1.8 %copy-start.16 = (bf16[512,512]{1,0:T(8,128)(2,1)}, bf16[512,512]{1,0:T(8,128)(2,1)S(1)}, u32[]{:S(2)}) copy-start(bf16[512,512]{1,0:T(8,128)(2,1)S(1)} %collective-permute-done.3.refs_4_) | copy-start | bytes 1572868
  70.2 1.5 copy-start.17
  71.8 0.8 copy-start.18
  72.6 10.9 %collective-permute-start.12 = (bf16[512,2048]{1,0:T(8,128)(2,1)S(1)}, bf16[512,2048]{1,0:T(8,128)(2,1)S(1)}, u32[]{:S(2)}, u32[]{:S(2)}) collective-permute-start(bf16[512,2048]{1,0:T(8,128)(2,1)S(1)} %bitcast.14), channel_id=1, source_target_pairs={{0,1},{1,0},{2,3},{3,2},{4,5},{5,4},{6,7},{7,6},{8,9},{9,8},{10,11... | collective-permute-start | bytes 6291464 | tf_op jit(solution)/shard_map/ppermute | solution.py:362
  72.7 9.2 %collective-permute-start.13 = (bf16[128,512]{1,0:T(8,128)(2,1)S(1)}, bf16[128,512]{1,0:T(8,128)(2,1)S(1)}, u32[]{:S(2)}, u32[]{:S(2)}) collective-permute-start(bf16[128,512]{1,0:T(8,128)(2,1)S(1)} %get-tuple-element.58), channel_id=1, source_target_pairs={{0,6},{1,7},{2,0},{3,1},{4,2},{5,3},{6,4},{7,5},{8,14},{9,15},{10,... | collective-permute-start | bytes 393224 | tf_op jit(solution)/shard_map/ppermute | solution.py:357
  73.7 8.3 %collective-permute-start.14 = (bf16[128,512]{1,0:T(8,128)(2,1)S(1)}, bf16[128,512]{1,0:T(8,128)(2,1)S(1)}, u32[]{:S(2)}, u32[]{:S(2)}) collective-permute-start(bf16[128,512]{1,0:T(8,128)(2,1)S(1)} %get-tuple-element.59), channel_id=1, source_target_pairs={{0,4},{1,5},{2,6},{3,7},{4,0},{5,1},{6,2},{7,3},{8,12},{9,13},{10,... | collective-permute-start | bytes 393224 | tf_op jit(solution)/shard_map/ppermute | solution.py:357
  74.0 9.5 %collective-permute-start.15 = (bf16[128,512]{1,0:T(8,128)(2,1)S(1)}, bf16[128,512]{1,0:T(8,128)(2,1)S(1)}, u32[]{:S(2)}, u32[]{:S(2)}) collective-permute-start(bf16[128,512]{1,0:T(8,128)(2,1)S(1)} %get-tuple-element.60), channel_id=1, source_target_pairs={{0,2},{1,3},{2,4},{3,5},{4,6},{5,7},{6,0},{7,1},{8,10},{9,11},{10,... | collective-permute-start | bytes 393224 | tf_op jit(solution)/shard_map/ppermute | solution.py:357
  89.9 7.0 %collective-permute-start.16 = (bf16[512,2048]{1,0:T(8,128)(2,1)S(1)}, bf16[512,2048]{1,0:T(8,128)(2,1)S(1)}, u32[]{:S(2)}, u32[]{:S(2)}) collective-permute-start(bf16[512,2048]{1,0:T(8,128)(2,1)S(1)} %get-tuple-element.67), channel_id=1, source_target_pairs={{0,1},{1,0},{2,3},{3,2},{4,5},{5,4},{6,7},{7,6},{8,9},{9,8},{10,11... | collective-permute-start | bytes 6291464 | tf_op jit(solution)/shard_map/ppermute | solution.py:362
  96.4 9.6 %collective-permute-start.20 = (bf16[512,2048]{1,0:T(8,128)(2,1)}, bf16[512,2048]{1,0:T(8,128)(2,1)}, u32[]{:S(2)}, u32[]{:S(2)}) collective-permute-start(bf16[512,2048]{1,0:T(8,128)(2,1)} %get-tuple-element.73), channel_id=1, source_target_pairs={{0,1},{1,0},{2,3},{3,2},{4,5},{5,4},{6,7},{7,6},{8,9},{9,8},{10,11... | collective-permute-start | bytes 6291464 | tf_op jit(solution)/shard_map/ppermute | solution.py:362
  98.8 34.7 %all-to-all-start.2 = ((bf16[16,32,2048]{2,1,0:T(8,128)(2,1)}), bf16[16,32,2048]{2,1,0:T(8,128)(2,1)S(1)}, u32[]{:S(2)}, u32[]{:S(2)}) async-start(bf16[16,32,2048]{2,1,0:T(8,128)(2,1)} %bitcast.9), calls=%async_computation.2 | async-start | bytes 4194304 | tf_op jit(solution)/shard_map/all_to_all | solution.py:365
  106.0 27.5 %copy-start.7 = (f32[128,2]{0,1:T(2,128)S(1)}, f32[128,2]{0,1:T(2,128)}, u32[]{:S(2)}) copy-start(f32[128,2]{0,1:T(2,128)} %param.12) | copy-start | bytes 3076
  110.7 0.8 copy-start.4
  111.5 27.3 %copy-start.5 = (bf16[512,512]{1,0:T(8,128)(2,1)S(1)}, bf16[512,512]{1,0:T(8,128)(2,1)}, u32[]{:S(2)}) copy-start(bf16[512,512]{1,0:T(8,128)(2,1)} %copy-done.4) | copy-start | bytes 1572868
  111.5 25.0 %collective-permute-start.21 = (bf16[512,512]{1,0:T(8,128)(2,1)}, bf16[512,512]{1,0:T(8,128)(2,1)}, u32[]{:S(2)}, u32[]{:S(2)}) collective-permute-start(bf16[512,512]{1,0:T(8,128)(2,1)} %get-tuple-element.75), channel_id=1, source_target_pairs={{0,6},{1,7},{2,0},{3,1},{4,2},{5,3},{6,4},{7,5},{8,14},{9,15},{10,... | collective-permute-start | bytes 1572872 | tf_op jit(solution)/shard_map/ppermute | solution.py:357
  112.7 23.8 %collective-permute-start.22 = (bf16[512,512]{1,0:T(8,128)(2,1)}, bf16[512,512]{1,0:T(8,128)(2,1)}, u32[]{:S(2)}, u32[]{:S(2)}) collective-permute-start(bf16[512,512]{1,0:T(8,128)(2,1)} %get-tuple-element.76), channel_id=1, source_target_pairs={{0,4},{1,5},{2,6},{3,7},{4,0},{5,1},{6,2},{7,3},{8,12},{9,13},{10,... | collective-permute-start | bytes 1572872 | tf_op jit(solution)/shard_map/ppermute | solution.py:357
  114.5 24.3 %collective-permute-start.23 = (bf16[512,512]{1,0:T(8,128)(2,1)}, bf16[512,512]{1,0:T(8,128)(2,1)}, u32[]{:S(2)}, u32[]{:S(2)}) collective-permute-start(bf16[512,512]{1,0:T(8,128)(2,1)} %get-tuple-element.77), channel_id=1, source_target_pairs={{0,2},{1,3},{2,4},{3,5},{4,6},{5,7},{6,0},{7,1},{8,10},{9,11},{10,... | collective-permute-start | bytes 1572872 | tf_op jit(solution)/shard_map/ppermute | solution.py:357
  136.3 5.0 %copy-start.10 = (bf16[128,512]{1,0:T(8,128)(2,1)}, bf16[128,512]{1,0:T(8,128)(2,1)S(1)}, u32[]{:S(2)}) copy-start(bf16[128,512]{1,0:T(8,128)(2,1)S(1)} %get-tuple-element.71) | copy-start | bytes 393220
  136.4 5.0 %copy-start.11 = (bf16[128,512]{1,0:T(8,128)(2,1)}, bf16[128,512]{1,0:T(8,128)(2,1)S(1)}, u32[]{:S(2)}) copy-start(bf16[128,512]{1,0:T(8,128)(2,1)S(1)} %get-tuple-element.70) | copy-start | bytes 393220
  136.4 12.2 %collective-permute-start.24 = (f32[128,2]{1,0:T(8,128)S(1)}, f32[128,2]{1,0:T(8,128)S(1)}, u32[]{:S(2)}, u32[]{:S(2)}) collective-permute-start(f32[128,2]{1,0:T(8,128)S(1)} %bitcast.24), channel_id=1, source_target_pairs={{0,1},{1,0},{2,3},{3,2},{4,5},{5,4},{6,7},{7,6},{8,9},{9,8},{10,11... | collective-permute-start | bytes 3080 | tf_op jit(solution)/shard_map/ppermute | solution.py:362
  138.8 24.4 %copy-start.2 = (bf16[256,512]{1,0:T(8,128)(2,1)S(1)}, bf16[256,512]{1,0:T(8,128)(2,1)}, u32[]{:S(2)}) copy-start(bf16[256,512]{1,0:T(8,128)(2,1)} %copy-done.1) | copy-start | bytes 786436
  141.3 21.8 %all-to-all-start.3 = ((bf16[16,32,512]{2,1,0:T(8,128)(2,1)}), bf16[16,32,512]{2,1,0:T(8,128)(2,1)S(1)}, u32[]{:S(2)}, u32[]{:S(2)}) async-start(bf16[16,32,512]{2,1,0:T(8,128)(2,1)} %bitcast.11), calls=%async_computation.3 | async-start | bytes 1048576 | tf_op jit(solution)/shard_map/all_to_all | solution.py:365
  148.6 6.2 %collective-permute-start.27 = (f32[128,2]{1,0:T(8,128)S(1)}, f32[128,2]{1,0:T(8,128)S(1)}, u32[]{:S(2)}, u32[]{:S(2)}) collective-permute-start(f32[128,2]{1,0:T(8,128)S(1)} %slice_add_fusion), channel_id=1, source_target_pairs={{0,6},{1,7},{2,0},{3,1},{4,2},{5,3},{6,4},{7,5},{8,14},{9,15},{10,... | collective-permute-start | bytes 3080 | tf_op jit(solution)/shard_map/ppermute | solution.py:357
  149.3 7.0 %collective-permute-start.26 = (f32[128,2]{1,0:T(8,128)S(1)}, f32[128,2]{1,0:T(8,128)S(1)}, u32[]{:S(2)}, u32[]{:S(2)}) collective-permute-start(f32[128,2]{1,0:T(8,128)S(1)} %slice_add_fusion), channel_id=1, source_target_pairs={{0,4},{1,5},{2,6},{3,7},{4,0},{5,1},{6,2},{7,3},{8,12},{9,13},{10,... | collective-permute-start | bytes 3080 | tf_op jit(solution)/shard_map/ppermute | solution.py:357
  151.0 5.5 %collective-permute-start.25 = (f32[128,2]{1,0:T(8,128)S(1)}, f32[128,2]{1,0:T(8,128)S(1)}, u32[]{:S(2)}, u32[]{:S(2)}) collective-permute-start(f32[128,2]{1,0:T(8,128)S(1)} %slice_add_fusion), channel_id=1, source_target_pairs={{0,2},{1,3},{2,4},{3,5},{4,6},{5,7},{6,0},{7,1},{8,10},{9,11},{10,... | collective-permute-start | bytes 3080 | tf_op jit(solution)/shard_map/ppermute | solution.py:357
  151.8 7.4 %collective-permute-start.17 = (bf16[128,512]{1,0:T(8,128)(2,1)}, bf16[128,512]{1,0:T(8,128)(2,1)S(1)}, u32[]{:S(2)}, u32[]{:S(2)}) collective-permute-start(bf16[128,512]{1,0:T(8,128)(2,1)} %copy-done.11), channel_id=1, source_target_pairs={{0,6},{1,7},{2,0},{3,1},{4,2},{5,3},{6,4},{7,5},{8,14},{9,15},{10,... | collective-permute-start | bytes 393224 | tf_op jit(solution)/shard_map/ppermute | solution.py:357
  154.3 7.1 %collective-permute-start.18 = (bf16[128,512]{1,0:T(8,128)(2,1)}, bf16[128,512]{1,0:T(8,128)(2,1)S(1)}, u32[]{:S(2)}, u32[]{:S(2)}) collective-permute-start(bf16[128,512]{1,0:T(8,128)(2,1)} %copy-done.10), channel_id=1, source_target_pairs={{0,4},{1,5},{2,6},{3,7},{4,0},{5,1},{6,2},{7,3},{8,12},{9,13},{10,... | collective-permute-start | bytes 393224 | tf_op jit(solution)/shard_map/ppermute | solution.py:357
  154.8 7.6 %collective-permute-start.19 = (bf16[128,512]{1,0:T(8,128)(2,1)S(1)}, bf16[128,512]{1,0:T(8,128)(2,1)S(1)}, u32[]{:S(2)}, u32[]{:S(2)}) collective-permute-start(bf16[128,512]{1,0:T(8,128)(2,1)S(1)} %get-tuple-element.72), channel_id=1, source_target_pairs={{0,2},{1,3},{2,4},{3,5},{4,6},{5,7},{6,0},{7,1},{8,10},{9,11},{10,... | collective-permute-start | bytes 393224 | tf_op jit(solution)/shard_map/ppermute | solution.py:357

commit v4 on v3

--- a/solution.py
+++ b/solution.py
@@ -374,7 +374,7 @@
         [((2 * rows, slots), BF16), ((slots, width), BF16), ((2 * rows, width), BF16)],
         12,
         2 * 2 * rows * slots * width,
-        (routes.T, gates.T, tokens, cotangent),
+        (pin(routes.T), pin(gates.T), pin(tokens), pin(cotangent)),
         "plan",
         far_args=range(4),
         scratch=[pltpu.VMEM((2, rows), jnp.int32), pltpu.VMEM((2, rows), F32), sems((4,))],

time: 165 us -> 162 us (0.982)
  local copies, waits for them, and re-layouts: 6.28 us -> 3.11 us
    unnamed x39 -> x31, local copies, waits for them, and re-layouts: 6.28 us -> 3.11 us
  transfers between devices with their start and end apart: 32 -> 32, of which waited for: 15 -> 15; matrix products, arithmetic and copies ran while one was open for 1% -> 1% of each run, Pallas kernels for 21% -> 22%
where the time goes in v4:
time: 162 us; the launch traced here: 161 us
  waiting for transfers between devices  56.5 us (35%)
  starting transfers between devices  52.5 us (32%)
  Pallas kernels  47.4 us (29%)
  local copies, waits for them, and re-layouts  3.11 us (2%)
    pallas_call x12, Pallas kernels, call(): pl.pallas_call(kernel, out_shape=[pltpu.HBM(*o) if far_out and i == 0 els...  47.4 us
    ppermute x18, waiting for transfers between devices, along(): lax.ppermute(v, 'tensor', [(i, (i + 2 * d) % devices) for i in range(devi...  36.8 us
    all_to_all x4, starting transfers between devices, spread(): return lax.all_to_all(v, 'dp', split_axis=0, concat_axis=0, tiled=True)  30 us
    ppermute x18, starting transfers between devices, along(): lax.ppermute(v, 'tensor', [(i, (i + 2 * d) % devices) for i in range(devi...  20.4 us
    all_to_all x4, waiting for transfers between devices, spread(): return lax.all_to_all(v, 'dp', split_axis=0, concat_axis=0, tiled=True)  17.9 us
  transfers between devices with their start and end apart: 32, of which 15 were waited for; matrix products, arithmetic and copies ran while one was open for 1% of the time, Pallas kernels for 22%

profile of v4, /device:TPU:2, one launch (start us, length us, event | category | flops | bytes accessed | tf_op | source)
XLA Modules:
  0.0 161.2 jit_solution(12582017983950876202)
XLA Ops:
  0.6 2.4 %plan.1 = (bf16[256,512]{1,0:T(8,128)(2,1)S(1)}, bf16[512,512]{1,0:T(8,128)(2,1)}, bf16[256,512]{1,0:T(8,128)(2,1)S(1)}) custom-call(s32[2,128]{1,0:T(2,128)} %bitcast.39, f32[2,128]{1,0:T(2,128)} %bitcast.25, bf16[128,512]{1,0:T(8,128)(2,1)} %tokens.1, bf16[128,512]{1,0:T(8,128)(2,1)} %cotangent.1), custom_call_target="tpu_custom_call" | custom-call | flops 134217728 | bytes 264192 | tf_op jit(solution)/shard_map/plan/pallas_call | solution.py:321
  3.0 8.3 %all-to-all-start = ((bf16[16,32,512]{2,1,0:T(8,128)(2,1)}), bf16[16,32,512]{2,1,0:T(8,128)(2,1)S(1)}, u32[]{:S(2)}, u32[]{:S(2)}) async-start(bf16[16,32,512]{2,1,0:T(8,128)(2,1)} %bitcast.2), calls=%async_computation | async-start | bytes 1048576 | tf_op jit(solution)/shard_map/all_to_all | solution.py:365
  11.4 3.0 %collective-permute-start.2 = (bf16[256,512]{1,0:T(8,128)(2,1)S(1)}, bf16[256,512]{1,0:T(8,128)(2,1)S(1)}, u32[]{:S(2)}, u32[]{:S(2)}) collective-permute-start(bf16[256,512]{1,0:T(8,128)(2,1)S(1)} %get-tuple-element.44.p0), channel_id=1, source_target_pairs={{0,6},{1,7},{2,0},{3,1},{4,2},{5,3},{6,4},{7,5},{8,14},{9,15},{10,... | collective-permute-start | bytes 786440 | tf_op jit(solution)/shard_map/ppermute | solution.py:357
  14.4 0.6 collective-permute-start.1
  15.0 1.0 collective-permute-start
  16.0 9.0 %collective-permute-done.2.p3 = bf16[256,512]{1,0:T(8,128)(2,1)S(1)} collective-permute-done((bf16[256,512]{1,0:T(8,128)(2,1)S(1)}, bf16[256,512]{1,0:T(8,128)(2,1)S(1)}, u32[]{:S(2)}, u32[]{:S(2)}) %collective-permute-start.2) | collective-permute-done | bytes 262176 | tf_op jit(solution)/shard_map/ppermute | solution.py:357
  25.0 0.1 collective-permute-done.1.p2
  25.1 3.6 %collective-permute-done.p1 = bf16[256,512]{1,0:T(8,128)(2,1)S(1)} collective-permute-done((bf16[256,512]{1,0:T(8,128)(2,1)S(1)}, bf16[256,512]{1,0:T(8,128)(2,1)S(1)}, u32[]{:S(2)}, u32[]{:S(2)}) %collective-permute-start) | collective-permute-done | bytes 262176 | tf_op jit(solution)/shard_map/ppermute | solution.py:357
  28.7 2.7 %rows.1 = (bf16[512,2048]{1,0:T(8,128)(2,1)}, bf16[4,256,512]{2,1,0:T(8,128)(2,1)}) custom-call(bf16[256,512]{1,0:T(8,128)(2,1)S(1)} %get-tuple-element.41.pick_ref.pick, bf16[256,512]{1,0:T(8,128)(2,1)S(1)} %get-tuple-element.44.p0, bf16[256,512]{1,0:T(8,128)(2,1)S(1)} %collective-permute-done.p1, bf16[256,512]{1,0:T(8,128)(2,1)S(1)} %collective-permute-done.1.p2, ...), custom_call_target="tpu_custom_call" | custom-call | flops 268435456 | bytes 1835008 | tf_op jit(solution)/shard_map/rows/pallas_call | solution.py:321
  31.4 0.1 collective-permute-start.7
  31.5 7.2 %all-to-all-start.1 = ((bf16[16,32,2048]{2,1,0:T(8,128)(2,1)}), bf16[16,32,2048]{2,1,0:T(8,128)(2,1)S(1)}, u32[]{:S(2)}, u32[]{:S(2)}) async-start(bf16[16,32,2048]{2,1,0:T(8,128)(2,1)} %bitcast.38), calls=%async_computation.1 | async-start | bytes 4194304 | tf_op jit(solution)/shard_map/all_to_all | solution.py:365
  38.8 0.6 collective-permute-start.6
  39.4 0.6 collective-permute-start.5
  40.0 0.8 collective-permute-start.4
  40.8 9.4 %dense.1 = (bf16[256,2048]{1,0:T(8,128)(2,1)S(1)}, bf16[256,2048]{1,0:T(8,128)(2,1)S(1)}) custom-call(bf16[4,256,512]{2,1,0:T(8,128)(2,1)} %get-tuple-element.50.refs_0_.pack, bf16[4,256,512]{2,1,0:T(8,128)(2,1)} %collective-permute-done.7.refs_1_, bf16[4096,512]{1,0:T(8,128)(2,1)} %refs_2_.1, bf16[4096,512]{1,0:T(8,128)(2,1)} %refs_3_.1, ...), custom_call_target="tpu_custom_call" | custom-call | flops 3221225472 | bytes 14680064 | tf_op jit(solution)/shard_map/dense/pallas_call | solution.py:321
  50.2 0.1 collective-permute-start.11
  50.3 0.5 collective-permute-start.3
  50.8 2.8 %collective-permute-done.6.refs_3_ = bf16[512,512]{1,0:T(8,128)(2,1)S(1)} collective-permute-done((bf16[512,512]{1,0:T(8,128)(2,1)S(1)}, bf16[512,512]{1,0:T(8,128)(2,1)S(1)}, u32[]{:S(2)}, u32[]{:S(2)}) %collective-permute-start.6) | collective-permute-done | bytes 524320 | tf_op jit(solution)/shard_map/ppermute | solution.py:357
  53.6 2.2 %collective-permute-done.5.refs_2_ = bf16[512,512]{1,0:T(8,128)(2,1)S(1)} collective-permute-done((bf16[512,512]{1,0:T(8,128)(2,1)S(1)}, bf16[512,512]{1,0:T(8,128)(2,1)S(1)}, u32[]{:S(2)}, u32[]{:S(2)}) %collective-permute-start.5) | collective-permute-done | bytes 524320 | tf_op jit(solution)/shard_map/ppermute | solution.py:357
  55.8 9.8 %collective-permute-done.4.refs_1_ = bf16[512,512]{1,0:T(8,128)(2,1)S(1)} collective-permute-done((bf16[512,512]{1,0:T(8,128)(2,1)S(1)}, bf16[512,512]{1,0:T(8,128)(2,1)S(1)}, u32[]{:S(2)}, u32[]{:S(2)}) %collective-permute-start.4) | collective-permute-done | bytes 524320 | tf_op jit(solution)/shard_map/ppermute | solution.py:357
  65.6 0.0 collective-permute-start.8
  65.6 0.5 collective-permute-start.9
  66.1 0.0 collective-permute-start.10
  66.1 0.2 dense_sum.1
  66.4 0.8 copy-done.3
  67.2 0.3 collective-permute-done.8.refs_5_
  67.5 1.5 collective-permute-done.9.refs_6_
  69.0 0.8 copy-done.14
  69.8 0.1 collective-permute-start.12
  70.0 0.9 collective-permute-start.13
  70.9 0.3 collective-permute-start.14
  71.2 0.8 collective-permute-start.15
  72.0 7.1 %early.1 = (f32[512,384]{1,0:T(8,128)S(1)}, f32[512,768]{1,0:T(8,128)S(1)}) custom-call(bf16[512,512]{1,0:T(8,128)(2,1)} %bitcast.22, bf16[512,512]{1,0:T(8,128)(2,1)} %copy-done.11, bf16[512,512]{1,0:T(8,128)(2,1)} %copy-done.10, bf16[512,512]{1,0:T(8,128)(2,1)} %copy-done.9, bf16[512,512]{1,0:T(8,128)(2,1)} %copy-done.12, bf16[512,512]{1,0:T(8,128)(2,1)} %copy-done.13, ...), custom_call_target="tpu_custom_call" | custom-call | flops 3221225472 | bytes 15728640 | tf_op jit(solution)/shard_map/early/pallas_call | solution.py:321
  79.2 1.5 collective-permute-done.15.a3.d3
  80.7 6.4 %forth.1 = (bf16[512,2048]{1,0:T(8,128)(2,1)S(1)}, bf16[512,384]{1,0:T(8,128)(2,1)S(1)}, bf16[512,768]{1,0:T(8,128)(2,1)S(1)}) custom-call(bf16[512,2048]{1,0:T(8,128)(2,1)S(1)} %collective-permute-done.12.x, f32[512,768]{1,0:T(8,128)S(1)} %get-tuple-element.62.part, f32[512,384]{1,0:T(8,128)S(1)} %get-tuple-element.63.g_ref, bf16[4096,384]{1,0:T(8,128)(2,1)} %bitcast.28, ...), custom_call_target="tpu_custom_call" | custom-call | flops 2415919104 | bytes 14286848 | tf_op jit(solution)/shard_map/forth/pallas_call | solution.py:321
  87.1 0.1 collective-permute-start.16
  87.2 6.3 %cross.1 = (bf16[512,2048]{1,0:T(8,128)(2,1)S(1)}, bf16[512,2048]{1,0:T(8,128)(2,1)}) custom-call(bf16[512,384]{1,0:T(8,128)(2,1)S(1)} %get-tuple-element.64.hid_ref, bf16[512,768]{1,0:T(8,128)(2,1)S(1)} %get-tuple-element.65.dadu_ref, bf16[4096,384]{1,0:T(8,128)(2,1)} %bitcast.29, bf16[4096,384]{1,0:T(8,128)(2,1)} %bitcast.33, bf16[384,4096]{1,0:T(8,128)(2,1)} %bitcast.37), custom_call_target="tpu_custom_call" | custom-call | flops 2415919104 | bytes 10616832 | tf_op jit(solution)/shard_map/cross/pallas_call | solution.py:321
  93.6 0.5 collective-permute-start.20
  94.1 1.8 %add.36 = bf16[512,2048]{1,0:T(8,128)(2,1)} custom-call(bf16[512,2048]{1,0:T(8,128)(2,1)S(1)} %get-tuple-element.66.mine, bf16[512,2048]{1,0:T(8,128)(2,1)S(1)} %collective-permute-done.16.got), custom_call_target="tpu_custom_call" | custom-call | flops 1048576 | bytes 4194304 | tf_op jit(solution)/shard_map/add/pallas_call | solution.py:321
  96.0 7.2 %all-to-all-start.2 = ((bf16[16,32,2048]{2,1,0:T(8,128)(2,1)}), bf16[16,32,2048]{2,1,0:T(8,128)(2,1)S(1)}, u32[]{:S(2)}, u32[]{:S(2)}) async-start(bf16[16,32,2048]{2,1,0:T(8,128)(2,1)} %bitcast.9), calls=%async_computation.2 | async-start | bytes 4194304 | tf_op jit(solution)/shard_map/all_to_all | solution.py:365
  103.2 4.7 %down.1 = (bf16[512,512]{1,0:T(8,128)(2,1)S(1)}, bf16[512,512]{1,0:T(8,128)(2,1)}, bf16[512,512]{1,0:T(8,128)(2,1)}, bf16[512,512]{1,0:T(8,128)(2,1)}) custom-call(bf16[512,768]{1,0:T(8,128)(2,1)S(1)} %get-tuple-element.65.dadu_ref, bf16[4096,384]{1,0:T(8,128)(2,1)} %bitcast.30, bf16[4096,384]{1,0:T(8,128)(2,1)} %bitcast.34, ...), custom_call_target="tpu_custom_call" | custom-call | flops 1610612736 | bytes 9175040 | tf_op jit(solution)/shard_map/down/pallas_call | solution.py:321
  107.9 0.8 copy-done.4
  108.7 1.2 collective-permute-start.21
  109.9 1.8 %collective-permute-start.22 = (bf16[512,512]{1,0:T(8,128)(2,1)}, bf16[512,512]{1,0:T(8,128)(2,1)}, u32[]{:S(2)}, u32[]{:S(2)}) collective-permute-start(bf16[512,512]{1,0:T(8,128)(2,1)} %get-tuple-element.76), channel_id=1, source_target_pairs={{0,4},{1,5},{2,6},{3,7},{4,0},{5,1},{6,2},{7,3},{8,12},{9,13},{10,... | collective-permute-start | bytes 1572872 | tf_op jit(solution)/shard_map/ppermute | solution.py:357
  111.7 1.1 collective-permute-start.23
  112.8 17.9 %all-to-all-done.2 = bf16[16,32,2048]{2,1,0:T(8,128)(2,1)S(1)} async-done(((bf16[16,32,2048]{2,1,0:T(8,128)(2,1)}), bf16[16,32,2048]{2,1,0:T(8,128)(2,1)S(1)}, u32[]{:S(2)}, u32[]{:S(2)}) %all-to-all-start.2) | async-done | bytes 2097184 | tf_op jit(solution)/shard_map/all_to_all | solution.py:365
  130.7 2.9 %mix.1 = (bf16[128,512]{1,0:T(8,128)(2,1)S(1)}, bf16[128,512]{1,0:T(8,128)(2,1)S(1)}, bf16[128,512]{1,0:T(8,128)(2,1)S(1)}, bf16[128,512]{1,0:T(8,128)(2,1)S(1)}, f32[128,128]{1,0:T(8,128)S(1)}) custom-call(bf16[512,2048]{1,0:T(8,128)(2,1)S(1)} %bitcast.16, bf16[256,512]{1,0:T(8,128)(2,1)} %copy-done.1, f32[2,128]{1,0:T(2,128)S(1)} %bitcast.26, ...), custom_call_target="tpu_custom_call" | custom-call | flops 536870912 | bytes 3933184 | tf_op jit(solution)/shard_map/mix/pallas_call | solution.py:321
  133.6 0.1 collective-permute-start.24
  133.7 2.3 %collective-permute-done.23.p3 = bf16[512,512]{1,0:T(8,128)(2,1)} collective-permute-done((bf16[512,512]{1,0:T(8,128)(2,1)}, bf16[512,512]{1,0:T(8,128)(2,1)}, u32[]{:S(2)}, u32[]{:S(2)}) %collective-permute-start.23) | collective-permute-done | bytes 524320 | tf_op jit(solution)/shard_map/ppermute | solution.py:357
  136.0 2.5 %sum.1 = bf16[512,512]{1,0:T(8,128)(2,1)} custom-call(bf16[512,512]{1,0:T(8,128)(2,1)S(1)} %copy-done.5, bf16[512,512]{1,0:T(8,128)(2,1)} %collective-permute-done.21.p1, bf16[512,512]{1,0:T(8,128)(2,1)} %collective-permute-done.22.p2, bf16[512,512]{1,0:T(8,128)(2,1)} %collective-permute-done.23.p3, f32[128,128]{1,0:T(8,128)S(1)} %get-tuple-element.78.after), custom_call_target="tpu_custom_call" | custom-call | flops 786432 | bytes 2162688 | tf_op jit(solution)/shard_map/sum/pallas_call | solution.py:321
  138.5 7.2 %all-to-all-start.3 = ((bf16[16,32,512]{2,1,0:T(8,128)(2,1)}), bf16[16,32,512]{2,1,0:T(8,128)(2,1)S(1)}, u32[]{:S(2)}, u32[]{:S(2)}) async-start(bf16[16,32,512]{2,1,0:T(8,128)(2,1)} %bitcast.11), calls=%async_computation.3 | async-start | bytes 1048576 | tf_op jit(solution)/shard_map/all_to_all | solution.py:365
  145.8 0.7 collective-permute-start.27
  146.5 1.8 %collective-permute-start.26 = (f32[128,2]{1,0:T(8,128)S(1)}, f32[128,2]{1,0:T(8,128)S(1)}, u32[]{:S(2)}, u32[]{:S(2)}) collective-permute-start(f32[128,2]{1,0:T(8,128)S(1)} %slice_add_fusion), channel_id=1, source_target_pairs={{0,4},{1,5},{2,6},{3,7},{4,0},{5,1},{6,2},{7,3},{8,12},{9,13},{10,... | collective-permute-start | bytes 3080 | tf_op jit(solution)/shard_map/ppermute | solution.py:357
  148.2 0.8 collective-permute-start.25
  149.0 2.4 %collective-permute-start.17 = (bf16[128,512]{1,0:T(8,128)(2,1)}, bf16[128,512]{1,0:T(8,128)(2,1)S(1)}, u32[]{:S(2)}, u32[]{:S(2)}) collective-permute-start(bf16[128,512]{1,0:T(8,128)(2,1)} %copy-done.8), channel_id=1, source_target_pairs={{0,6},{1,7},{2,0},{3,1},{4,2},{5,3},{6,4},{7,5},{8,14},{9,15},{10,... | collective-permute-start | bytes 393224 | tf_op jit(solution)/shard_map/ppermute | solution.py:357
  151.5 0.5 collective-permute-start.18
  152.0 1.4 collective-permute-start.19
  153.4 0.3 collective-permute-done.25
  153.7 0.6 copy.13
  154.4 2.0 %collective-permute-done.17 = bf16[128,512]{1,0:T(8,128)(2,1)S(1)} collective-permute-done((bf16[128,512]{1,0:T(8,128)(2,1)}, bf16[128,512]{1,0:T(8,128)(2,1)S(1)}, u32[]{:S(2)}, u32[]{:S(2)}) %collective-permute-start.17) | collective-permute-done | bytes 131104 | tf_op jit(solution)/shard_map/ppermute | solution.py:357
  156.4 2.2 %collective-permute-done.18 = bf16[128,512]{1,0:T(8,128)(2,1)S(1)} collective-permute-done((bf16[128,512]{1,0:T(8,128)(2,1)}, bf16[128,512]{1,0:T(8,128)(2,1)S(1)}, u32[]{:S(2)}, u32[]{:S(2)}) %collective-permute-start.18) | collective-permute-done | bytes 131104 | tf_op jit(solution)/shard_map/ppermute | solution.py:357
  158.6 1.0 collective-permute-done.19
  159.6 0.7 add_convert_fusion
  160.3 0.9 grad.1
  (46 shorter events, 0.1 us)
Async XLA Ops:
  3.0 28.5 %copy-start.1 = (bf16[256,512]{1,0:T(8,128)(2,1)}, bf16[256,512]{1,0:T(8,128)(2,1)S(1)}, u32[]{:S(2)}) copy-start(bf16[256,512]{1,0:T(8,128)(2,1)S(1)} %get-tuple-element.41.pick_ref.pick) | copy-start | bytes 786436
  3.0 25.7 %all-to-all-start = ((bf16[16,32,512]{2,1,0:T(8,128)(2,1)}), bf16[16,32,512]{2,1,0:T(8,128)(2,1)S(1)}, u32[]{:S(2)}, u32[]{:S(2)}) async-start(bf16[16,32,512]{2,1,0:T(8,128)(2,1)} %bitcast.2), calls=%async_computation | async-start | bytes 1048576 | tf_op jit(solution)/shard_map/all_to_all | solution.py:365
  11.4 13.6 %collective-permute-start.2 = (bf16[256,512]{1,0:T(8,128)(2,1)S(1)}, bf16[256,512]{1,0:T(8,128)(2,1)S(1)}, u32[]{:S(2)}, u32[]{:S(2)}) collective-permute-start(bf16[256,512]{1,0:T(8,128)(2,1)S(1)} %get-tuple-element.44.p0), channel_id=1, source_target_pairs={{0,6},{1,7},{2,0},{3,1},{4,2},{5,3},{6,4},{7,5},{8,14},{9,15},{10,... | collective-permute-start | bytes 786440 | tf_op jit(solution)/shard_map/ppermute | solution.py:357
  14.4 10.8 %collective-permute-start.1 = (bf16[256,512]{1,0:T(8,128)(2,1)S(1)}, bf16[256,512]{1,0:T(8,128)(2,1)S(1)}, u32[]{:S(2)}, u32[]{:S(2)}) collective-permute-start(bf16[256,512]{1,0:T(8,128)(2,1)S(1)} %get-tuple-element.44.p0), channel_id=1, source_target_pairs={{0,4},{1,5},{2,6},{3,7},{4,0},{5,1},{6,2},{7,3},{8,12},{9,13},{10,... | collective-permute-start | bytes 786440 | tf_op jit(solution)/shard_map/ppermute | solution.py:357
  15.0 13.7 %collective-permute-start = (bf16[256,512]{1,0:T(8,128)(2,1)S(1)}, bf16[256,512]{1,0:T(8,128)(2,1)S(1)}, u32[]{:S(2)}, u32[]{:S(2)}) collective-permute-start(bf16[256,512]{1,0:T(8,128)(2,1)S(1)} %get-tuple-element.44.p0), channel_id=1, source_target_pairs={{0,2},{1,3},{2,4},{3,5},{4,6},{5,7},{6,0},{7,1},{8,10},{9,11},{10,... | collective-permute-start | bytes 786440 | tf_op jit(solution)/shard_map/ppermute | solution.py:357
  28.7 21.6 %copy-start = (bf16[16,32,512]{2,1,0:T(8,128)(2,1)}, bf16[16,32,512]{2,1,0:T(8,128)(2,1)S(1)}, u32[]{:S(2)}) copy-start(bf16[16,32,512]{2,1,0:T(8,128)(2,1)S(1)} %all-to-all-done) | copy-start | bytes 1572868
  31.4 9.4 %collective-permute-start.7 = (bf16[4,256,512]{2,1,0:T(8,128)(2,1)}, bf16[4,256,512]{2,1,0:T(8,128)(2,1)}, u32[]{:S(2)}, u32[]{:S(2)}) collective-permute-start(bf16[4,256,512]{2,1,0:T(8,128)(2,1)} %get-tuple-element.50.refs_0_.pack), channel_id=1, source_target_pairs={{0,1},{1,0},{2,3},{3,2},{4,5},{5,4},{6,7},{7,6},{8,9},{9,8},{10,11... | collective-permute-start | bytes 3145736 | tf_op jit(solution)/shard_map/ppermute | solution.py:362
  31.5 38.3 %all-to-all-start.1 = ((bf16[16,32,2048]{2,1,0:T(8,128)(2,1)}), bf16[16,32,2048]{2,1,0:T(8,128)(2,1)S(1)}, u32[]{:S(2)}, u32[]{:S(2)}) async-start(bf16[16,32,2048]{2,1,0:T(8,128)(2,1)} %bitcast.38), calls=%async_computation.1 | async-start | bytes 4194304 | tf_op jit(solution)/shard_map/all_to_all | solution.py:365
  38.8 14.8 %collective-permute-start.6 = (bf16[512,512]{1,0:T(8,128)(2,1)S(1)}, bf16[512,512]{1,0:T(8,128)(2,1)S(1)}, u32[]{:S(2)}, u32[]{:S(2)}) collective-permute-start(bf16[512,512]{1,0:T(8,128)(2,1)S(1)} %bitcast.18), channel_id=1, source_target_pairs={{0,6},{1,7},{2,0},{3,1},{4,2},{5,3},{6,4},{7,5},{8,14},{9,15},{10,... | collective-permute-start | bytes 1572872 | tf_op jit(solution)/shard_map/ppermute | solution.py:357
  39.4 16.4 %collective-permute-start.5 = (bf16[512,512]{1,0:T(8,128)(2,1)S(1)}, bf16[512,512]{1,0:T(8,128)(2,1)S(1)}, u32[]{:S(2)}, u32[]{:S(2)}) collective-permute-start(bf16[512,512]{1,0:T(8,128)(2,1)S(1)} %bitcast.19), channel_id=1, source_target_pairs={{0,4},{1,5},{2,6},{3,7},{4,0},{5,1},{6,2},{7,3},{8,12},{9,13},{10,... | collective-permute-start | bytes 1572872 | tf_op jit(solution)/shard_map/ppermute | solution.py:357
  40.0 25.6 %collective-permute-start.4 = (bf16[512,512]{1,0:T(8,128)(2,1)S(1)}, bf16[512,512]{1,0:T(8,128)(2,1)S(1)}, u32[]{:S(2)}, u32[]{:S(2)}) collective-permute-start(bf16[512,512]{1,0:T(8,128)(2,1)S(1)} %bitcast.20), channel_id=1, source_target_pairs={{0,2},{1,3},{2,4},{3,5},{4,6},{5,7},{6,0},{7,1},{8,10},{9,11},{10,... | collective-permute-start | bytes 1572872 | tf_op jit(solution)/shard_map/ppermute | solution.py:357
  50.2 15.9 %collective-permute-start.11 = (bf16[256,2048]{1,0:T(8,128)(2,1)S(1)}, bf16[256,2048]{1,0:T(8,128)(2,1)S(1)}, u32[]{:S(2)}, u32[]{:S(2)}) collective-permute-start(bf16[256,2048]{1,0:T(8,128)(2,1)S(1)} %get-tuple-element.56), channel_id=1, source_target_pairs={{0,1},{1,0},{2,3},{3,2},{4,5},{5,4},{6,7},{7,6},{8,9},{9,8},{10,11... | collective-permute-start | bytes 3145736 | tf_op jit(solution)/shard_map/ppermute | solution.py:362
  50.3 16.9 %collective-permute-start.3 = (bf16[512,512]{1,0:T(8,128)(2,1)S(1)}, bf16[512,512]{1,0:T(8,128)(2,1)S(1)}, u32[]{:S(2)}, u32[]{:S(2)}) collective-permute-start(bf16[512,512]{1,0:T(8,128)(2,1)S(1)} %bitcast.21), channel_id=1, source_target_pairs={{0,1},{1,0},{2,3},{3,2},{4,5},{5,4},{6,7},{7,6},{8,9},{9,8},{10,11... | collective-permute-start | bytes 1572872 | tf_op jit(solution)/shard_map/ppermute | solution.py:362
  53.6 15.4 %copy-start.9 = (bf16[512,512]{1,0:T(8,128)(2,1)}, bf16[512,512]{1,0:T(8,128)(2,1)S(1)}, u32[]{:S(2)}) copy-start(bf16[512,512]{1,0:T(8,128)(2,1)S(1)} %collective-permute-done.6.refs_3_) | copy-start | bytes 1572868
  55.8 13.2 %copy-start.10 = (bf16[512,512]{1,0:T(8,128)(2,1)}, bf16[512,512]{1,0:T(8,128)(2,1)S(1)}, u32[]{:S(2)}) copy-start(bf16[512,512]{1,0:T(8,128)(2,1)S(1)} %collective-permute-done.5.refs_2_) | copy-start | bytes 1572868
  65.6 3.4 %copy-start.11 = (bf16[512,512]{1,0:T(8,128)(2,1)}, bf16[512,512]{1,0:T(8,128)(2,1)S(1)}, u32[]{:S(2)}) copy-start(bf16[512,512]{1,0:T(8,128)(2,1)S(1)} %collective-permute-done.4.refs_1_) | copy-start | bytes 1572868
  65.6 1.9 %collective-permute-start.8 = (bf16[512,512]{1,0:T(8,128)(2,1)S(1)}, bf16[512,512]{1,0:T(8,128)(2,1)S(1)}, u32[]{:S(2)}, u32[]{:S(2)}) collective-permute-start(bf16[512,512]{1,0:T(8,128)(2,1)S(1)} %collective-permute-done.4.refs_1_), channel_id=1, source_target_pairs={{0,1},{1,0},{2,3},{3,2},{4,5},{5,4},{6,7},{7,6},{8,9},{9,8},{10,11... | collective-permute-start | bytes 1572872 | tf_op jit(solution)/shard_map/ppermute | solution.py:362
  65.6 3.4 %collective-permute-start.9 = (bf16[512,512]{1,0:T(8,128)(2,1)S(1)}, bf16[512,512]{1,0:T(8,128)(2,1)S(1)}, u32[]{:S(2)}, u32[]{:S(2)}) collective-permute-start(bf16[512,512]{1,0:T(8,128)(2,1)S(1)} %collective-permute-done.5.refs_2_), channel_id=1, source_target_pairs={{0,1},{1,0},{2,3},{3,2},{4,5},{5,4},{6,7},{7,6},{8,9},{9,8},{10,11... | collective-permute-start | bytes 1572872 | tf_op jit(solution)/shard_map/ppermute | solution.py:362
  66.1 3.7 %collective-permute-start.10 = (bf16[512,512]{1,0:T(8,128)(2,1)S(1)}, bf16[512,512]{1,0:T(8,128)(2,1)}, u32[]{:S(2)}, u32[]{:S(2)}) collective-permute-start(bf16[512,512]{1,0:T(8,128)(2,1)S(1)} %collective-permute-done.6.refs_3_), channel_id=1, source_target_pairs={{0,1},{1,0},{2,3},{3,2},{4,5},{5,4},{6,7},{7,6},{8,9},{9,8},{10,11... | collective-permute-start | bytes 1572872 | tf_op jit(solution)/shard_map/ppermute | solution.py:362
  66.4 0.9 copy-start.3
  67.2 1.8 %copy-start.12 = (bf16[512,512]{1,0:T(8,128)(2,1)}, bf16[512,512]{1,0:T(8,128)(2,1)S(1)}, u32[]{:S(2)}) copy-start(bf16[512,512]{1,0:T(8,128)(2,1)S(1)} %collective-permute-done.3.refs_4_) | copy-start | bytes 1572868
  67.5 1.5 copy-start.13
  69.0 0.8 copy-start.14
  69.8 10.9 %collective-permute-start.12 = (bf16[512,2048]{1,0:T(8,128)(2,1)S(1)}, bf16[512,2048]{1,0:T(8,128)(2,1)S(1)}, u32[]{:S(2)}, u32[]{:S(2)}) collective-permute-start(bf16[512,2048]{1,0:T(8,128)(2,1)S(1)} %bitcast.14), channel_id=1, source_target_pairs={{0,1},{1,0},{2,3},{3,2},{4,5},{5,4},{6,7},{7,6},{8,9},{9,8},{10,11... | collective-permute-start | bytes 6291464 | tf_op jit(solution)/shard_map/ppermute | solution.py:362
  70.0 9.2 %collective-permute-start.13 = (bf16[128,512]{1,0:T(8,128)(2,1)S(1)}, bf16[128,512]{1,0:T(8,128)(2,1)S(1)}, u32[]{:S(2)}, u32[]{:S(2)}) collective-permute-start(bf16[128,512]{1,0:T(8,128)(2,1)S(1)} %get-tuple-element.58), channel_id=1, source_target_pairs={{0,6},{1,7},{2,0},{3,1},{4,2},{5,3},{6,4},{7,5},{8,14},{9,15},{10,... | collective-permute-start | bytes 393224 | tf_op jit(solution)/shard_map/ppermute | solution.py:357
  70.9 8.3 %collective-permute-start.14 = (bf16[128,512]{1,0:T(8,128)(2,1)S(1)}, bf16[128,512]{1,0:T(8,128)(2,1)S(1)}, u32[]{:S(2)}, u32[]{:S(2)}) collective-permute-start(bf16[128,512]{1,0:T(8,128)(2,1)S(1)} %get-tuple-element.59), channel_id=1, source_target_pairs={{0,4},{1,5},{2,6},{3,7},{4,0},{5,1},{6,2},{7,3},{8,12},{9,13},{10,... | collective-permute-start | bytes 393224 | tf_op jit(solution)/shard_map/ppermute | solution.py:357
  71.2 9.5 %collective-permute-start.15 = (bf16[128,512]{1,0:T(8,128)(2,1)S(1)}, bf16[128,512]{1,0:T(8,128)(2,1)S(1)}, u32[]{:S(2)}, u32[]{:S(2)}) collective-permute-start(bf16[128,512]{1,0:T(8,128)(2,1)S(1)} %get-tuple-element.60), channel_id=1, source_target_pairs={{0,2},{1,3},{2,4},{3,5},{4,6},{5,7},{6,0},{7,1},{8,10},{9,11},{10,... | collective-permute-start | bytes 393224 | tf_op jit(solution)/shard_map/ppermute | solution.py:357
  87.1 7.0 %collective-permute-start.16 = (bf16[512,2048]{1,0:T(8,128)(2,1)S(1)}, bf16[512,2048]{1,0:T(8,128)(2,1)S(1)}, u32[]{:S(2)}, u32[]{:S(2)}) collective-permute-start(bf16[512,2048]{1,0:T(8,128)(2,1)S(1)} %get-tuple-element.67), channel_id=1, source_target_pairs={{0,1},{1,0},{2,3},{3,2},{4,5},{5,4},{6,7},{7,6},{8,9},{9,8},{10,11... | collective-permute-start | bytes 6291464 | tf_op jit(solution)/shard_map/ppermute | solution.py:362
  93.6 9.6 %collective-permute-start.20 = (bf16[512,2048]{1,0:T(8,128)(2,1)}, bf16[512,2048]{1,0:T(8,128)(2,1)}, u32[]{:S(2)}, u32[]{:S(2)}) collective-permute-start(bf16[512,2048]{1,0:T(8,128)(2,1)} %get-tuple-element.73), channel_id=1, source_target_pairs={{0,1},{1,0},{2,3},{3,2},{4,5},{5,4},{6,7},{7,6},{8,9},{9,8},{10,11... | collective-permute-start | bytes 6291464 | tf_op jit(solution)/shard_map/ppermute | solution.py:362
  96.0 34.7 %all-to-all-start.2 = ((bf16[16,32,2048]{2,1,0:T(8,128)(2,1)}), bf16[16,32,2048]{2,1,0:T(8,128)(2,1)S(1)}, u32[]{:S(2)}, u32[]{:S(2)}) async-start(bf16[16,32,2048]{2,1,0:T(8,128)(2,1)} %bitcast.9), calls=%async_computation.2 | async-start | bytes 4194304 | tf_op jit(solution)/shard_map/all_to_all | solution.py:365
  103.2 27.5 %copy-start.6 = (f32[128,2]{0,1:T(2,128)S(1)}, f32[128,2]{0,1:T(2,128)}, u32[]{:S(2)}) copy-start(f32[128,2]{0,1:T(2,128)} %param.12) | copy-start | bytes 3076
  107.9 0.8 copy-start.4
  108.7 27.3 %copy-start.5 = (bf16[512,512]{1,0:T(8,128)(2,1)S(1)}, bf16[512,512]{1,0:T(8,128)(2,1)}, u32[]{:S(2)}) copy-start(bf16[512,512]{1,0:T(8,128)(2,1)} %copy-done.4) | copy-start | bytes 1572868
  108.7 25.0 %collective-permute-start.21 = (bf16[512,512]{1,0:T(8,128)(2,1)}, bf16[512,512]{1,0:T(8,128)(2,1)}, u32[]{:S(2)}, u32[]{:S(2)}) collective-permute-start(bf16[512,512]{1,0:T(8,128)(2,1)} %get-tuple-element.75), channel_id=1, source_target_pairs={{0,6},{1,7},{2,0},{3,1},{4,2},{5,3},{6,4},{7,5},{8,14},{9,15},{10,... | collective-permute-start | bytes 1572872 | tf_op jit(solution)/shard_map/ppermute | solution.py:357
  109.9 23.8 %collective-permute-start.22 = (bf16[512,512]{1,0:T(8,128)(2,1)}, bf16[512,512]{1,0:T(8,128)(2,1)}, u32[]{:S(2)}, u32[]{:S(2)}) collective-permute-start(bf16[512,512]{1,0:T(8,128)(2,1)} %get-tuple-element.76), channel_id=1, source_target_pairs={{0,4},{1,5},{2,6},{3,7},{4,0},{5,1},{6,2},{7,3},{8,12},{9,13},{10,... | collective-permute-start | bytes 1572872 | tf_op jit(solution)/shard_map/ppermute | solution.py:357
  111.7 24.3 %collective-permute-start.23 = (bf16[512,512]{1,0:T(8,128)(2,1)}, bf16[512,512]{1,0:T(8,128)(2,1)}, u32[]{:S(2)}, u32[]{:S(2)}) collective-permute-start(bf16[512,512]{1,0:T(8,128)(2,1)} %get-tuple-element.77), channel_id=1, source_target_pairs={{0,2},{1,3},{2,4},{3,5},{4,6},{5,7},{6,0},{7,1},{8,10},{9,11},{10,... | collective-permute-start | bytes 1572872 | tf_op jit(solution)/shard_map/ppermute | solution.py:357
  133.6 4.9 %copy-start.7 = (bf16[128,512]{1,0:T(8,128)(2,1)}, bf16[128,512]{1,0:T(8,128)(2,1)S(1)}, u32[]{:S(2)}) copy-start(bf16[128,512]{1,0:T(8,128)(2,1)S(1)} %get-tuple-element.71) | copy-start | bytes 393220
  133.6 4.9 %copy-start.8 = (bf16[128,512]{1,0:T(8,128)(2,1)}, bf16[128,512]{1,0:T(8,128)(2,1)S(1)}, u32[]{:S(2)}) copy-start(bf16[128,512]{1,0:T(8,128)(2,1)S(1)} %get-tuple-element.70) | copy-start | bytes 393220
  133.6 12.2 %collective-permute-start.24 = (f32[128,2]{1,0:T(8,128)S(1)}, f32[128,2]{1,0:T(8,128)S(1)}, u32[]{:S(2)}, u32[]{:S(2)}) collective-permute-start(f32[128,2]{1,0:T(8,128)S(1)} %bitcast.24), channel_id=1, source_target_pairs={{0,1},{1,0},{2,3},{3,2},{4,5},{5,4},{6,7},{7,6},{8,9},{9,8},{10,11... | collective-permute-start | bytes 3080 | tf_op jit(solution)/shard_map/ppermute | solution.py:362
  136.0 24.4 %copy-start.2 = (bf16[256,512]{1,0:T(8,128)(2,1)S(1)}, bf16[256,512]{1,0:T(8,128)(2,1)}, u32[]{:S(2)}) copy-start(bf16[256,512]{1,0:T(8,128)(2,1)} %copy-done.1) | copy-start | bytes 786436
  138.5 21.8 %all-to-all-start.3 = ((bf16[16,32,512]{2,1,0:T(8,128)(2,1)}), bf16[16,32,512]{2,1,0:T(8,128)(2,1)S(1)}, u32[]{:S(2)}, u32[]{:S(2)}) async-start(bf16[16,32,512]{2,1,0:T(8,128)(2,1)} %bitcast.11), calls=%async_computation.3 | async-start | bytes 1048576 | tf_op jit(solution)/shard_map/all_to_all | solution.py:365
  145.8 6.2 %collective-permute-start.27 = (f32[128,2]{1,0:T(8,128)S(1)}, f32[128,2]{1,0:T(8,128)S(1)}, u32[]{:S(2)}, u32[]{:S(2)}) collective-permute-start(f32[128,2]{1,0:T(8,128)S(1)} %slice_add_fusion), channel_id=1, source_target_pairs={{0,6},{1,7},{2,0},{3,1},{4,2},{5,3},{6,4},{7,5},{8,14},{9,15},{10,... | collective-permute-start | bytes 3080 | tf_op jit(solution)/shard_map/ppermute | solution.py:357
  146.5 7.0 %collective-permute-start.26 = (f32[128,2]{1,0:T(8,128)S(1)}, f32[128,2]{1,0:T(8,128)S(1)}, u32[]{:S(2)}, u32[]{:S(2)}) collective-permute-start(f32[128,2]{1,0:T(8,128)S(1)} %slice_add_fusion), channel_id=1, source_target_pairs={{0,4},{1,5},{2,6},{3,7},{4,0},{5,1},{6,2},{7,3},{8,12},{9,13},{10,... | collective-permute-start | bytes 3080 | tf_op jit(solution)/shard_map/ppermute | solution.py:357
  148.2 5.5 %collective-permute-start.25 = (f32[128,2]{1,0:T(8,128)S(1)}, f32[128,2]{1,0:T(8,128)S(1)}, u32[]{:S(2)}, u32[]{:S(2)}) collective-permute-start(f32[128,2]{1,0:T(8,128)S(1)} %slice_add_fusion), channel_id=1, source_target_pairs={{0,2},{1,3},{2,4},{3,5},{4,6},{5,7},{6,0},{7,1},{8,10},{9,11},{10,... | collective-permute-start | bytes 3080 | tf_op jit(solution)/shard_map/ppermute | solution.py:357
  149.0 7.4 %collective-permute-start.17 = (bf16[128,512]{1,0:T(8,128)(2,1)}, bf16[128,512]{1,0:T(8,128)(2,1)S(1)}, u32[]{:S(2)}, u32[]{:S(2)}) collective-permute-start(bf16[128,512]{1,0:T(8,128)(2,1)} %copy-done.8), channel_id=1, source_target_pairs={{0,6},{1,7},{2,0},{3,1},{4,2},{5,3},{6,4},{7,5},{8,14},{9,15},{10,... | collective-permute-start | bytes 393224 | tf_op jit(solution)/shard_map/ppermute | solution.py:357
  151.5 7.1 %collective-permute-start.18 = (bf16[128,512]{1,0:T(8,128)(2,1)}, bf16[128,512]{1,0:T(8,128)(2,1)S(1)}, u32[]{:S(2)}, u32[]{:S(2)}) collective-permute-start(bf16[128,512]{1,0:T(8,128)(2,1)} %copy-done.7), channel_id=1, source_target_pairs={{0,4},{1,5},{2,6},{3,7},{4,0},{5,1},{6,2},{7,3},{8,12},{9,13},{10,... | collective-permute-start | bytes 393224 | tf_op jit(solution)/shard_map/ppermute | solution.py:357
  152.0 7.6 %collective-permute-start.19 = (bf16[128,512]{1,0:T(8,128)(2,1)S(1)}, bf16[128,512]{1,0:T(8,128)(2,1)S(1)}, u32[]{:S(2)}, u32[]{:S(2)}) collective-permute-start(bf16[128,512]{1,0:T(8,128)(2,1)S(1)} %get-tuple-element.72), channel_id=1, source_target_pairs={{0,2},{1,3},{2,4},{3,5},{4,6},{5,7},{6,0},{7,1},{8,10},{9,11},{10,... | collective-permute-start | bytes 393224 | tf_op jit(solution)/shard_map/ppermute | solution.py:357

commit v5 on v4

--- a/solution.py
+++ b/solution.py
@@ -244,6 +244,7 @@
 def down_kernel(dadu_ref, wg, wu, got, *refs):
     outs, (ws, gs, sems) = refs[:SIDES], refs[SIDES:]
     width = ws.shape[1]
+    sent = []
     units = wg.shape[1]
     load = Loads(sems)
     at = starts(width)
@@ -257,7 +258,9 @@
     ]
     for d in range(SIDES):
         wait(copies[d])
-        outs[d][...] = (dot_nt(dadu_ref[...], ws[d]) + gs[d].astype(F32)).astype(BF16)
+        gs[d] = (dot_nt(dadu_ref[...], ws[d]) + gs[d].astype(F32)).astype(BF16)
+        sent.append(load(gs.at[d], outs[d]))
+    wait(sent)
 
 
 def add_kernel(mine, got, out):
@@ -314,18 +317,18 @@
     out[...] = (dense + z).astype(BF16)
 
 
-def call(kernel, outs, limit, flops, args, name, far_args=(), scratch=(), far_out=False):
+def call(kernel, outs, limit, flops, args, name, far_args=(), scratch=(), far_out=0):
     vmem = pl.BlockSpec(memory_space=pltpu.VMEM)
     far = pl.BlockSpec(memory_space=pl.ANY)
     moved = sum(a.size * a.dtype.itemsize for a in args)
     return pl.pallas_call(
         kernel,
         out_shape=[
-            pltpu.HBM(*o) if far_out and i == 0 else jax.ShapeDtypeStruct(*o)
+            pltpu.HBM(*o) if i < far_out else jax.ShapeDtypeStruct(*o)
             for i, o in enumerate(outs)
         ],
         in_specs=[far if i in far_args else vmem for i in range(len(args))],
-        out_specs=[far if far_out and i == 0 else vmem for i in range(len(outs))],
+        out_specs=[far if i < far_out else vmem for i in range(len(outs))],
         compiler_params=pltpu.CompilerParams(vmem_limit_bytes=limit * MIB),
         cost_estimate=pl.CostEstimate(flops=flops, bytes_accessed=moved, transcendentals=0),
         scratch_shapes=list(scratch),
@@ -390,7 +393,7 @@
         "rows",
         far_args=(5,),
         scratch=[pltpu.VMEM((slots, half), BF16), sems((SIDES,))],
-        far_out=True,
+        far_out=1,
     )
     got_rows = spread(rows_send)
     grads_own = [got_grads] + [along(got_grads, d) for d in (1, 2, 3)]
@@ -484,7 +487,8 @@
         (dadu, wg, wu, grad_got),
         "down",
         far_args=(1, 2, 3),
-        scratch=[half_scratch[1], pltpu.VMEM((SIDES, slots, width), BF16), sems((12,))],
+        scratch=[half_scratch[1], pltpu.VMEM((SIDES, slots, width), BF16), sems((16,))],
+        far_out=SIDES,
     )
     grad_all = [grad_part[0]] + [along(grad_part[d], SIDES - d) for d in (1, 2, 3)]
     m0, m1, m2, m3, inner = call(

time: 162 us -> 161 us (level)
  no operation moved by 1% of the time
where the time goes in v5:
time: 161 us
  waiting for transfers between devices  56.5 us (35%)
  starting transfers between devices  52.8 us (33%)
  Pallas kernels  47.4 us (29%)
  local copies, waits for them, and re-layouts  2.34 us (1%)
    pallas_call x12, Pallas kernels, call(): pl.pallas_call(kernel, out_shape=[pltpu.HBM(*o) if i < far_out else jax.S...  47.4 us
    ppermute x18, waiting for transfers between devices, along(): lax.ppermute(v, 'tensor', [(i, (i + 2 * d) % devices) for i in range(devi...  36.3 us
    all_to_all x4, starting transfers between devices, spread(): return lax.all_to_all(v, 'dp', split_axis=0, concat_axis=0, tiled=True)  30 us
    ppermute x18, starting transfers between devices, along(): lax.ppermute(v, 'tensor', [(i, (i + 2 * d) % devices) for i in range(devi...  20.7 us
    all_to_all x4, waiting for transfers between devices, spread(): return lax.all_to_all(v, 'dp', split_axis=0, concat_axis=0, tiled=True)  18.4 us
  transfers between devices with their start and end apart: 32, of which 15 were waited for; matrix products, arithmetic and copies ran while one was open for 1% of the time, Pallas kernels for 22%

profile of v5, /device:TPU:2, one launch (start us, length us, event | category | flops | bytes accessed | tf_op | source)
XLA Modules:
  0.0 160.8 jit_solution(13522933891635552797)
XLA Ops:
  0.6 2.4 %plan.1 = (bf16[256,512]{1,0:T(8,128)(2,1)S(1)}, bf16[512,512]{1,0:T(8,128)(2,1)}, bf16[256,512]{1,0:T(8,128)(2,1)S(1)}) custom-call(s32[2,128]{1,0:T(2,128)} %bitcast.39, f32[2,128]{1,0:T(2,128)} %bitcast.25, bf16[128,512]{1,0:T(8,128)(2,1)} %tokens.1, bf16[128,512]{1,0:T(8,128)(2,1)} %cotangent.1), custom_call_target="tpu_custom_call" | custom-call | flops 134217728 | bytes 264192 | tf_op jit(solution)/shard_map/plan/pallas_call | solution.py:324
  3.0 8.3 %all-to-all-start = ((bf16[16,32,512]{2,1,0:T(8,128)(2,1)}), bf16[16,32,512]{2,1,0:T(8,128)(2,1)S(1)}, u32[]{:S(2)}, u32[]{:S(2)}) async-start(bf16[16,32,512]{2,1,0:T(8,128)(2,1)} %bitcast.2), calls=%async_computation | async-start | bytes 1048576 | tf_op jit(solution)/shard_map/all_to_all | solution.py:368
  11.4 3.0 %collective-permute-start.2 = (bf16[256,512]{1,0:T(8,128)(2,1)S(1)}, bf16[256,512]{1,0:T(8,128)(2,1)S(1)}, u32[]{:S(2)}, u32[]{:S(2)}) collective-permute-start(bf16[256,512]{1,0:T(8,128)(2,1)S(1)} %get-tuple-element.44.p0), channel_id=1, source_target_pairs={{0,6},{1,7},{2,0},{3,1},{4,2},{5,3},{6,4},{7,5},{8,14},{9,15},{10,... | collective-permute-start | bytes 786440 | tf_op jit(solution)/shard_map/ppermute | solution.py:360
  14.4 0.6 collective-permute-start.1
  15.0 1.0 collective-permute-start
  16.0 9.0 %collective-permute-done.2.p3 = bf16[256,512]{1,0:T(8,128)(2,1)S(1)} collective-permute-done((bf16[256,512]{1,0:T(8,128)(2,1)S(1)}, bf16[256,512]{1,0:T(8,128)(2,1)S(1)}, u32[]{:S(2)}, u32[]{:S(2)}) %collective-permute-start.2) | collective-permute-done | bytes 262176 | tf_op jit(solution)/shard_map/ppermute | solution.py:360
  25.0 0.1 collective-permute-done.1.p2
  25.1 3.6 %collective-permute-done.p1 = bf16[256,512]{1,0:T(8,128)(2,1)S(1)} collective-permute-done((bf16[256,512]{1,0:T(8,128)(2,1)S(1)}, bf16[256,512]{1,0:T(8,128)(2,1)S(1)}, u32[]{:S(2)}, u32[]{:S(2)}) %collective-permute-start) | collective-permute-done | bytes 262176 | tf_op jit(solution)/shard_map/ppermute | solution.py:360
  28.7 2.7 %rows.1 = (bf16[512,2048]{1,0:T(8,128)(2,1)}, bf16[4,256,512]{2,1,0:T(8,128)(2,1)}) custom-call(bf16[256,512]{1,0:T(8,128)(2,1)S(1)} %get-tuple-element.41.pick_ref.pick, bf16[256,512]{1,0:T(8,128)(2,1)S(1)} %get-tuple-element.44.p0, bf16[256,512]{1,0:T(8,128)(2,1)S(1)} %collective-permute-done.p1, bf16[256,512]{1,0:T(8,128)(2,1)S(1)} %collective-permute-done.1.p2, ...), custom_call_target="tpu_custom_call" | custom-call | flops 268435456 | bytes 1835008 | tf_op jit(solution)/shard_map/rows/pallas_call | solution.py:324
  31.5 0.1 collective-permute-start.7
  31.6 7.2 %all-to-all-start.1 = ((bf16[16,32,2048]{2,1,0:T(8,128)(2,1)}), bf16[16,32,2048]{2,1,0:T(8,128)(2,1)S(1)}, u32[]{:S(2)}, u32[]{:S(2)}) async-start(bf16[16,32,2048]{2,1,0:T(8,128)(2,1)} %bitcast.38), calls=%async_computation.1 | async-start | bytes 4194304 | tf_op jit(solution)/shard_map/all_to_all | solution.py:368
  38.8 0.6 collective-permute-start.6
  39.4 0.6 collective-permute-start.5
  40.1 0.8 collective-permute-start.4
  40.9 9.4 %dense.1 = (bf16[256,2048]{1,0:T(8,128)(2,1)S(1)}, bf16[256,2048]{1,0:T(8,128)(2,1)S(1)}) custom-call(bf16[4,256,512]{2,1,0:T(8,128)(2,1)} %get-tuple-element.50.refs_0_.pack, bf16[4,256,512]{2,1,0:T(8,128)(2,1)} %collective-permute-done.7.refs_1_, bf16[4096,512]{1,0:T(8,128)(2,1)} %refs_2_.1, bf16[4096,512]{1,0:T(8,128)(2,1)} %refs_3_.1, ...), custom_call_target="tpu_custom_call" | custom-call | flops 3221225472 | bytes 14680064 | tf_op jit(solution)/shard_map/dense/pallas_call | solution.py:324
  50.2 0.1 collective-permute-start.11
  50.3 0.5 collective-permute-start.3
  50.8 2.8 %collective-permute-done.6.refs_3_ = bf16[512,512]{1,0:T(8,128)(2,1)S(1)} collective-permute-done((bf16[512,512]{1,0:T(8,128)(2,1)S(1)}, bf16[512,512]{1,0:T(8,128)(2,1)S(1)}, u32[]{:S(2)}, u32[]{:S(2)}) %collective-permute-start.6) | collective-permute-done | bytes 524320 | tf_op jit(solution)/shard_map/ppermute | solution.py:360
  53.6 2.2 %collective-permute-done.5.refs_2_ = bf16[512,512]{1,0:T(8,128)(2,1)S(1)} collective-permute-done((bf16[512,512]{1,0:T(8,128)(2,1)S(1)}, bf16[512,512]{1,0:T(8,128)(2,1)S(1)}, u32[]{:S(2)}, u32[]{:S(2)}) %collective-permute-start.5) | collective-permute-done | bytes 524320 | tf_op jit(solution)/shard_map/ppermute | solution.py:360
  55.8 9.8 %collective-permute-done.4.refs_1_ = bf16[512,512]{1,0:T(8,128)(2,1)S(1)} collective-permute-done((bf16[512,512]{1,0:T(8,128)(2,1)S(1)}, bf16[512,512]{1,0:T(8,128)(2,1)S(1)}, u32[]{:S(2)}, u32[]{:S(2)}) %collective-permute-start.4) | collective-permute-done | bytes 524320 | tf_op jit(solution)/shard_map/ppermute | solution.py:360
  65.6 0.0 collective-permute-start.8
  65.6 0.5 collective-permute-start.9
  66.1 0.0 collective-permute-start.10
  66.2 0.2 dense_sum.1
  66.4 0.9 copy-done.3
  67.3 0.3 collective-permute-done.8.refs_5_
  67.5 1.5 collective-permute-done.9.refs_6_
  69.1 0.8 copy-done.13
  69.9 0.1 collective-permute-start.12
  70.0 0.9 collective-permute-start.13
  71.0 0.3 collective-permute-start.14
  71.3 0.8 collective-permute-start.15
  72.1 7.1 %early.1 = (f32[512,384]{1,0:T(8,128)S(1)}, f32[512,768]{1,0:T(8,128)S(1)}) custom-call(bf16[512,512]{1,0:T(8,128)(2,1)} %bitcast.22, bf16[512,512]{1,0:T(8,128)(2,1)} %copy-done.10, bf16[512,512]{1,0:T(8,128)(2,1)} %copy-done.9, bf16[512,512]{1,0:T(8,128)(2,1)} %copy-done.8, bf16[512,512]{1,0:T(8,128)(2,1)} %copy-done.11, bf16[512,512]{1,0:T(8,128)(2,1)} %copy-done.12, ...), custom_call_target="tpu_custom_call" | custom-call | flops 3221225472 | bytes 15728640 | tf_op jit(solution)/shard_map/early/pallas_call | solution.py:324
  79.2 1.5 collective-permute-done.15.a3.d3
  80.8 6.4 %forth.1 = (bf16[512,2048]{1,0:T(8,128)(2,1)S(1)}, bf16[512,384]{1,0:T(8,128)(2,1)S(1)}, bf16[512,768]{1,0:T(8,128)(2,1)S(1)}) custom-call(bf16[512,2048]{1,0:T(8,128)(2,1)S(1)} %collective-permute-done.12.x, f32[512,768]{1,0:T(8,128)S(1)} %get-tuple-element.62.part, f32[512,384]{1,0:T(8,128)S(1)} %get-tuple-element.63.g_ref, bf16[4096,384]{1,0:T(8,128)(2,1)} %bitcast.28, ...), custom_call_target="tpu_custom_call" | custom-call | flops 2415919104 | bytes 14286848 | tf_op jit(solution)/shard_map/forth/pallas_call | solution.py:324
  87.2 0.1 collective-permute-start.16
  87.3 6.4 %cross.1 = (bf16[512,2048]{1,0:T(8,128)(2,1)S(1)}, bf16[512,2048]{1,0:T(8,128)(2,1)}) custom-call(bf16[512,384]{1,0:T(8,128)(2,1)S(1)} %get-tuple-element.64.hid_ref, bf16[512,768]{1,0:T(8,128)(2,1)S(1)} %get-tuple-element.65.dadu_ref, bf16[4096,384]{1,0:T(8,128)(2,1)} %bitcast.29, bf16[4096,384]{1,0:T(8,128)(2,1)} %bitcast.33, bf16[384,4096]{1,0:T(8,128)(2,1)} %bitcast.37), custom_call_target="tpu_custom_call" | custom-call | flops 2415919104 | bytes 10616832 | tf_op jit(solution)/shard_map/cross/pallas_call | solution.py:324
  93.6 0.5 collective-permute-start.20
  94.2 1.8 %add.36 = bf16[512,2048]{1,0:T(8,128)(2,1)} custom-call(bf16[512,2048]{1,0:T(8,128)(2,1)S(1)} %get-tuple-element.66.mine, bf16[512,2048]{1,0:T(8,128)(2,1)S(1)} %collective-permute-done.16.got), custom_call_target="tpu_custom_call" | custom-call | flops 1048576 | bytes 4194304 | tf_op jit(solution)/shard_map/add/pallas_call | solution.py:324
  96.0 7.2 %all-to-all-start.2 = ((bf16[16,32,2048]{2,1,0:T(8,128)(2,1)}), bf16[16,32,2048]{2,1,0:T(8,128)(2,1)S(1)}, u32[]{:S(2)}, u32[]{:S(2)}) async-start(bf16[16,32,2048]{2,1,0:T(8,128)(2,1)} %bitcast.9), calls=%async_computation.2 | async-start | bytes 4194304 | tf_op jit(solution)/shard_map/all_to_all | solution.py:368
  103.2 4.7 %down.1 = (bf16[512,512]{1,0:T(8,128)(2,1)}, bf16[512,512]{1,0:T(8,128)(2,1)}, bf16[512,512]{1,0:T(8,128)(2,1)}, bf16[512,512]{1,0:T(8,128)(2,1)}) custom-call(bf16[512,768]{1,0:T(8,128)(2,1)S(1)} %get-tuple-element.65.dadu_ref, bf16[4096,384]{1,0:T(8,128)(2,1)} %bitcast.30, bf16[4096,384]{1,0:T(8,128)(2,1)} %bitcast.34, ...), custom_call_target="tpu_custom_call" | custom-call | flops 1610612736 | bytes 9175040 | tf_op jit(solution)/shard_map/down/pallas_call | solution.py:324
  107.9 1.5 collective-permute-start.21
  109.4 1.8 %collective-permute-start.22 = (bf16[512,512]{1,0:T(8,128)(2,1)}, bf16[512,512]{1,0:T(8,128)(2,1)}, u32[]{:S(2)}, u32[]{:S(2)}) collective-permute-start(bf16[512,512]{1,0:T(8,128)(2,1)} %get-tuple-element.76), channel_id=1, source_target_pairs={{0,4},{1,5},{2,6},{3,7},{4,0},{5,1},{6,2},{7,3},{8,12},{9,13},{10,... | collective-permute-start | bytes 1572872 | tf_op jit(solution)/shard_map/ppermute | solution.py:360
  111.2 1.1 collective-permute-start.23
  112.3 18.4 %all-to-all-done.2 = bf16[16,32,2048]{2,1,0:T(8,128)(2,1)S(1)} async-done(((bf16[16,32,2048]{2,1,0:T(8,128)(2,1)}), bf16[16,32,2048]{2,1,0:T(8,128)(2,1)S(1)}, u32[]{:S(2)}, u32[]{:S(2)}) %all-to-all-start.2) | async-done | bytes 2097184 | tf_op jit(solution)/shard_map/all_to_all | solution.py:368
  130.7 2.9 %mix.1 = (bf16[128,512]{1,0:T(8,128)(2,1)S(1)}, bf16[128,512]{1,0:T(8,128)(2,1)S(1)}, bf16[128,512]{1,0:T(8,128)(2,1)S(1)}, bf16[128,512]{1,0:T(8,128)(2,1)S(1)}, f32[128,128]{1,0:T(8,128)S(1)}) custom-call(bf16[512,2048]{1,0:T(8,128)(2,1)S(1)} %bitcast.16, bf16[256,512]{1,0:T(8,128)(2,1)} %copy-done.1, f32[2,128]{1,0:T(2,128)S(1)} %bitcast.26, ...), custom_call_target="tpu_custom_call" | custom-call | flops 536870912 | bytes 3933184 | tf_op jit(solution)/shard_map/mix/pallas_call | solution.py:324
  133.6 0.0 copy-start.6
  133.6 0.1 collective-permute-start.24
  133.7 1.8 %collective-permute-done.23.p3 = bf16[512,512]{1,0:T(8,128)(2,1)} collective-permute-done((bf16[512,512]{1,0:T(8,128)(2,1)}, bf16[512,512]{1,0:T(8,128)(2,1)}, u32[]{:S(2)}, u32[]{:S(2)}) %collective-permute-start.23) | collective-permute-done | bytes 524320 | tf_op jit(solution)/shard_map/ppermute | solution.py:360
  135.5 2.5 %sum.1 = bf16[512,512]{1,0:T(8,128)(2,1)} custom-call(bf16[512,512]{1,0:T(8,128)(2,1)S(1)} %copy-done.4, bf16[512,512]{1,0:T(8,128)(2,1)} %collective-permute-done.21.p1, bf16[512,512]{1,0:T(8,128)(2,1)} %collective-permute-done.22.p2, bf16[512,512]{1,0:T(8,128)(2,1)} %collective-permute-done.23.p3, f32[128,128]{1,0:T(8,128)S(1)} %get-tuple-element.78.after), custom_call_target="tpu_custom_call" | custom-call | flops 786432 | bytes 2162688 | tf_op jit(solution)/shard_map/sum/pallas_call | solution.py:324
  138.0 7.2 %all-to-all-start.3 = ((bf16[16,32,512]{2,1,0:T(8,128)(2,1)}), bf16[16,32,512]{2,1,0:T(8,128)(2,1)S(1)}, u32[]{:S(2)}, u32[]{:S(2)}) async-start(bf16[16,32,512]{2,1,0:T(8,128)(2,1)} %bitcast.11), calls=%async_computation.3 | async-start | bytes 1048576 | tf_op jit(solution)/shard_map/all_to_all | solution.py:368
  145.3 0.7 collective-permute-start.27
  146.0 1.8 %collective-permute-start.26 = (f32[128,2]{1,0:T(8,128)S(1)}, f32[128,2]{1,0:T(8,128)S(1)}, u32[]{:S(2)}, u32[]{:S(2)}) collective-permute-start(f32[128,2]{1,0:T(8,128)S(1)} %slice_add_fusion), channel_id=1, source_target_pairs={{0,4},{1,5},{2,6},{3,7},{4,0},{5,1},{6,2},{7,3},{8,12},{9,13},{10,... | collective-permute-start | bytes 3080 | tf_op jit(solution)/shard_map/ppermute | solution.py:360
  147.8 0.7 collective-permute-start.25
  148.5 2.5 %collective-permute-start.17 = (bf16[128,512]{1,0:T(8,128)(2,1)}, bf16[128,512]{1,0:T(8,128)(2,1)S(1)}, u32[]{:S(2)}, u32[]{:S(2)}) collective-permute-start(bf16[128,512]{1,0:T(8,128)(2,1)} %copy-done.7), channel_id=1, source_target_pairs={{0,6},{1,7},{2,0},{3,1},{4,2},{5,3},{6,4},{7,5},{8,14},{9,15},{10,... | collective-permute-start | bytes 393224 | tf_op jit(solution)/shard_map/ppermute | solution.py:360
  151.1 0.5 collective-permute-start.18
  151.5 1.4 collective-permute-start.19
  153.0 0.3 collective-permute-done.25
  153.3 0.6 copy.13
  154.0 2.0 %collective-permute-done.17 = bf16[128,512]{1,0:T(8,128)(2,1)S(1)} collective-permute-done((bf16[128,512]{1,0:T(8,128)(2,1)}, bf16[128,512]{1,0:T(8,128)(2,1)S(1)}, u32[]{:S(2)}, u32[]{:S(2)}) %collective-permute-start.17) | collective-permute-done | bytes 131104 | tf_op jit(solution)/shard_map/ppermute | solution.py:360
  155.9 2.2 %collective-permute-done.18 = bf16[128,512]{1,0:T(8,128)(2,1)S(1)} collective-permute-done((bf16[128,512]{1,0:T(8,128)(2,1)}, bf16[128,512]{1,0:T(8,128)(2,1)S(1)}, u32[]{:S(2)}, u32[]{:S(2)}) %collective-permute-start.18) | collective-permute-done | bytes 131104 | tf_op jit(solution)/shard_map/ppermute | solution.py:360
  158.1 1.0 collective-permute-done.19
  159.1 0.7 add_convert_fusion
  159.9 0.9 grad.1
  (44 shorter events, 0.1 us)
Async XLA Ops:
  3.0 28.5 %copy-start.1 = (bf16[256,512]{1,0:T(8,128)(2,1)}, bf16[256,512]{1,0:T(8,128)(2,1)S(1)}, u32[]{:S(2)}) copy-start(bf16[256,512]{1,0:T(8,128)(2,1)S(1)} %get-tuple-element.41.pick_ref.pick) | copy-start | bytes 786436
  3.0 25.7 %all-to-all-start = ((bf16[16,32,512]{2,1,0:T(8,128)(2,1)}), bf16[16,32,512]{2,1,0:T(8,128)(2,1)S(1)}, u32[]{:S(2)}, u32[]{:S(2)}) async-start(bf16[16,32,512]{2,1,0:T(8,128)(2,1)} %bitcast.2), calls=%async_computation | async-start | bytes 1048576 | tf_op jit(solution)/shard_map/all_to_all | solution.py:368
  11.4 13.6 %collective-permute-start.2 = (bf16[256,512]{1,0:T(8,128)(2,1)S(1)}, bf16[256,512]{1,0:T(8,128)(2,1)S(1)}, u32[]{:S(2)}, u32[]{:S(2)}) collective-permute-start(bf16[256,512]{1,0:T(8,128)(2,1)S(1)} %get-tuple-element.44.p0), channel_id=1, source_target_pairs={{0,6},{1,7},{2,0},{3,1},{4,2},{5,3},{6,4},{7,5},{8,14},{9,15},{10,... | collective-permute-start | bytes 786440 | tf_op jit(solution)/shard_map/ppermute | solution.py:360
  14.4 10.8 %collective-permute-start.1 = (bf16[256,512]{1,0:T(8,128)(2,1)S(1)}, bf16[256,512]{1,0:T(8,128)(2,1)S(1)}, u32[]{:S(2)}, u32[]{:S(2)}) collective-permute-start(bf16[256,512]{1,0:T(8,128)(2,1)S(1)} %get-tuple-element.44.p0), channel_id=1, source_target_pairs={{0,4},{1,5},{2,6},{3,7},{4,0},{5,1},{6,2},{7,3},{8,12},{9,13},{10,... | collective-permute-start | bytes 786440 | tf_op jit(solution)/shard_map/ppermute | solution.py:360
  15.0 13.7 %collective-permute-start = (bf16[256,512]{1,0:T(8,128)(2,1)S(1)}, bf16[256,512]{1,0:T(8,128)(2,1)S(1)}, u32[]{:S(2)}, u32[]{:S(2)}) collective-permute-start(bf16[256,512]{1,0:T(8,128)(2,1)S(1)} %get-tuple-element.44.p0), channel_id=1, source_target_pairs={{0,2},{1,3},{2,4},{3,5},{4,6},{5,7},{6,0},{7,1},{8,10},{9,11},{10,... | collective-permute-start | bytes 786440 | tf_op jit(solution)/shard_map/ppermute | solution.py:360
  28.7 21.6 %copy-start = (bf16[16,32,512]{2,1,0:T(8,128)(2,1)}, bf16[16,32,512]{2,1,0:T(8,128)(2,1)S(1)}, u32[]{:S(2)}) copy-start(bf16[16,32,512]{2,1,0:T(8,128)(2,1)S(1)} %all-to-all-done) | copy-start | bytes 1572868
  31.5 9.4 %collective-permute-start.7 = (bf16[4,256,512]{2,1,0:T(8,128)(2,1)}, bf16[4,256,512]{2,1,0:T(8,128)(2,1)}, u32[]{:S(2)}, u32[]{:S(2)}) collective-permute-start(bf16[4,256,512]{2,1,0:T(8,128)(2,1)} %get-tuple-element.50.refs_0_.pack), channel_id=1, source_target_pairs={{0,1},{1,0},{2,3},{3,2},{4,5},{5,4},{6,7},{7,6},{8,9},{9,8},{10,11... | collective-permute-start | bytes 3145736 | tf_op jit(solution)/shard_map/ppermute | solution.py:365
  31.6 38.3 %all-to-all-start.1 = ((bf16[16,32,2048]{2,1,0:T(8,128)(2,1)}), bf16[16,32,2048]{2,1,0:T(8,128)(2,1)S(1)}, u32[]{:S(2)}, u32[]{:S(2)}) async-start(bf16[16,32,2048]{2,1,0:T(8,128)(2,1)} %bitcast.38), calls=%async_computation.1 | async-start | bytes 4194304 | tf_op jit(solution)/shard_map/all_to_all | solution.py:368
  38.8 14.8 %collective-permute-start.6 = (bf16[512,512]{1,0:T(8,128)(2,1)S(1)}, bf16[512,512]{1,0:T(8,128)(2,1)S(1)}, u32[]{:S(2)}, u32[]{:S(2)}) collective-permute-start(bf16[512,512]{1,0:T(8,128)(2,1)S(1)} %bitcast.18), channel_id=1, source_target_pairs={{0,6},{1,7},{2,0},{3,1},{4,2},{5,3},{6,4},{7,5},{8,14},{9,15},{10,... | collective-permute-start | bytes 1572872 | tf_op jit(solution)/shard_map/ppermute | solution.py:360
  39.4 16.4 %collective-permute-start.5 = (bf16[512,512]{1,0:T(8,128)(2,1)S(1)}, bf16[512,512]{1,0:T(8,128)(2,1)S(1)}, u32[]{:S(2)}, u32[]{:S(2)}) collective-permute-start(bf16[512,512]{1,0:T(8,128)(2,1)S(1)} %bitcast.19), channel_id=1, source_target_pairs={{0,4},{1,5},{2,6},{3,7},{4,0},{5,1},{6,2},{7,3},{8,12},{9,13},{10,... | collective-permute-start | bytes 1572872 | tf_op jit(solution)/shard_map/ppermute | solution.py:360
  40.1 25.6 %collective-permute-start.4 = (bf16[512,512]{1,0:T(8,128)(2,1)S(1)}, bf16[512,512]{1,0:T(8,128)(2,1)S(1)}, u32[]{:S(2)}, u32[]{:S(2)}) collective-permute-start(bf16[512,512]{1,0:T(8,128)(2,1)S(1)} %bitcast.20), channel_id=1, source_target_pairs={{0,2},{1,3},{2,4},{3,5},{4,6},{5,7},{6,0},{7,1},{8,10},{9,11},{10,... | collective-permute-start | bytes 1572872 | tf_op jit(solution)/shard_map/ppermute | solution.py:360
  50.2 15.9 %collective-permute-start.11 = (bf16[256,2048]{1,0:T(8,128)(2,1)S(1)}, bf16[256,2048]{1,0:T(8,128)(2,1)S(1)}, u32[]{:S(2)}, u32[]{:S(2)}) collective-permute-start(bf16[256,2048]{1,0:T(8,128)(2,1)S(1)} %get-tuple-element.56), channel_id=1, source_target_pairs={{0,1},{1,0},{2,3},{3,2},{4,5},{5,4},{6,7},{7,6},{8,9},{9,8},{10,11... | collective-permute-start | bytes 3145736 | tf_op jit(solution)/shard_map/ppermute | solution.py:365
  50.3 16.9 %collective-permute-start.3 = (bf16[512,512]{1,0:T(8,128)(2,1)S(1)}, bf16[512,512]{1,0:T(8,128)(2,1)S(1)}, u32[]{:S(2)}, u32[]{:S(2)}) collective-permute-start(bf16[512,512]{1,0:T(8,128)(2,1)S(1)} %bitcast.21), channel_id=1, source_target_pairs={{0,1},{1,0},{2,3},{3,2},{4,5},{5,4},{6,7},{7,6},{8,9},{9,8},{10,11... | collective-permute-start | bytes 1572872 | tf_op jit(solution)/shard_map/ppermute | solution.py:365
  53.6 15.4 %copy-start.8 = (bf16[512,512]{1,0:T(8,128)(2,1)}, bf16[512,512]{1,0:T(8,128)(2,1)S(1)}, u32[]{:S(2)}) copy-start(bf16[512,512]{1,0:T(8,128)(2,1)S(1)} %collective-permute-done.6.refs_3_) | copy-start | bytes 1572868
  55.8 13.2 %copy-start.9 = (bf16[512,512]{1,0:T(8,128)(2,1)}, bf16[512,512]{1,0:T(8,128)(2,1)S(1)}, u32[]{:S(2)}) copy-start(bf16[512,512]{1,0:T(8,128)(2,1)S(1)} %collective-permute-done.5.refs_2_) | copy-start | bytes 1572868
  65.6 3.4 %copy-start.10 = (bf16[512,512]{1,0:T(8,128)(2,1)}, bf16[512,512]{1,0:T(8,128)(2,1)S(1)}, u32[]{:S(2)}) copy-start(bf16[512,512]{1,0:T(8,128)(2,1)S(1)} %collective-permute-done.4.refs_1_) | copy-start | bytes 1572868
  65.6 1.9 %collective-permute-start.8 = (bf16[512,512]{1,0:T(8,128)(2,1)S(1)}, bf16[512,512]{1,0:T(8,128)(2,1)S(1)}, u32[]{:S(2)}, u32[]{:S(2)}) collective-permute-start(bf16[512,512]{1,0:T(8,128)(2,1)S(1)} %collective-permute-done.4.refs_1_), channel_id=1, source_target_pairs={{0,1},{1,0},{2,3},{3,2},{4,5},{5,4},{6,7},{7,6},{8,9},{9,8},{10,11... | collective-permute-start | bytes 1572872 | tf_op jit(solution)/shard_map/ppermute | solution.py:365
  65.6 3.4 %collective-permute-start.9 = (bf16[512,512]{1,0:T(8,128)(2,1)S(1)}, bf16[512,512]{1,0:T(8,128)(2,1)S(1)}, u32[]{:S(2)}, u32[]{:S(2)}) collective-permute-start(bf16[512,512]{1,0:T(8,128)(2,1)S(1)} %collective-permute-done.5.refs_2_), channel_id=1, source_target_pairs={{0,1},{1,0},{2,3},{3,2},{4,5},{5,4},{6,7},{7,6},{8,9},{9,8},{10,11... | collective-permute-start | bytes 1572872 | tf_op jit(solution)/shard_map/ppermute | solution.py:365
  66.1 3.7 %collective-permute-start.10 = (bf16[512,512]{1,0:T(8,128)(2,1)S(1)}, bf16[512,512]{1,0:T(8,128)(2,1)}, u32[]{:S(2)}, u32[]{:S(2)}) collective-permute-start(bf16[512,512]{1,0:T(8,128)(2,1)S(1)} %collective-permute-done.6.refs_3_), channel_id=1, source_target_pairs={{0,1},{1,0},{2,3},{3,2},{4,5},{5,4},{6,7},{7,6},{8,9},{9,8},{10,11... | collective-permute-start | bytes 1572872 | tf_op jit(solution)/shard_map/ppermute | solution.py:365
  66.4 0.9 copy-start.3
  67.3 1.8 %copy-start.11 = (bf16[512,512]{1,0:T(8,128)(2,1)}, bf16[512,512]{1,0:T(8,128)(2,1)S(1)}, u32[]{:S(2)}) copy-start(bf16[512,512]{1,0:T(8,128)(2,1)S(1)} %collective-permute-done.3.refs_4_) | copy-start | bytes 1572868
  67.5 1.5 copy-start.12
  69.1 0.8 copy-start.13
  69.9 10.9 %collective-permute-start.12 = (bf16[512,2048]{1,0:T(8,128)(2,1)S(1)}, bf16[512,2048]{1,0:T(8,128)(2,1)S(1)}, u32[]{:S(2)}, u32[]{:S(2)}) collective-permute-start(bf16[512,2048]{1,0:T(8,128)(2,1)S(1)} %bitcast.14), channel_id=1, source_target_pairs={{0,1},{1,0},{2,3},{3,2},{4,5},{5,4},{6,7},{7,6},{8,9},{9,8},{10,11... | collective-permute-start | bytes 6291464 | tf_op jit(solution)/shard_map/ppermute | solution.py:365
  70.0 9.2 %collective-permute-start.13 = (bf16[128,512]{1,0:T(8,128)(2,1)S(1)}, bf16[128,512]{1,0:T(8,128)(2,1)S(1)}, u32[]{:S(2)}, u32[]{:S(2)}) collective-permute-start(bf16[128,512]{1,0:T(8,128)(2,1)S(1)} %get-tuple-element.58), channel_id=1, source_target_pairs={{0,6},{1,7},{2,0},{3,1},{4,2},{5,3},{6,4},{7,5},{8,14},{9,15},{10,... | collective-permute-start | bytes 393224 | tf_op jit(solution)/shard_map/ppermute | solution.py:360
  71.0 8.3 %collective-permute-start.14 = (bf16[128,512]{1,0:T(8,128)(2,1)S(1)}, bf16[128,512]{1,0:T(8,128)(2,1)S(1)}, u32[]{:S(2)}, u32[]{:S(2)}) collective-permute-start(bf16[128,512]{1,0:T(8,128)(2,1)S(1)} %get-tuple-element.59), channel_id=1, source_target_pairs={{0,4},{1,5},{2,6},{3,7},{4,0},{5,1},{6,2},{7,3},{8,12},{9,13},{10,... | collective-permute-start | bytes 393224 | tf_op jit(solution)/shard_map/ppermute | solution.py:360
  71.3 9.5 %collective-permute-start.15 = (bf16[128,512]{1,0:T(8,128)(2,1)S(1)}, bf16[128,512]{1,0:T(8,128)(2,1)S(1)}, u32[]{:S(2)}, u32[]{:S(2)}) collective-permute-start(bf16[128,512]{1,0:T(8,128)(2,1)S(1)} %get-tuple-element.60), channel_id=1, source_target_pairs={{0,2},{1,3},{2,4},{3,5},{4,6},{5,7},{6,0},{7,1},{8,10},{9,11},{10,... | collective-permute-start | bytes 393224 | tf_op jit(solution)/shard_map/ppermute | solution.py:360
  87.2 7.0 %collective-permute-start.16 = (bf16[512,2048]{1,0:T(8,128)(2,1)S(1)}, bf16[512,2048]{1,0:T(8,128)(2,1)S(1)}, u32[]{:S(2)}, u32[]{:S(2)}) collective-permute-start(bf16[512,2048]{1,0:T(8,128)(2,1)S(1)} %get-tuple-element.67), channel_id=1, source_target_pairs={{0,1},{1,0},{2,3},{3,2},{4,5},{5,4},{6,7},{7,6},{8,9},{9,8},{10,11... | collective-permute-start | bytes 6291464 | tf_op jit(solution)/shard_map/ppermute | solution.py:365
  93.6 9.6 %collective-permute-start.20 = (bf16[512,2048]{1,0:T(8,128)(2,1)}, bf16[512,2048]{1,0:T(8,128)(2,1)}, u32[]{:S(2)}, u32[]{:S(2)}) collective-permute-start(bf16[512,2048]{1,0:T(8,128)(2,1)} %get-tuple-element.73), channel_id=1, source_target_pairs={{0,1},{1,0},{2,3},{3,2},{4,5},{5,4},{6,7},{7,6},{8,9},{9,8},{10,11... | collective-permute-start | bytes 6291464 | tf_op jit(solution)/shard_map/ppermute | solution.py:365
  96.0 34.7 %all-to-all-start.2 = ((bf16[16,32,2048]{2,1,0:T(8,128)(2,1)}), bf16[16,32,2048]{2,1,0:T(8,128)(2,1)S(1)}, u32[]{:S(2)}, u32[]{:S(2)}) async-start(bf16[16,32,2048]{2,1,0:T(8,128)(2,1)} %bitcast.9), calls=%async_computation.2 | async-start | bytes 4194304 | tf_op jit(solution)/shard_map/all_to_all | solution.py:368
  103.2 27.5 %copy-start.5 = (f32[128,2]{0,1:T(2,128)S(1)}, f32[128,2]{0,1:T(2,128)}, u32[]{:S(2)}) copy-start(f32[128,2]{0,1:T(2,128)} %param.12) | copy-start | bytes 3076
  107.9 27.6 %copy-start.4 = (bf16[512,512]{1,0:T(8,128)(2,1)S(1)}, bf16[512,512]{1,0:T(8,128)(2,1)}, u32[]{:S(2)}) copy-start(bf16[512,512]{1,0:T(8,128)(2,1)} %get-tuple-element.74.p0) | copy-start | bytes 1572868
  107.9 25.8 %collective-permute-start.21 = (bf16[512,512]{1,0:T(8,128)(2,1)}, bf16[512,512]{1,0:T(8,128)(2,1)}, u32[]{:S(2)}, u32[]{:S(2)}) collective-permute-start(bf16[512,512]{1,0:T(8,128)(2,1)} %get-tuple-element.75), channel_id=1, source_target_pairs={{0,6},{1,7},{2,0},{3,1},{4,2},{5,3},{6,4},{7,5},{8,14},{9,15},{10,... | collective-permute-start | bytes 1572872 | tf_op jit(solution)/shard_map/ppermute | solution.py:360
  109.4 24.3 %collective-permute-start.22 = (bf16[512,512]{1,0:T(8,128)(2,1)}, bf16[512,512]{1,0:T(8,128)(2,1)}, u32[]{:S(2)}, u32[]{:S(2)}) collective-permute-start(bf16[512,512]{1,0:T(8,128)(2,1)} %get-tuple-element.76), channel_id=1, source_target_pairs={{0,4},{1,5},{2,6},{3,7},{4,0},{5,1},{6,2},{7,3},{8,12},{9,13},{10,... | collective-permute-start | bytes 1572872 | tf_op jit(solution)/shard_map/ppermute | solution.py:360
  111.2 24.3 %collective-permute-start.23 = (bf16[512,512]{1,0:T(8,128)(2,1)}, bf16[512,512]{1,0:T(8,128)(2,1)}, u32[]{:S(2)}, u32[]{:S(2)}) collective-permute-start(bf16[512,512]{1,0:T(8,128)(2,1)} %get-tuple-element.77), channel_id=1, source_target_pairs={{0,2},{1,3},{2,4},{3,5},{4,6},{5,7},{6,0},{7,1},{8,10},{9,11},{10,... | collective-permute-start | bytes 1572872 | tf_op jit(solution)/shard_map/ppermute | solution.py:360
  133.6 4.4 %copy-start.6 = (bf16[128,512]{1,0:T(8,128)(2,1)}, bf16[128,512]{1,0:T(8,128)(2,1)S(1)}, u32[]{:S(2)}) copy-start(bf16[128,512]{1,0:T(8,128)(2,1)S(1)} %get-tuple-element.71) | copy-start | bytes 393220
  133.6 4.4 %copy-start.7 = (bf16[128,512]{1,0:T(8,128)(2,1)}, bf16[128,512]{1,0:T(8,128)(2,1)S(1)}, u32[]{:S(2)}) copy-start(bf16[128,512]{1,0:T(8,128)(2,1)S(1)} %get-tuple-element.70) | copy-start | bytes 393220
  133.6 11.7 %collective-permute-start.24 = (f32[128,2]{1,0:T(8,128)S(1)}, f32[128,2]{1,0:T(8,128)S(1)}, u32[]{:S(2)}, u32[]{:S(2)}) collective-permute-start(f32[128,2]{1,0:T(8,128)S(1)} %bitcast.24), channel_id=1, source_target_pairs={{0,1},{1,0},{2,3},{3,2},{4,5},{5,4},{6,7},{7,6},{8,9},{9,8},{10,11... | collective-permute-start | bytes 3080 | tf_op jit(solution)/shard_map/ppermute | solution.py:365
  135.5 24.4 %copy-start.2 = (bf16[256,512]{1,0:T(8,128)(2,1)S(1)}, bf16[256,512]{1,0:T(8,128)(2,1)}, u32[]{:S(2)}) copy-start(bf16[256,512]{1,0:T(8,128)(2,1)} %copy-done.1) | copy-start | bytes 786436
  138.0 21.8 %all-to-all-start.3 = ((bf16[16,32,512]{2,1,0:T(8,128)(2,1)}), bf16[16,32,512]{2,1,0:T(8,128)(2,1)S(1)}, u32[]{:S(2)}, u32[]{:S(2)}) async-start(bf16[16,32,512]{2,1,0:T(8,128)(2,1)} %bitcast.11), calls=%async_computation.3 | async-start | bytes 1048576 | tf_op jit(solution)/shard_map/all_to_all | solution.py:368
  145.3 6.2 %collective-permute-start.27 = (f32[128,2]{1,0:T(8,128)S(1)}, f32[128,2]{1,0:T(8,128)S(1)}, u32[]{:S(2)}, u32[]{:S(2)}) collective-permute-start(f32[128,2]{1,0:T(8,128)S(1)} %slice_add_fusion), channel_id=1, source_target_pairs={{0,6},{1,7},{2,0},{3,1},{4,2},{5,3},{6,4},{7,5},{8,14},{9,15},{10,... | collective-permute-start | bytes 3080 | tf_op jit(solution)/shard_map/ppermute | solution.py:360
  146.0 7.0 %collective-permute-start.26 = (f32[128,2]{1,0:T(8,128)S(1)}, f32[128,2]{1,0:T(8,128)S(1)}, u32[]{:S(2)}, u32[]{:S(2)}) collective-permute-start(f32[128,2]{1,0:T(8,128)S(1)} %slice_add_fusion), channel_id=1, source_target_pairs={{0,4},{1,5},{2,6},{3,7},{4,0},{5,1},{6,2},{7,3},{8,12},{9,13},{10,... | collective-permute-start | bytes 3080 | tf_op jit(solution)/shard_map/ppermute | solution.py:360
  147.8 5.5 %collective-permute-start.25 = (f32[128,2]{1,0:T(8,128)S(1)}, f32[128,2]{1,0:T(8,128)S(1)}, u32[]{:S(2)}, u32[]{:S(2)}) collective-permute-start(f32[128,2]{1,0:T(8,128)S(1)} %slice_add_fusion), channel_id=1, source_target_pairs={{0,2},{1,3},{2,4},{3,5},{4,6},{5,7},{6,0},{7,1},{8,10},{9,11},{10,... | collective-permute-start | bytes 3080 | tf_op jit(solution)/shard_map/ppermute | solution.py:360
  148.5 7.4 %collective-permute-start.17 = (bf16[128,512]{1,0:T(8,128)(2,1)}, bf16[128,512]{1,0:T(8,128)(2,1)S(1)}, u32[]{:S(2)}, u32[]{:S(2)}) collective-permute-start(bf16[128,512]{1,0:T(8,128)(2,1)} %copy-done.7), channel_id=1, source_target_pairs={{0,6},{1,7},{2,0},{3,1},{4,2},{5,3},{6,4},{7,5},{8,14},{9,15},{10,... | collective-permute-start | bytes 393224 | tf_op jit(solution)/shard_map/ppermute | solution.py:360
  151.1 7.0 %collective-permute-start.18 = (bf16[128,512]{1,0:T(8,128)(2,1)}, bf16[128,512]{1,0:T(8,128)(2,1)S(1)}, u32[]{:S(2)}, u32[]{:S(2)}) collective-permute-start(bf16[128,512]{1,0:T(8,128)(2,1)} %copy-done.6), channel_id=1, source_target_pairs={{0,4},{1,5},{2,6},{3,7},{4,0},{5,1},{6,2},{7,3},{8,12},{9,13},{10,... | collective-permute-start | bytes 393224 | tf_op jit(solution)/shard_map/ppermute | solution.py:360
  151.5 7.6 %collective-permute-start.19 = (bf16[128,512]{1,0:T(8,128)(2,1)S(1)}, bf16[128,512]{1,0:T(8,128)(2,1)S(1)}, u32[]{:S(2)}, u32[]{:S(2)}) collective-permute-start(bf16[128,512]{1,0:T(8,128)(2,1)S(1)} %get-tuple-element.72), channel_id=1, source_target_pairs={{0,2},{1,3},{2,4},{3,5},{4,6},{5,7},{6,0},{7,1},{8,10},{9,11},{10,... | collective-permute-start | bytes 393224 | tf_op jit(solution)/shard_map/ppermute | solution.py:360
